TPU v7x, 256 devices: a whole 4x4x8 slice. The times are simulated.
256 devices in a mesh: gx: 16 (over z, x_lo), gy: 16 (over x_hi, y, core).
Axes of the slice: x: 4 (x_hi: 2, x_lo: 2; x = x_hi * 2 + x_lo), y: 4, z: 8, core: 2. Of those that a mesh axis runs over, the one named last changes fastest.
Arguments:
- tokens: bfloat16 [128, 128, 24, 192], P('gx', 'gy'), may hold values from -8 to 8
- cotangent: bfloat16 [128, 128, 24, 192], P('gx', 'gy'), may hold values from -12 to 12
- ln_gain: float32 [192], replicated, may hold values from 0.1 to 1.9
- ln_bias: float32 [192], replicated, may hold values from -3 to 3
- qkv_weight: bfloat16 [192, 576], replicated, may hold values from -1 to 1
- proj_weight: bfloat16 [192, 192], replicated, may hold values from -0.4375 to 0.4375
Outputs:
- block_out: bfloat16 [128, 128, 24, 192], P('gx', 'gy')
- d_tokens: bfloat16 [128, 128, 24, 192], P('gx', 'gy')
- grad_qkv: float32 [192, 576], replicated
- grad_proj: float32 [192, 192], replicated
- grad_gain: float32 [192], replicated
- grad_bias: float32 [192], replicated
All inputs are finite; a program needn't handle non-finite values.
Results may differ from a plain program's by a relative error of at most 0.005.
The roundings to bfloat16 on the way count: a program that leaves them out, or rounds other values in their place, can miss the bound.
Values may be sent and summed in bfloat16 or wider, within the bound.
No kernel may reach another device: no remote copies, remote signals or barrier semaphores. Data moves between devices by JAX's collectives and lax.ppermute only.
A program may use at most 192 MiB of HBM per device.

v0:
```python
import functools
import math

import jax
import jax.numpy as jnp
from jax import lax
from jax.experimental import pallas as pl
from jax.experimental.pallas import tpu as pltpu
from jax.sharding import PartitionSpec as P

HEADS = 12
WIN = 8
SHIFT = 4
F32 = jnp.float32
BF16 = jnp.bfloat16
LOG2E = math.log2(math.e)
MASKED = 2.0**100
LANES = 128
VMEM = pl.BlockSpec(memory_space=pltpu.VMEM)

NT = (((1,), (1,)), ((), ()))
TN = (((0,), (0,)), ((), ()))


def dot(a, b):
    return jnp.dot(a, b, preferred_element_type=F32)


def pieces_of(block):
    channels = block.shape[-1]
    pieces = {}
    for xh in range(2):
        for yh in range(2):
            quad = block[xh * 4 : xh * 4 + 4, yh * 4 : yh * 4 + 4].reshape(16, 24, channels)
            first = quad[:, 4:12].reshape(LANES, channels)
            second = quad[:, 12:20].reshape(LANES, channels)
            pairs = quad.reshape(8, 2, 24, channels)
            high = jnp.concatenate([pairs[:, 0, 20:24], pairs[:, 1, 20:24]], axis=1)
            low = jnp.concatenate([pairs[:, 0, 0:4], pairs[:, 1, 0:4]], axis=1)
            last = jnp.concatenate([high.reshape(64, channels), low.reshape(64, channels)], axis=0)
            pieces[xh, yh] = [piece.T.astype(BF16) for piece in (first, second, last)]
    return pieces


def quadrant_of(first, second, last):
    channels = first.shape[0]
    first = first.astype(F32).T.reshape(16, 8, channels)
    second = second.astype(F32).T.reshape(16, 8, channels)
    last = last.astype(F32).T
    high = last[:64].reshape(8, 8, channels)
    low = last[64:].reshape(8, 8, channels)
    even = jnp.concatenate([low[:, 0:4]], axis=1)
    odd = low[:, 4:8]
    low = jnp.stack([even, odd], axis=1).reshape(16, 4, channels)
    high = jnp.stack([high[:, 0:4], high[:, 4:8]], axis=1).reshape(16, 4, channels)
    whole = jnp.concatenate([low, first, second, high], axis=1)
    return whole.reshape(4, 4, 24, channels).astype(BF16)


def pack_kernel(tokens_ref, cot_ref, *refs):
    first_refs, rest_refs, (buffer, sems) = refs[:4], refs[4:8], refs[8:]
    sources = (tokens_ref, cot_ref)

    def copy(which, x):
        return pltpu.make_async_copy(
            sources[which].at[pl.ds(2 * x, 2)], buffer.at[which, pl.ds(2 * x, 2)], sems.at[which, x]
        )

    for which in range(2):
        for x in range(4):
            copy(which, x).start()
    for which in range(2):
        for x in range(4):
            copy(which, x).wait()
    for which in range(2):
        pieces = pieces_of(buffer[which].astype(F32))
        for xh in range(2):
            for yh in range(2):
                first, second, last = pieces[xh, yh]
                first_refs[xh * 2 + yh][which] = first
                rest_refs[xh * 2 + yh][0, which] = last
                rest_refs[xh * 2 + yh][1, which] = second


def packed(tokens, cotangent):
    channels = tokens.shape[-1]
    S = jax.ShapeDtypeStruct
    outs = pl.pallas_call(
        pack_kernel,
        out_shape=(S((2, channels, LANES), BF16),) * 4 + (S((2, 2, channels, LANES), BF16),) * 4,
        in_specs=[pl.BlockSpec(memory_space=pltpu.HBM)] * 2,
        out_specs=(VMEM,) * 8,
        scratch_shapes=[pltpu.VMEM((2, *tokens.shape), BF16), pltpu.SemaphoreType.DMA((2, 4))],
        compiler_params=pltpu.CompilerParams(vmem_limit_bytes=62 * 2**20),
        name="pack",
    )(tokens, cotangent)
    return outs[:4], outs[4:]


def prepare_kernel(
    gain_ref, bias_ref, wqkv_ref, proj_ref,
    gain_out, bias_out, wqkv_t_out, proj_t_out, kf_out, qf_out,
):
    gain_out[...] = gain_ref[...].T
    bias_out[...] = bias_ref[...].T
    wqkv_t_out[...] = wqkv_ref[...].astype(F32).T.astype(BF16)
    proj_t_out[...] = proj_ref[...].astype(F32).T.astype(BF16)
    edge_x = lax.axis_index("gx") == lax.axis_size("gx") - 1
    edge_y = lax.axis_index("gy") == lax.axis_size("gy") - 1
    shape = kf_out.shape[1:]
    row = lax.broadcasted_iota(jnp.int32, shape, 0)
    lane = lax.broadcasted_iota(jnp.int32, shape, 1)
    for layout, span in enumerate((LANES, LANES // 2)):
        quad = (lane // span) % 4
        far_x = jnp.where(jnp.logical_and(quad // 2 == 0, edge_x), 1.0, 0.0)
        far_y = jnp.where(jnp.logical_and(quad % 2 == 0, edge_y), 1.0, 0.0)
        key = jnp.where(row == 0, far_x, jnp.where(row == 1, 1 - far_x, jnp.where(row == 2, far_y, 1 - far_y)))
        query = jnp.where(row == 0, 1 - far_x, jnp.where(row == 1, far_x, jnp.where(row == 2, 1 - far_y, far_y)))
        kf_out[layout] = jnp.where(row < 4, key, 0.0).astype(BF16)
        qf_out[layout] = jnp.where(row < 4, query * -MASKED, 0.0).astype(BF16)


def prepared(gain, bias, wqkv, proj):
    channels = gain.shape[0]
    cells = 4 * LANES
    S = jax.ShapeDtypeStruct
    return pl.pallas_call(
        prepare_kernel,
        out_shape=(
            S((channels, 1), F32),
            S((channels, 1), F32),
            S((3 * channels, channels), BF16),
            S((channels, channels), BF16),
            S((2, 16, cells), BF16),
            S((2, 16, cells), BF16),
        ),
        in_specs=[VMEM] * 4,
        out_specs=(VMEM,) * 6,
        compiler_params=pltpu.CompilerParams(vmem_limit_bytes=40 * 2**20),
        name="prepare",
    )(gain[None], bias[None], wqkv, proj)


def unpack_kernel(*refs):
    paired, middle, outs = refs[:4], refs[4:8], refs[8:]
    for which, out in enumerate(outs):
        for xh in range(2):
            for yh in range(2):
                i = xh * 2 + yh
                quad = quadrant_of(paired[i][0, which], middle[i][which], paired[i][1, which])
                out[xh * 4 : xh * 4 + 4, yh * 4 : yh * 4 + 4] = quad


def unpacked(paired, middle, shape):
    return pl.pallas_call(
        unpack_kernel,
        out_shape=(jax.ShapeDtypeStruct(shape, BF16),) * 2,
        in_specs=[VMEM] * 8,
        out_specs=(VMEM,) * 2,
        compiler_params=pltpu.CompilerParams(vmem_limit_bytes=40 * 2**20),
        name="unpack",
    )(*paired, *middle)


def attend_kernel(
    turn,
    q00_ref, q01_ref, q10_ref, q11_ref,
    kf_ref, qf_ref, gain_ref, bias_ref, wqkv_t_ref, wqkv_ref, proj_ref, proj_t_ref,
    *refs,
):
    halves = turn == 1
    given = (0, 5, 1)[turn]
    earlier_refs, refs = refs[:given], refs[given:]
    y_refs, grads_ref, scratch = refs[:4], refs[4], refs[5:]
    (qkv_s, gm_s, mix_s, gqkv_s, kv_s, qa_s, ga_s, e_s, pb_s, dp_s, ds_s, r_s, d_s) = scratch
    quads = (q00_ref, q01_ref, q10_ref, q11_ref)
    if turn:
        quads = [quad.at[turn - 1] for quad in quads]
    channels = q00_ref.shape[-2]
    hd = channels // HEADS
    cells = 4 * LANES
    half = LANES // 2

    def whole(which):
        if halves:
            parts = [q[which].astype(F32) for q in quads]
            return jnp.concatenate(
                [p[:, :half] for p in parts] + [p[:, half:] for p in parts], axis=1
            )
        return jnp.concatenate([q[which].astype(F32) for q in quads], axis=1)

    xf = whole(0)
    gf = whole(1)
    g = gf.astype(BF16)
    mean = jnp.mean(xf, axis=0, keepdims=True)
    centered = xf - mean
    var = jnp.mean(centered * centered, axis=0, keepdims=True)
    inv = lax.rsqrt(var + 1e-5)
    std = centered * inv
    gain = gain_ref[...]
    normed = (std * gain + bias_ref[...]).astype(BF16)
    qkv = dot(wqkv_t_ref[...], normed).astype(BF16)
    qkv_s[...] = qkv
    gm_s[...] = dot(proj_ref[...], g).astype(BF16)

    layout = 1 if halves else 0
    size = cells // 2 if halves else cells
    groups = [slice(start, start + size) for start in range(0, cells, size)]
    step_rows = 64 * (cells // size)
    chunks = [
        (gi, slice(c, c + step_rows), group)
        for gi, group in enumerate(groups)
        for c in range(group.start, group.stop, step_rows)
    ]
    scale = hd**-0.5

    def head_rows(base, h):
        if isinstance(h, int):
            return slice(base + h * hd, base + (h + 1) * hd)
        return pl.ds(pl.multiple_of(base + h * hd, hd), hd)

    def q_rows(h):
        return head_rows(0, h)

    def k_rows(h):
        return head_rows(channels, h)

    def v_rows(h):
        return head_rows(2 * channels, h)

    def folded(x):
        return jnp.sum(x.reshape(-1, 8, x.shape[-1]), axis=0)

    def added(total, gi, x):
        total[gi] = x if total[gi] is None else total[gi] + x

    def prepare(h, slot):
        k = qkv_s[k_rows(h)]
        qf = qkv_s[q_rows(h)].astype(F32) * (scale * LOG2E)
        q_hi = qf.astype(BF16)
        q_lo = (qf - q_hi.astype(F32)).astype(BF16)
        none = jnp.zeros_like(k)
        kv_s[slot] = jnp.concatenate([k, k, kf_ref[layout], qkv_s[v_rows(h)]], axis=0).T
        qa_s[slot] = jnp.concatenate([q_hi, q_lo, qf_ref[layout], none], axis=0)
        ga_s[slot] = jnp.concatenate([none, none, none, gm_s[q_rows(h)]], axis=0)

    def exponentials(slot, chunk, total):
        gi, rows, cols = chunk
        e = jnp.exp2(dot(kv_s[slot, rows], qa_s[slot, :, cols]))
        e_s[slot, rows] = e
        added(total, gi, folded(e))

    def attention(slot, chunk, total):
        gi, rows, cols = chunk
        p = e_s[slot, rows] * r_s[slot, 0:1, cols]
        e_s[slot, rows] = p
        pb_s[rows] = p.astype(BF16)
        dp = dot(kv_s[slot, rows], ga_s[slot, :, cols])
        dp_s[rows] = dp
        added(total, gi, folded(p * dp))

    def grad_scores(slot, chunk):
        _, rows, cols = chunk
        ds_s[slot, rows] = (e_s[slot, rows] * (dp_s[rows] - d_s[0:1, cols])).astype(BF16)

    def mixed_of(h):
        for cols in groups:
            mix_s[q_rows(h), cols] = dot(qkv_s[v_rows(h), cols], pb_s[cols]).astype(BF16)

    def grad_values_of(h):
        for cols in groups:
            gv = lax.dot_general(gm_s[q_rows(h), cols], pb_s[cols], NT, preferred_element_type=F32)
            gqkv_s[v_rows(h), cols] = gv.astype(BF16)

    def grad_queries_of(h, slot):
        for cols in groups:
            gq = dot(qkv_s[k_rows(h), cols], ds_s[slot, cols]) * scale
            gqkv_s[q_rows(h), cols] = gq.astype(BF16)

    def grad_keys_of(h, slot):
        for cols in groups:
            gk = lax.dot_general(
                qkv_s[q_rows(h), cols], ds_s[slot, cols], NT, preferred_element_type=F32
            )
            gqkv_s[k_rows(h), cols] = (gk * scale).astype(BF16)

    def keep_inverse(slot, total):
        for gi, cols in enumerate(groups):
            r_s[slot, 0:1, cols] = 1.0 / jnp.sum(total[gi], axis=0, keepdims=True)

    def step(i, slot, first=True, final=True, ahead=True):
        sums = [None] * len(groups)
        inner = [None] * len(groups)
        count = len(chunks)
        for c, chunk in enumerate(chunks):
            if first:
                exponentials(slot, chunk, sums)
            attention(1 - slot, chunk, inner)
            if final and c == count // 4:
                grad_queries_of(i - 2, slot)
            if final and c == 3 * count // 4:
                grad_keys_of(i - 2, slot)
        if first:
            keep_inverse(slot, sums)
        for gi, cols in enumerate(groups):
            d_s[0:1, cols] = jnp.sum(inner[gi], axis=0, keepdims=True)
        for c, chunk in enumerate(chunks):
            grad_scores(1 - slot, chunk)
            if c == 0:
                mixed_of(i - 1)
            if c == count // 2:
                grad_values_of(i - 1)
        if ahead:
            prepare(i + 1, 1 - slot)

    squares = jnp.square(qkv[: 2 * channels].astype(F32)).reshape(2 * HEADS, hd, cells)
    longest = jnp.max(jnp.sum(squares, axis=1), axis=1, keepdims=True)
    bound = jnp.max(longest[:HEADS] * longest[HEADS:]) * (scale * LOG2E) ** 2
    in_range = bound <= 110.0**2

    @pl.when(in_range)
    def _():
        prepare(0, 0)
        prepare(1, 1)
        sums = [None] * len(groups)
        for chunk in chunks:
            exponentials(0, chunk, sums)
        keep_inverse(0, sums)
        step(1, 1, final=False)

        def two_steps(j, carry):
            step(2 + 2 * j, 0)
            step(3 + 2 * j, 1)
            return carry

        lax.fori_loop(0, (HEADS - 4) // 2, two_steps, 0)
        step(HEADS - 2, 0)
        step(HEADS - 1, 1, ahead=False)
        step(HEADS, 0, first=False, ahead=False)
        grad_queries_of(HEADS - 1, 1)
        grad_keys_of(HEADS - 1, 1)

    @pl.when(jnp.logical_not(in_range))
    def _():
        def head(h, carry):
            prepare(h, 0)
            for cols in groups:
                s = dot(kv_s[0, cols], qa_s[0, :, cols])
                e = jnp.exp2(s - jnp.max(s, axis=0, keepdims=True))
                p = e * (1.0 / jnp.sum(e, axis=0, keepdims=True))
                pb_s[cols] = p.astype(BF16)
                dp = dot(kv_s[0, cols], ga_s[0, :, cols])
                inner = jnp.sum(p * dp, axis=0, keepdims=True)
                ds_s[0, cols] = (p * (dp - inner)).astype(BF16)
            mixed_of(h)
            grad_values_of(h)
            grad_queries_of(h, 0)
            grad_keys_of(h, 0)
            return carry

        lax.fori_loop(0, HEADS, head, 0)

    mixed = mix_s[...]
    block_out = xf + dot(proj_t_ref[...], mixed)
    gqkv = gqkv_s[...]
    gn = dot(wqkv_ref[...], gqkv)
    scaled = gn * gain
    gx = inv * (
        scaled
        - jnp.mean(scaled, axis=0, keepdims=True)
        - std * jnp.mean(scaled * std, axis=0, keepdims=True)
    )
    d_tokens = gf + gx
    for which, y in enumerate((block_out, d_tokens)):
        for i, ref in enumerate(y_refs):
            if halves:
                lo = y[:, i * half : (i + 1) * half]
                hi = y[:, cells // 2 + i * half : cells // 2 + (i + 1) * half]
                part = jnp.concatenate([lo, hi], axis=1)
            else:
                part = y[:, i * LANES : (i + 1) * LANES]
            if turn == 1:
                ref[0, which] = earlier_refs[i][which]
                ref[1, which] = part.astype(BF16)
            else:
                ref[which] = part.astype(BF16)

    dw = lax.dot_general(normed, gqkv, NT, preferred_element_type=F32)
    dproj = lax.dot_general(mixed, g, NT, preferred_element_type=F32)
    dgain = jnp.sum(gn * std, axis=1, keepdims=True)
    dbias = jnp.sum(gn, axis=1, keepdims=True)
    joined = jnp.concatenate([dw, dproj], axis=1)
    blocks = [joined[:, i * LANES : (i + 1) * LANES] for i in range(joined.shape[1] // LANES)]
    lane = lax.broadcasted_iota(jnp.int32, (channels, LANES), 1)
    tail = jnp.where(lane == 0, dgain, jnp.where(lane == 1, dbias, 0.0)).T[:8]
    used = len(blocks) * channels
    grads = jnp.concatenate(blocks, axis=0)
    pad = jnp.zeros((8, 2 * LANES - channels), F32)
    extra = jnp.concatenate(
        [tail[:, :LANES], jnp.concatenate([tail[:, LANES:], pad], axis=1)], axis=0
    )
    if turn:
        grads = grads + earlier_refs[-1][:used]
        extra = extra + earlier_refs[-1][used : used + 16]
    grads_ref[:used] = grads.astype(grads_ref.dtype)
    grads_ref[used : used + 16] = extra.astype(grads_ref.dtype)
    grads_ref[used + 16 :] = jnp.zeros(
        (grads_ref.shape[0] - used - 16, LANES), grads_ref.dtype
    )


GRAD_ROWS = 1280


def attend(turn, quads, features, weights, earlier):
    channels = quads[0].shape[-2]
    cells = 4 * LANES
    width = cells // 2 if turn == 1 else cells
    S = jax.ShapeDtypeStruct
    piece = (2, channels, LANES)
    return pl.pallas_call(
        functools.partial(attend_kernel, turn),
        out_shape=(S((2, *piece) if turn == 1 else piece, BF16),) * 4
        + (S((GRAD_ROWS, LANES), BF16 if turn == 2 else F32),),
        in_specs=[VMEM] * (12 + len(earlier)),
        out_specs=(VMEM,) * 5,
        scratch_shapes=[
            pltpu.VMEM((3 * channels, cells), BF16),
            pltpu.VMEM((channels, cells), BF16),
            pltpu.VMEM((channels, cells), BF16),
            pltpu.VMEM((3 * channels, cells), BF16),
            pltpu.VMEM((2, cells, 64), BF16),
            pltpu.VMEM((2, 64, cells), BF16),
            pltpu.VMEM((2, 64, cells), BF16),
            pltpu.VMEM((2, cells, width), F32),
            pltpu.VMEM((cells, width), BF16),
            pltpu.VMEM((cells, width), F32),
            pltpu.VMEM((2, cells, width), BF16),
            pltpu.VMEM((2, 8, cells), F32),
            pltpu.VMEM((8, cells), F32),
        ],
        compiler_params=pltpu.CompilerParams(vmem_limit_bytes=40 * 2**20),
        cost_estimate=pl.CostEstimate(
            flops=12 * 12 * 512 * 512 * 256, bytes_accessed=4 * 2**20, transcendentals=12 * 512 * 512
        ),
        name="attend",
    )(*quads, *features, *weights, *earlier)


def moved(block, step_x, step_y):
    nx, ny = lax.axis_size("gx"), lax.axis_size("gy")
    route = []
    for i in range(nx):
        for j in range(ny):
            to = ((i + step_x) % nx) * ny + (j + step_y) % ny
            route.append((i * ny + j, to))
    return lax.ppermute(block, ("gx", "gy"), route)


def summed(rows):
    nx, ny = lax.axis_size("gx"), lax.axis_size("gy")
    near = 2 * ny
    planes = [[near * i + j for j in range(near)] for i in range(nx // 2)]
    across = [list(ids) for ids in zip(*planes)]

    def exchanged(pieces, groups):
        return lax.all_to_all(pieces, ("gx", "gy"), 0, 0, axis_index_groups=groups)

    def copies(piece, count):
        return jnp.broadcast_to(piece[None], (count, *piece.shape))

    got = exchanged(rows.reshape(near, -1, LANES), planes)
    mine = jnp.sum(got.astype(F32), axis=0).astype(BF16)
    got = exchanged(copies(mine, nx // 2), across)
    total = jnp.sum(got.astype(F32), axis=0).astype(BF16)
    return exchanged(copies(total, near), planes).reshape(rows.shape)


def grads_kernel(
    factor, rows_ref, dw_ref, dproj_ref, gain_ref, bias_ref, dw_s, dproj_s, ends_s, out_sems
):
    channels = dw_s.shape[0]
    blocks = 4 * channels // LANES
    used = blocks * channels
    outgoing = []

    def send(src, dst):
        copy = pltpu.make_async_copy(src, dst, out_sems.at[len(outgoing)])
        copy.start()
        outgoing.append(copy)

    def block(i):
        return rows_ref[i * channels : (i + 1) * channels].astype(F32) * factor

    whole = 3 * channels // LANES
    for i in range(whole):
        dw_s[:, i * LANES : (i + 1) * LANES] = block(i)
        if i % 2:
            cols = pl.ds((i - 1) * LANES, 2 * LANES)
            send(dw_s.at[:, cols], dw_ref.at[:, cols])
    rest = jnp.concatenate([block(i) for i in range(whole, blocks)], axis=1)
    edge = 3 * channels - whole * LANES
    dw_s[:, whole * LANES :] = rest[:, :edge]
    send(dw_s.at[:, pl.ds(whole * LANES, edge)], dw_ref.at[:, pl.ds(whole * LANES, edge)])
    dproj_s[...] = rest[:, edge:]
    send(dproj_s, dproj_ref)
    tail = rows_ref[used : used + 16].astype(F32) * factor
    ends_s[...] = jnp.concatenate([tail[:8], tail[8:]], axis=1)[:, :channels]
    gain_ref[...] = ends_s[0:1]
    bias_ref[...] = ends_s[1:2]
    for copy in outgoing:
        copy.wait()


def grads_of(rows, channels, factor):
    S = jax.ShapeDtypeStruct
    anywhere = pl.BlockSpec(memory_space=pltpu.HBM)
    return pl.pallas_call(
        functools.partial(grads_kernel, factor),
        out_shape=(
            S((channels, 3 * channels), F32),
            S((channels, channels), F32),
            S((1, channels), F32),
            S((1, channels), F32),
        ),
        in_specs=[VMEM],
        out_specs=(anywhere, anywhere, VMEM, VMEM),
        scratch_shapes=[
            pltpu.VMEM((channels, 3 * channels), F32),
            pltpu.VMEM((channels, channels), F32),
            pltpu.VMEM((8, channels), F32),
            pltpu.SemaphoreType.DMA((4,)),
        ],
        name="unpack_grads",
    )(rows)


def shards(tokens, cotangent, ln_gain, ln_bias, qkv_weight, proj_weight):
    tile_x, tile_y, depth, channels = tokens.shape
    nx, ny = lax.axis_size("gx"), lax.axis_size("gy")
    first, rest = packed(tokens, cotangent)
    first, ln_gain, ln_bias, qkv_weight, proj_weight = lax.optimization_barrier(
        (first, ln_gain, ln_bias, qkv_weight, proj_weight)
    )
    gain, bias, wqkv_t, proj_t, *features = prepared(ln_gain, ln_bias, qkv_weight, proj_weight)
    weights = (gain, bias, wqkv_t, qkv_weight, proj_weight, proj_t)

    steps = ((1, 1), (1, 0), (0, 1))

    def gathered(quads):
        return [moved(quad, -x, -y) for quad, (x, y) in zip(quads, steps)] + [quads[3]]

    def returned(quads):
        return [moved(quad, x, y) for quad, (x, y) in zip(quads, steps)] + [quads[3]]

    first, rest = gathered(first), gathered(rest)
    *y, sums = attend(0, first, features, weights, ())
    *y, sums = attend(1, rest, features, weights, (*y, sums))
    paired = returned(y)
    *y, sums = attend(2, rest, features, weights, (sums,))
    middle = returned(y)
    sums, paired = lax.optimization_barrier((sums, paired))
    total = summed(sums)
    block_out, d_tokens = unpacked(paired, middle, tokens.shape)
    factor = 1.0 / math.sqrt(tile_x * nx * tile_y * ny * depth)
    dw, dproj, dgain, dbias = grads_of(total, channels, factor)
    return block_out, d_tokens, dw, dproj, dgain[0], dbias[0]


def solution(mesh):
    placed = (P("gx", "gy", None, None), P("gx", "gy", None, None), P(), P(), P(), P())
    return jax.shard_map(
        shards,
        mesh=mesh,
        in_specs=placed,
        out_specs=(P("gx", "gy", None, None), P("gx", "gy", None, None), P(), P(), P(), P()),
        check_vma=False,
    )
```

profile of v0, /device:TPU:1, one launch (start us, length us, event | category | flops | bytes accessed | tf_op | source)
XLA Modules:
  0.0 118.3 jit_solution(9479152186680688559)
XLA Ops:
  0.6 0.0 copy-start.1
  0.6 0.0 copy-start
  0.7 0.0 copy-start.3
  0.7 3.0 %pack.1 = (bf16[2,192,128]{2,1,0:T(8,128)(2,1)}, bf16[2,192,128]{2,1,0:T(8,128)(2,1)}, bf16[2,192,128]{2,1,0:T(8,128)(2,1)}, bf16[2,192,128]{2,1,0:T(8,128)(2,1)...) custom-call(bf16[8,8,24,192]{3,2,1,0:T(8,128)(2,1)} %tokens_ref.1, ...), custom_call_target="tpu_custom_call" | custom-call | tf_op jit(solution)/shard_map/pack/pallas_call | solution.py:88
  3.7 8.0 %collective-permute-start.3 = (bf16[2,192,128]{2,1,0:T(8,128)(2,1)}, bf16[2,192,128]{2,1,0:T(8,128)(2,1)S(1)}, u32[]{:S(2)}, u32[]{:S(2)}) collective-permute-start(bf16[2,192,128]{2,1,0:T(8,128)(2,1)} %get-tuple-element.72), channel_id=1, source_target_pairs={{0,255},{1,240},{2,241},{3,242},{4,243},{5,244},{6,245},{7,246},{8... | collective-permute-start | bytes 294920 | tf_op jit(solution)/shard_map/ppermute | solution.py:457
  11.7 0.3 collective-permute-start.4
  11.9 3.5 %collective-permute-start.5 = (bf16[2,192,128]{2,1,0:T(8,128)(2,1)}, bf16[2,192,128]{2,1,0:T(8,128)(2,1)S(1)}, u32[]{:S(2)}, u32[]{:S(2)}) collective-permute-start(bf16[2,192,128]{2,1,0:T(8,128)(2,1)} %get-tuple-element.74), channel_id=1, source_target_pairs={{0,15},{1,0},{2,1},{3,2},{4,3},{5,4},{6,5},{7,6},{8,7},{9,8},{10,9... | collective-permute-start | bytes 294920 | tf_op jit(solution)/shard_map/ppermute | solution.py:457
  15.5 2.7 %collective-permute-start = (bf16[2,2,192,128]{3,2,1,0:T(8,128)(2,1)}, bf16[2,2,192,128]{3,2,1,0:T(8,128)(2,1)S(1)}, u32[]{:S(2)}, u32[]{:S(2)}) collective-permute-start(bf16[2,2,192,128]{3,2,1,0:T(8,128)(2,1)} %get-tuple-element.54), channel_id=1, source_target_pairs={{0,255},{1,240},{2,241},{3,242},{4,243},{5,244},{6,245},{7,246},{8... | collective-permute-start | bytes 589832 | tf_op jit(solution)/shard_map/ppermute | solution.py:457
  18.2 1.2 collective-permute-start.1
  19.3 0.0 copy-done.1
  19.3 0.0 copy-done
  19.3 0.0 copy-done.3
  19.4 0.7 copy-done.2
  20.0 0.3 prepare.1
  20.3 0.0 collective-permute-done.3.q00_ref
  20.3 0.0 copy-done.7
  20.3 0.1 collective-permute-start.2
  20.4 0.0 collective-permute-done.4.q01_ref
  20.4 0.0 collective-permute-done.5.q10_ref
  20.4 0.5 copy-done.5
  20.9 11.8 %attend.3 = (bf16[2,192,128]{2,1,0:T(8,128)(2,1)S(1)}, bf16[2,192,128]{2,1,0:T(8,128)(2,1)S(1)}, bf16[2,192,128]{2,1,0:T(8,128)(2,1)S(1)}, bf16[2,192,128]{2,1,0:T(8,128)(2,1)S(1)}, f32[1280,128]{1,0:T(8,128)S(1)}) custom-call(bf16[2,192,128]{2,1,0:T(8,128)(2,1)S(1)} %collective-permute-done.3.q00_ref, ...), custom_call_target="tpu_custom_call" | custom-call | flops 9663676416 | bytes 4194304 | tf_op jit(solution)/shard_map/attend/pallas_call | solution.py:421
  32.7 0.0 collective-permute-done.q00_ref
  32.7 0.0 collective-permute-done.1.q01_ref
  32.7 0.0 collective-permute-done.2.q10_ref
  32.7 0.0 copy-done.4
  32.7 11.8 %attend.4 = (bf16[2,2,192,128]{3,2,1,0:T(8,128)(2,1)S(1)}, bf16[2,2,192,128]{3,2,1,0:T(8,128)(2,1)S(1)}, bf16[2,2,192,128]{3,2,1,0:T(8,128)(2,1)S(1)}, bf16[2,2,...) custom-call(bf16[2,2,192,128]{3,2,1,0:T(8,128)(2,1)S(1)} %collective-permute-done.q00_ref, ...), custom_call_target="tpu_custom_call" | custom-call | flops 9663676416 | bytes 4194304 | tf_op jit(solution)/shard_map/attend/pallas_call | solution.py:421
  44.5 1.0 collective-permute-start.6
  45.5 1.6 %collective-permute-start.7 = (bf16[2,2,192,128]{3,2,1,0:T(8,128)(2,1)S(1)}, bf16[2,2,192,128]{3,2,1,0:T(8,128)(2,1)S(1)}, u32[]{:S(2)}, u32[]{:S(2)}) collective-permute-start(bf16[2,2,192,128]{3,2,1,0:T(8,128)(2,1)S(1)} %get-tuple-element.84), channel_id=1, source_target_pairs={{0,16},{1,17},{2,18},{3,19},{4,20},{5,21},{6,22},{7,23},{8,24},{9,... | collective-permute-start | bytes 589832 | tf_op jit(solution)/shard_map/ppermute | solution.py:457
  47.0 3.8 %collective-permute-start.8 = (bf16[2,2,192,128]{3,2,1,0:T(8,128)(2,1)S(1)}, bf16[2,2,192,128]{3,2,1,0:T(8,128)(2,1)S(1)}, u32[]{:S(2)}, u32[]{:S(2)}) collective-permute-start(bf16[2,2,192,128]{3,2,1,0:T(8,128)(2,1)S(1)} %get-tuple-element.85), channel_id=1, source_target_pairs={{0,1},{1,2},{2,3},{3,4},{4,5},{5,6},{6,7},{7,8},{8,9},{9,10},{10,1... | collective-permute-start | bytes 589832 | tf_op jit(solution)/shard_map/ppermute | solution.py:457
  50.8 11.8 %attend.5 = (bf16[2,192,128]{2,1,0:T(8,128)(2,1)S(1)}, bf16[2,192,128]{2,1,0:T(8,128)(2,1)S(1)}, bf16[2,192,128]{2,1,0:T(8,128)(2,1)S(1)}, bf16[2,192,128]{2,1,0:T(8,128)(2,1)S(1)}, bf16[1280,128]{1,0:T(8,128)(2,1)S(1)}) custom-call(bf16[2,2,192,128]{3,2,1,0:T(8,128)(2,1)S(1)} %collective-permute-done.q00_ref, ...), custom_call_target="tpu_custom_call" | custom-call | flops 9663676416 | bytes 4194304 | tf_op jit(solution)/shard_map/attend/pallas_call | solution.py:421
  62.6 0.0 collective-permute-done.6.refs_0_
  62.6 0.0 collective-permute-done.7.refs_1_
  62.6 0.0 collective-permute-done.8.refs_2_
  62.6 18.0 %all_to_all.15 = bf16[32,40,128]{2,1,0:T(8,128)(2,1)S(1)} all-to-all(bf16[32,40,128]{2,1,0:T(8,128)(2,1)S(1)} %bitcast.6), channel_id=1, replica_groups={{0,1,2,3,4,5,6,7,8,9,10,11,12,13,14,15,16,17,18,19,20,21,22,23,24,25,26..., dimensions={0} | all-to-all | bytes 655360 | tf_op jit(solution)/shard_map/all_to_all | solution.py:467
  80.6 0.1 reduce_sum.24
  80.7 15.3 %all_to_all.16 = bf16[8,40,128]{2,1,0:T(8,128)(2,1)S(1)} all-to-all(bf16[8,40,128]{2,1,0:T(8,128)(2,1)S(1)} %broadcast_in_dim.20), channel_id=1, replica_groups={{0,32,64,96,128,160,192,224},{1,33,65,97,129,161,193,225},{2,34,66,98,1..., dimensions={0} | all-to-all | bytes 163840 | tf_op jit(solution)/shard_map/all_to_all | solution.py:467
  96.0 0.8 broadcast_in_dim.21
  96.8 5.3 %all-to-all-start.2 = ((bf16[32,40,128]{2,1,0:T(8,128)(2,1)}), bf16[32,40,128]{2,1,0:T(8,128)(2,1)S(1)}, u32[]{:S(2)}, u32[]{:S(2)}) async-start(bf16[32,40,128]{2,1,0:T(8,128)(2,1)} %broadcast_in_dim.21), calls=%async_computation.2 | async-start | bytes 655360 | tf_op jit(solution)/shard_map/all_to_all | solution.py:467
  102.1 2.7 %collective-permute-start.9 = (bf16[2,192,128]{2,1,0:T(8,128)(2,1)S(1)}, bf16[2,192,128]{2,1,0:T(8,128)(2,1)S(1)}, u32[]{:S(2)}, u32[]{:S(2)}) collective-permute-start(bf16[2,192,128]{2,1,0:T(8,128)(2,1)S(1)} %get-tuple-element.91), channel_id=1, source_target_pairs={{0,17},{1,18},{2,19},{3,20},{4,21},{5,22},{6,23},{7,24},{8,25},{9,... | collective-permute-start | bytes 294920 | tf_op jit(solution)/shard_map/ppermute | solution.py:457
  104.8 0.1 collective-permute-start.10
  105.0 0.6 collective-permute-start.11
  105.6 3.4 %collective-permute-done.9.refs_4_ = bf16[2,192,128]{2,1,0:T(8,128)(2,1)S(1)} collective-permute-done((bf16[2,192,128]{2,1,0:T(8,128)(2,1)S(1)}, bf16[2,192,128]{2,1,0:T(8,128)(2,1)S(1)}, u32[]{:S(2)}, u32[]{:S(2)}) %collective-permute-start.9) | collective-permute-done | bytes 98336 | tf_op jit(solution)/shard_map/ppermute | solution.py:457
  108.9 2.9 %collective-permute-done.10.refs_5_ = bf16[2,192,128]{2,1,0:T(8,128)(2,1)S(1)} collective-permute-done((bf16[2,192,128]{2,1,0:T(8,128)(2,1)S(1)}, bf16[2,192,128]{2,1,0:T(8,128)(2,1)S(1)}, u32[]{:S(2)}, u32[]{:S(2)}) %collective-permute-start.10) | collective-permute-done | bytes 98336 | tf_op jit(solution)/shard_map/ppermute | solution.py:457
  111.8 0.0 collective-permute-done.11.refs_6_
  111.9 1.6 %unpack.1 = (bf16[8,8,24,192]{3,2,1,0:T(8,128)(2,1)}, bf16[8,8,24,192]{3,2,1,0:T(8,128)(2,1)}) custom-call(bf16[2,2,192,128]{3,2,1,0:T(8,128)(2,1)S(1)} %collective-permute-done.6.refs_0_, bf16[2,2,192,128]{3,2,1,0:T(8,128)(2,1)S(1)} %collective-permute-done.7.refs_1_, bf16[2,2,192,128]{3,2,1,0:T(8,128)(2,1)S(1)} %collective-permute-done.8.refs_2_, ...), custom_call_target="tpu_custom_call" | custom-call | tf_op jit(solution)/shard_map/unpack/pallas_call | solution.py:155
  113.5 1.4 %all-to-all-done.2 = bf16[32,40,128]{2,1,0:T(8,128)(2,1)S(1)} async-done(((bf16[32,40,128]{2,1,0:T(8,128)(2,1)}), bf16[32,40,128]{2,1,0:T(8,128)(2,1)S(1)}, u32[]{:S(2)}, u32[]{:S(2)}) %all-to-all-start.2) | async-done | bytes 327712 | tf_op jit(solution)/shard_map/all_to_all | solution.py:467
  114.9 0.7 copy-done.6
  115.6 2.5 %unpack_grads.1 = (f32[192,576]{1,0:T(8,128)}, f32[192,192]{1,0:T(8,128)}, f32[1,192]{1,0:T(1,128)}, f32[1,192]{1,0:T(1,128)}) custom-call(bf16[1280,128]{1,0:T(8,128)(2,1)} %bitcast.9), custom_call_target="tpu_custom_call" | custom-call | tf_op jit(solution)/shard_map/unpack_grads/pallas_call | solution.py:518
  (7 shorter events, 0.0 us)
Async XLA Ops:
  0.6 18.7 %copy-start.1 = (bf16[192,192]{1,0:T(8,128)(2,1)S(1)}, bf16[192,192]{1,0:T(8,128)(2,1)}, u32[]{:S(2)}) copy-start(bf16[192,192]{1,0:T(8,128)(2,1)} %proj_ref.3) | copy-start | bytes 221188
  0.6 18.7 %copy-start = (bf16[192,576]{1,0:T(8,128)(2,1)S(1)}, bf16[192,576]{1,0:T(8,128)(2,1)}, u32[]{:S(2)}) copy-start(bf16[192,576]{1,0:T(8,128)(2,1)} %wqkv_ref.3) | copy-start | bytes 663556
  0.7 18.7 %copy-start.3 = (f32[192]{0:T(256)S(1)}, f32[192]{0:T(256)}, u32[]{:S(2)}) copy-start(f32[192]{0:T(256)} %param.9) | copy-start | bytes 2308
  3.7 16.6 %collective-permute-start.3 = (bf16[2,192,128]{2,1,0:T(8,128)(2,1)}, bf16[2,192,128]{2,1,0:T(8,128)(2,1)S(1)}, u32[]{:S(2)}, u32[]{:S(2)}) collective-permute-start(bf16[2,192,128]{2,1,0:T(8,128)(2,1)} %get-tuple-element.72), channel_id=1, source_target_pairs={{0,255},{1,240},{2,241},{3,242},{4,243},{5,244},{6,245},{7,246},{8... | collective-permute-start | bytes 294920 | tf_op jit(solution)/shard_map/ppermute | solution.py:457
  11.7 8.7 %collective-permute-start.4 = (bf16[2,192,128]{2,1,0:T(8,128)(2,1)}, bf16[2,192,128]{2,1,0:T(8,128)(2,1)S(1)}, u32[]{:S(2)}, u32[]{:S(2)}) collective-permute-start(bf16[2,192,128]{2,1,0:T(8,128)(2,1)} %get-tuple-element.73), channel_id=1, source_target_pairs={{0,240},{1,241},{2,242},{3,243},{4,244},{5,245},{6,246},{7,247},{8... | collective-permute-start | bytes 294920 | tf_op jit(solution)/shard_map/ppermute | solution.py:457
  11.9 8.4 %collective-permute-start.5 = (bf16[2,192,128]{2,1,0:T(8,128)(2,1)}, bf16[2,192,128]{2,1,0:T(8,128)(2,1)S(1)}, u32[]{:S(2)}, u32[]{:S(2)}) collective-permute-start(bf16[2,192,128]{2,1,0:T(8,128)(2,1)} %get-tuple-element.74), channel_id=1, source_target_pairs={{0,15},{1,0},{2,1},{3,2},{4,3},{5,4},{6,5},{7,6},{8,7},{9,8},{10,9... | collective-permute-start | bytes 294920 | tf_op jit(solution)/shard_map/ppermute | solution.py:457
  15.5 17.2 %collective-permute-start = (bf16[2,2,192,128]{3,2,1,0:T(8,128)(2,1)}, bf16[2,2,192,128]{3,2,1,0:T(8,128)(2,1)S(1)}, u32[]{:S(2)}, u32[]{:S(2)}) collective-permute-start(bf16[2,2,192,128]{3,2,1,0:T(8,128)(2,1)} %get-tuple-element.54), channel_id=1, source_target_pairs={{0,255},{1,240},{2,241},{3,242},{4,243},{5,244},{6,245},{7,246},{8... | collective-permute-start | bytes 589832 | tf_op jit(solution)/shard_map/ppermute | solution.py:457
  18.2 14.5 %collective-permute-start.1 = (bf16[2,2,192,128]{3,2,1,0:T(8,128)(2,1)}, bf16[2,2,192,128]{3,2,1,0:T(8,128)(2,1)S(1)}, u32[]{:S(2)}, u32[]{:S(2)}) collective-permute-start(bf16[2,2,192,128]{3,2,1,0:T(8,128)(2,1)} %get-tuple-element.55), channel_id=1, source_target_pairs={{0,240},{1,241},{2,242},{3,243},{4,244},{5,245},{6,246},{7,247},{8... | collective-permute-start | bytes 589832 | tf_op jit(solution)/shard_map/ppermute | solution.py:457
  19.3 0.7 copy-start.2
  19.3 1.0 copy-start.7
  20.0 0.9 copy-start.5
  20.3 12.4 %collective-permute-start.2 = (bf16[2,2,192,128]{3,2,1,0:T(8,128)(2,1)S(1)}, bf16[2,2,192,128]{3,2,1,0:T(8,128)(2,1)S(1)}, u32[]{:S(2)}, u32[]{:S(2)}) collective-permute-start(bf16[2,2,192,128]{3,2,1,0:T(8,128)(2,1)S(1)} %copy-done.7), channel_id=1, source_target_pairs={{0,15},{1,0},{2,1},{3,2},{4,3},{5,4},{6,5},{7,6},{8,7},{9,8},{10,9... | collective-permute-start | bytes 589832 | tf_op jit(solution)/shard_map/ppermute | solution.py:457
  20.9 11.8 %copy-start.4 = (bf16[2,2,192,128]{3,2,1,0:T(8,128)(2,1)S(1)}, bf16[2,2,192,128]{3,2,1,0:T(8,128)(2,1)}, u32[]{:S(2)}) copy-start(bf16[2,2,192,128]{3,2,1,0:T(8,128)(2,1)} %get-tuple-element.57.q11_ref) | copy-start | bytes 589828
  44.5 18.1 %collective-permute-start.6 = (bf16[2,2,192,128]{3,2,1,0:T(8,128)(2,1)S(1)}, bf16[2,2,192,128]{3,2,1,0:T(8,128)(2,1)S(1)}, u32[]{:S(2)}, u32[]{:S(2)}) collective-permute-start(bf16[2,2,192,128]{3,2,1,0:T(8,128)(2,1)S(1)} %get-tuple-element.83), channel_id=1, source_target_pairs={{0,17},{1,18},{2,19},{3,20},{4,21},{5,22},{6,23},{7,24},{8,25},{9,... | collective-permute-start | bytes 589832 | tf_op jit(solution)/shard_map/ppermute | solution.py:457
  45.5 17.2 %collective-permute-start.7 = (bf16[2,2,192,128]{3,2,1,0:T(8,128)(2,1)S(1)}, bf16[2,2,192,128]{3,2,1,0:T(8,128)(2,1)S(1)}, u32[]{:S(2)}, u32[]{:S(2)}) collective-permute-start(bf16[2,2,192,128]{3,2,1,0:T(8,128)(2,1)S(1)} %get-tuple-element.84), channel_id=1, source_target_pairs={{0,16},{1,17},{2,18},{3,19},{4,20},{5,21},{6,22},{7,23},{8,24},{9,... | collective-permute-start | bytes 589832 | tf_op jit(solution)/shard_map/ppermute | solution.py:457
  47.0 15.6 %collective-permute-start.8 = (bf16[2,2,192,128]{3,2,1,0:T(8,128)(2,1)S(1)}, bf16[2,2,192,128]{3,2,1,0:T(8,128)(2,1)S(1)}, u32[]{:S(2)}, u32[]{:S(2)}) collective-permute-start(bf16[2,2,192,128]{3,2,1,0:T(8,128)(2,1)S(1)} %get-tuple-element.85), channel_id=1, source_target_pairs={{0,1},{1,2},{2,3},{3,4},{4,5},{5,6},{6,7},{7,8},{8,9},{9,10},{10,1... | collective-permute-start | bytes 589832 | tf_op jit(solution)/shard_map/ppermute | solution.py:457
  96.8 18.1 %all-to-all-start.2 = ((bf16[32,40,128]{2,1,0:T(8,128)(2,1)}), bf16[32,40,128]{2,1,0:T(8,128)(2,1)S(1)}, u32[]{:S(2)}, u32[]{:S(2)}) async-start(bf16[32,40,128]{2,1,0:T(8,128)(2,1)} %broadcast_in_dim.21), calls=%async_computation.2 | async-start | bytes 655360 | tf_op jit(solution)/shard_map/all_to_all | solution.py:467
  102.1 6.8 %collective-permute-start.9 = (bf16[2,192,128]{2,1,0:T(8,128)(2,1)S(1)}, bf16[2,192,128]{2,1,0:T(8,128)(2,1)S(1)}, u32[]{:S(2)}, u32[]{:S(2)}) collective-permute-start(bf16[2,192,128]{2,1,0:T(8,128)(2,1)S(1)} %get-tuple-element.91), channel_id=1, source_target_pairs={{0,17},{1,18},{2,19},{3,20},{4,21},{5,22},{6,23},{7,24},{8,25},{9,... | collective-permute-start | bytes 294920 | tf_op jit(solution)/shard_map/ppermute | solution.py:457
  104.8 7.0 %collective-permute-start.10 = (bf16[2,192,128]{2,1,0:T(8,128)(2,1)S(1)}, bf16[2,192,128]{2,1,0:T(8,128)(2,1)S(1)}, u32[]{:S(2)}, u32[]{:S(2)}) collective-permute-start(bf16[2,192,128]{2,1,0:T(8,128)(2,1)S(1)} %get-tuple-element.92), channel_id=1, source_target_pairs={{0,16},{1,17},{2,18},{3,19},{4,20},{5,21},{6,22},{7,23},{8,24},{9,... | collective-permute-start | bytes 294920 | tf_op jit(solution)/shard_map/ppermute | solution.py:457
  105.0 6.9 %collective-permute-start.11 = (bf16[2,192,128]{2,1,0:T(8,128)(2,1)S(1)}, bf16[2,192,128]{2,1,0:T(8,128)(2,1)S(1)}, u32[]{:S(2)}, u32[]{:S(2)}) collective-permute-start(bf16[2,192,128]{2,1,0:T(8,128)(2,1)S(1)} %get-tuple-element.93), channel_id=1, source_target_pairs={{0,1},{1,2},{2,3},{3,4},{4,5},{5,6},{6,7},{7,8},{8,9},{9,10},{10,1... | collective-permute-start | bytes 294920 | tf_op jit(solution)/shard_map/ppermute | solution.py:457
  114.9 0.7 copy-start.6
where the time goes:
time: 120 us; the launch traced here: 118 us
  Pallas kernels  42.7 us (36%)
  blocking collectives  33.3 us (28%)
  starting transfers between devices  30.8 us (26%)
  waiting for transfers between devices  7.71 us (6%)
  local copies, waits for them, and re-layouts  2.7 us (2%)
    pallas_call x3, Pallas kernels, attend(): pl.pallas_call(functools.partial(attend_kernel, turn), out_shape=(S((2, *...  35.3 us
    all_to_all x2, blocking collectives, exchanged(): return lax.all_to_all(pieces, ('gx', 'gy'), 0, 0, axis_index_groups=groups)  33.3 us
    ppermute x12, starting transfers between devices, moved(): return lax.ppermute(block, ('gx', 'gy'), route)  25.5 us
    ppermute x12, waiting for transfers between devices, moved(): return lax.ppermute(block, ('gx', 'gy'), route)  6.29 us
    all_to_all x1, starting transfers between devices, exchanged(): return lax.all_to_all(pieces, ('gx', 'gy'), 0, 0, axis_index_groups=groups)  5.31 us
    pallas_call x1, Pallas kernels, packed(): pl.pallas_call(pack_kernel, out_shape=(S((2, channels, LANES), BF16),) *...  3.05 us
    pallas_call x1, Pallas kernels, grads_of(): pl.pallas_call(functools.partial(grads_kernel, factor), out_shape=(S((cha...  2.47 us
  transfers between devices with their start and end apart: 13, of which 3 were waited for; matrix products, arithmetic and copies ran while one was open for 0% of the time, Pallas kernels for 21%

commit v1 on v0

--- a/solution.py
+++ b/solution.py
@@ -26,20 +26,23 @@
     return jnp.dot(a, b, preferred_element_type=F32)
 
 
-def pieces_of(block):
-    channels = block.shape[-1]
-    pieces = {}
-    for xh in range(2):
-        for yh in range(2):
-            quad = block[xh * 4 : xh * 4 + 4, yh * 4 : yh * 4 + 4].reshape(16, 24, channels)
-            first = quad[:, 4:12].reshape(LANES, channels)
-            second = quad[:, 12:20].reshape(LANES, channels)
-            pairs = quad.reshape(8, 2, 24, channels)
-            high = jnp.concatenate([pairs[:, 0, 20:24], pairs[:, 1, 20:24]], axis=1)
-            low = jnp.concatenate([pairs[:, 0, 0:4], pairs[:, 1, 0:4]], axis=1)
-            last = jnp.concatenate([high.reshape(64, channels), low.reshape(64, channels)], axis=0)
-            pieces[xh, yh] = [piece.T.astype(BF16) for piece in (first, second, last)]
-    return pieces
+def quadrants(block):
+    shape = (16, *block.shape[2:])
+    return [
+        block[x : x + 4, y : y + 4].reshape(shape) for x in (0, 4) for y in (0, 4)
+    ]
+
+
+def piece_of(cells):
+    return cells.reshape(LANES, cells.shape[-1]).T.astype(BF16)
+
+
+def last_piece_of(quad):
+    channels = quad.shape[-1]
+    pairs = quad.reshape(8, 2, *quad.shape[1:])
+    high = jnp.concatenate([pairs[:, 0, 20:24], pairs[:, 1, 20:24]], axis=1)
+    low = jnp.concatenate([pairs[:, 0, 0:4], pairs[:, 1, 0:4]], axis=1)
+    return piece_of(jnp.concatenate([high.reshape(64, channels), low.reshape(64, channels)], axis=0))
 
 
 def quadrant_of(first, second, last):
@@ -57,44 +60,59 @@
     return whole.reshape(4, 4, 24, channels).astype(BF16)
 
 
-def pack_kernel(tokens_ref, cot_ref, *refs):
-    first_refs, rest_refs, (buffer, sems) = refs[:4], refs[4:8], refs[8:]
-    sources = (tokens_ref, cot_ref)
-
-    def copy(which, x):
-        return pltpu.make_async_copy(
-            sources[which].at[pl.ds(2 * x, 2)], buffer.at[which, pl.ds(2 * x, 2)], sems.at[which, x]
+def read_block(sources, buffer, sems, depth):
+    copies = [
+        pltpu.make_async_copy(
+            source.at[pl.ds(2 * x, 2), :, pl.ds(0, depth)],
+            buffer.at[which, pl.ds(2 * x, 2)],
+            sems.at[which, x],
         )
-
+        for which, source in enumerate(sources)
+        for x in range(4)
+    ]
+    for copy in copies:
+        copy.start()
+    return copies
+
+
+def pack_first_kernel(tokens_ref, cot_ref, *refs):
+    outs, (buffer, sems) = refs[:4], refs[4:]
+    copies = read_block((tokens_ref, cot_ref), buffer, sems, buffer.shape[3])
     for which in range(2):
-        for x in range(4):
-            copy(which, x).start()
+        for copy in copies[4 * which : 4 * which + 4]:
+            copy.wait()
+        for i, quad in enumerate(quadrants(buffer[which].astype(F32))):
+            outs[i][which] = piece_of(quad[:, 4:12])
+
+
+def pack_rest_kernel(tokens_ref, cot_ref, *refs):
+    outs, (buffer, sems) = refs[:4], refs[4:]
+    copies = read_block((tokens_ref, cot_ref), buffer, sems, buffer.shape[3])
     for which in range(2):
-        for x in range(4):
-            copy(which, x).wait()
-    for which in range(2):
-        pieces = pieces_of(buffer[which].astype(F32))
-        for xh in range(2):
-            for yh in range(2):
-                first, second, last = pieces[xh, yh]
-                first_refs[xh * 2 + yh][which] = first
-                rest_refs[xh * 2 + yh][0, which] = last
-                rest_refs[xh * 2 + yh][1, which] = second
-
-
-def packed(tokens, cotangent):
-    channels = tokens.shape[-1]
-    S = jax.ShapeDtypeStruct
-    outs = pl.pallas_call(
-        pack_kernel,
-        out_shape=(S((2, channels, LANES), BF16),) * 4 + (S((2, 2, channels, LANES), BF16),) * 4,
+        for copy in copies[4 * which : 4 * which + 4]:
+            copy.wait()
+        for i, quad in enumerate(quadrants(buffer[which].astype(F32))):
+            outs[i][0, which] = last_piece_of(quad)
+            outs[i][1, which] = piece_of(quad[:, 12:20])
+
+
+def packed(tokens, cotangent, first):
+    tile_x, tile_y, depth, channels = tokens.shape
+    piece = (2, channels, LANES)
+    shape = piece if first else (2, *piece)
+    held = 2 * WIN if first else depth
+    return pl.pallas_call(
+        pack_first_kernel if first else pack_rest_kernel,
+        out_shape=(jax.ShapeDtypeStruct(shape, BF16),) * 4,
         in_specs=[pl.BlockSpec(memory_space=pltpu.HBM)] * 2,
-        out_specs=(VMEM,) * 8,
-        scratch_shapes=[pltpu.VMEM((2, *tokens.shape), BF16), pltpu.SemaphoreType.DMA((2, 4))],
+        out_specs=(VMEM,) * 4,
+        scratch_shapes=[
+            pltpu.VMEM((2, tile_x, tile_y, held, channels), BF16),
+            pltpu.SemaphoreType.DMA((2, 4)),
+        ],
         compiler_params=pltpu.CompilerParams(vmem_limit_bytes=62 * 2**20),
-        name="pack",
+        name="pack_first" if first else "pack_rest",
     )(tokens, cotangent)
-    return outs[:4], outs[4:]
 
 
 def prepare_kernel(
@@ -172,7 +190,7 @@
     given = (0, 5, 1)[turn]
     earlier_refs, refs = refs[:given], refs[given:]
     y_refs, grads_ref, scratch = refs[:4], refs[4], refs[5:]
-    (qkv_s, gm_s, mix_s, gqkv_s, kv_s, qa_s, ga_s, e_s, pb_s, dp_s, ds_s, r_s, d_s) = scratch
+    (qkv_s, gm_s, mix_s, gqkv_s, k_s, q_s, v_s, g_s, e_s, p_s, pb_s, dp_s, ds_s, dst_s, r_s, d_s) = scratch
     quads = (q00_ref, q01_ref, q10_ref, q11_ref)
     if turn:
         quads = [quad.at[turn - 1] for quad in quads]
@@ -206,11 +224,16 @@
     layout = 1 if halves else 0
     size = cells // 2 if halves else cells
     groups = [slice(start, start + size) for start in range(0, cells, size)]
-    step_rows = 64 * (cells // size)
     chunks = [
-        (gi, slice(c, c + step_rows), group)
+        (gi, slice(c, c + LANES), slice(c - group.start, c - group.start + LANES), group)
         for gi, group in enumerate(groups)
-        for c in range(group.start, group.stop, step_rows)
+        for c in range(group.start, group.stop, LANES)
+    ]
+    part = cells // 2
+    parts = [
+        (groups[min(i, len(groups) - 1)], slice(i * part, (i + 1) * part),
+         slice(i * part % size, i * part % size + part))
+        for i in range(2)
     ]
     scale = hd**-0.5
 
@@ -239,77 +262,77 @@
         qf = qkv_s[q_rows(h)].astype(F32) * (scale * LOG2E)
         q_hi = qf.astype(BF16)
         q_lo = (qf - q_hi.astype(F32)).astype(BF16)
-        none = jnp.zeros_like(k)
-        kv_s[slot] = jnp.concatenate([k, k, kf_ref[layout], qkv_s[v_rows(h)]], axis=0).T
-        qa_s[slot] = jnp.concatenate([q_hi, q_lo, qf_ref[layout], none], axis=0)
-        ga_s[slot] = jnp.concatenate([none, none, none, gm_s[q_rows(h)]], axis=0)
+        k_s[slot] = jnp.concatenate([k, k, kf_ref[layout]], axis=0).T
+        q_s[slot] = jnp.concatenate([q_hi, q_lo, qf_ref[layout]], axis=0)
+        v_s[slot] = qkv_s[v_rows(h)].T
+        g_s[slot] = gm_s[q_rows(h)]
 
     def exponentials(slot, chunk, total):
-        gi, rows, cols = chunk
-        e = jnp.exp2(dot(kv_s[slot, rows], qa_s[slot, :, cols]))
+        gi, rows, _, cols = chunk
+        e = jnp.exp2(dot(k_s[slot, rows], q_s[slot, :, cols]))
         e_s[slot, rows] = e
         added(total, gi, folded(e))
 
     def attention(slot, chunk, total):
-        gi, rows, cols = chunk
+        gi, rows, _, cols = chunk
         p = e_s[slot, rows] * r_s[slot, 0:1, cols]
-        e_s[slot, rows] = p
-        pb_s[rows] = p.astype(BF16)
-        dp = dot(kv_s[slot, rows], ga_s[slot, :, cols])
-        dp_s[rows] = dp
+        p_s[slot, rows] = p
+        pb_s[slot, rows] = p.astype(BF16)
+        dp = dot(v_s[slot, rows], g_s[slot, :, cols])
+        dp_s[slot, rows] = dp
         added(total, gi, folded(p * dp))
 
     def grad_scores(slot, chunk):
-        _, rows, cols = chunk
-        ds_s[slot, rows] = (e_s[slot, rows] * (dp_s[rows] - d_s[0:1, cols])).astype(BF16)
-
-    def mixed_of(h):
-        for cols in groups:
-            mix_s[q_rows(h), cols] = dot(qkv_s[v_rows(h), cols], pb_s[cols]).astype(BF16)
-
-    def grad_values_of(h):
-        for cols in groups:
-            gv = lax.dot_general(gm_s[q_rows(h), cols], pb_s[cols], NT, preferred_element_type=F32)
-            gqkv_s[v_rows(h), cols] = gv.astype(BF16)
-
-    def grad_queries_of(h, slot):
-        for cols in groups:
-            gq = dot(qkv_s[k_rows(h), cols], ds_s[slot, cols]) * scale
-            gqkv_s[q_rows(h), cols] = gq.astype(BF16)
-
-    def grad_keys_of(h, slot):
-        for cols in groups:
-            gk = lax.dot_general(
-                qkv_s[q_rows(h), cols], ds_s[slot, cols], NT, preferred_element_type=F32
-            )
-            gqkv_s[k_rows(h), cols] = (gk * scale).astype(BF16)
-
-    def keep_inverse(slot, total):
+        _, rows, place, cols = chunk
+        ds = (p_s[slot, rows] * (dp_s[slot, rows] - d_s[slot, 0:1, cols])).astype(BF16)
+        ds_s[slot, rows] = ds
+        dst_s[slot, cols, place] = ds.T
+
+    def mixed_part(h, slot, i):
+        over, out, place = parts[i]
+        mix_s[q_rows(h), out] = dot(qkv_s[v_rows(h), over], pb_s[slot, over, place]).astype(BF16)
+
+    def grad_values_part(h, slot, i):
+        over, out, _ = parts[i]
+        gv = lax.dot_general(
+            gm_s[q_rows(h), over], pb_s[slot, out], NT, preferred_element_type=F32
+        )
+        gqkv_s[v_rows(h), out] = gv.astype(BF16)
+
+    def grad_queries_part(h, slot, i):
+        over, out, place = parts[i]
+        gq = dot(qkv_s[k_rows(h), over], ds_s[slot, over, place]) * scale
+        gqkv_s[q_rows(h), out] = gq.astype(BF16)
+
+    def grad_keys_part(h, slot, i):
+        over, out, place = parts[i]
+        gk = dot(qkv_s[q_rows(h), over], dst_s[slot, over, place]) * scale
+        gqkv_s[k_rows(h), out] = gk.astype(BF16)
+
+    def kept(ref, slot, total, of):
         for gi, cols in enumerate(groups):
-            r_s[slot, 0:1, cols] = 1.0 / jnp.sum(total[gi], axis=0, keepdims=True)
-
-    def step(i, slot, first=True, final=True, ahead=True):
+            ref[slot, 0:1, cols] = of(jnp.sum(total[gi], axis=0, keepdims=True))
+
+    def step(i, slot, one=True, two=True, three=True, four=True, ahead=True):
         sums = [None] * len(groups)
         inner = [None] * len(groups)
-        count = len(chunks)
         for c, chunk in enumerate(chunks):
-            if first:
+            if c % 2 == 0 and three:
+                mixed_part(i - 2, slot, c // 2)
+                grad_values_part(i - 2, slot, c // 2)
+            if c % 2 == 1 and four:
+                grad_queries_part(i - 3, 1 - slot, c // 2)
+                grad_keys_part(i - 3, 1 - slot, c // 2)
+            if one:
                 exponentials(slot, chunk, sums)
-            attention(1 - slot, chunk, inner)
-            if final and c == count // 4:
-                grad_queries_of(i - 2, slot)
-            if final and c == 3 * count // 4:
-                grad_keys_of(i - 2, slot)
-        if first:
-            keep_inverse(slot, sums)
-        for gi, cols in enumerate(groups):
-            d_s[0:1, cols] = jnp.sum(inner[gi], axis=0, keepdims=True)
-        for c, chunk in enumerate(chunks):
-            grad_scores(1 - slot, chunk)
-            if c == 0:
-                mixed_of(i - 1)
-            if c == count // 2:
-                grad_values_of(i - 1)
+            if two:
+                attention(1 - slot, chunk, inner)
+            if three:
+                grad_scores(slot, chunk)
+        if one:
+            kept(r_s, slot, sums, lambda total: 1.0 / total)
+        if two:
+            kept(d_s, 1 - slot, inner, lambda total: total)
         if ahead:
             prepare(i + 1, 1 - slot)
 
@@ -321,41 +344,40 @@
     @pl.when(in_range)
     def _():
         prepare(0, 0)
-        prepare(1, 1)
-        sums = [None] * len(groups)
-        for chunk in chunks:
-            exponentials(0, chunk, sums)
-        keep_inverse(0, sums)
-        step(1, 1, final=False)
+        step(0, 0, two=False, three=False, four=False)
+        step(1, 1, three=False, four=False)
+        step(2, 0, four=False)
 
         def two_steps(j, carry):
-            step(2 + 2 * j, 0)
             step(3 + 2 * j, 1)
+            step(4 + 2 * j, 0)
             return carry
 
         lax.fori_loop(0, (HEADS - 4) // 2, two_steps, 0)
-        step(HEADS - 2, 0)
         step(HEADS - 1, 1, ahead=False)
-        step(HEADS, 0, first=False, ahead=False)
-        grad_queries_of(HEADS - 1, 1)
-        grad_keys_of(HEADS - 1, 1)
+        step(HEADS, 0, one=False, ahead=False)
+        step(HEADS + 1, 1, one=False, two=False, ahead=False)
+        step(HEADS + 2, 0, one=False, two=False, three=False, ahead=False)
 
     @pl.when(jnp.logical_not(in_range))
     def _():
         def head(h, carry):
             prepare(h, 0)
             for cols in groups:
-                s = dot(kv_s[0, cols], qa_s[0, :, cols])
+                s = dot(k_s[0, cols], q_s[0, :, cols])
                 e = jnp.exp2(s - jnp.max(s, axis=0, keepdims=True))
                 p = e * (1.0 / jnp.sum(e, axis=0, keepdims=True))
-                pb_s[cols] = p.astype(BF16)
-                dp = dot(kv_s[0, cols], ga_s[0, :, cols])
+                pb_s[0, cols] = p.astype(BF16)
+                dp = dot(v_s[0, cols], g_s[0, :, cols])
                 inner = jnp.sum(p * dp, axis=0, keepdims=True)
-                ds_s[0, cols] = (p * (dp - inner)).astype(BF16)
-            mixed_of(h)
-            grad_values_of(h)
-            grad_queries_of(h, 0)
-            grad_keys_of(h, 0)
+                ds = (p * (dp - inner)).astype(BF16)
+                ds_s[0, cols] = ds
+                dst_s[0, cols] = ds.T
+            for i in range(2):
+                mixed_part(h, 0, i)
+                grad_values_part(h, 0, i)
+                grad_queries_part(h, 0, i)
+                grad_keys_part(h, 0, i)
             return carry
 
         lax.fori_loop(0, HEADS, head, 0)
@@ -429,15 +451,18 @@
             pltpu.VMEM((channels, cells), BF16),
             pltpu.VMEM((channels, cells), BF16),
             pltpu.VMEM((3 * channels, cells), BF16),
-            pltpu.VMEM((2, cells, 64), BF16),
-            pltpu.VMEM((2, 64, cells), BF16),
-            pltpu.VMEM((2, 64, cells), BF16),
+            pltpu.VMEM((2, cells, 48), BF16),
+            pltpu.VMEM((2, 48, cells), BF16),
+            pltpu.VMEM((2, cells, 16), BF16),
+            pltpu.VMEM((2, 16, cells), BF16),
             pltpu.VMEM((2, cells, width), F32),
-            pltpu.VMEM((cells, width), BF16),
-            pltpu.VMEM((cells, width), F32),
+            pltpu.VMEM((2, cells, width), F32),
+            pltpu.VMEM((2, cells, width), BF16),
+            pltpu.VMEM((2, cells, width), F32),
+            pltpu.VMEM((2, cells, width), BF16),
             pltpu.VMEM((2, cells, width), BF16),
             pltpu.VMEM((2, 8, cells), F32),
-            pltpu.VMEM((8, cells), F32),
+            pltpu.VMEM((2, 8, cells), F32),
         ],
         compiler_params=pltpu.CompilerParams(vmem_limit_bytes=40 * 2**20),
         cost_estimate=pl.CostEstimate(
@@ -457,64 +482,46 @@
     return lax.ppermute(block, ("gx", "gy"), route)
 
 
-def summed(rows):
+def summed(rows, beside):
     nx, ny = lax.axis_size("gx"), lax.axis_size("gy")
     near = 2 * ny
     planes = [[near * i + j for j in range(near)] for i in range(nx // 2)]
     across = [list(ids) for ids in zip(*planes)]
-
-    def exchanged(pieces, groups):
-        return lax.all_to_all(pieces, ("gx", "gy"), 0, 0, axis_index_groups=groups)
+    beside = list(beside)
+
+    def exchanged(pieces, groups, turn):
+        got = lax.all_to_all(pieces, ("gx", "gy"), 0, 0, axis_index_groups=groups)
+        if turn < 2:
+            got, beside[turn] = lax.optimization_barrier((got, beside[turn]))
+        return got
 
     def copies(piece, count):
         return jnp.broadcast_to(piece[None], (count, *piece.shape))
 
-    got = exchanged(rows.reshape(near, -1, LANES), planes)
+    got = exchanged(rows.reshape(near, -1, LANES), planes, 0)
     mine = jnp.sum(got.astype(F32), axis=0).astype(BF16)
-    got = exchanged(copies(mine, nx // 2), across)
+    got = exchanged(copies(mine, nx // 2), across, 1)
     total = jnp.sum(got.astype(F32), axis=0).astype(BF16)
-    return exchanged(copies(total, near), planes).reshape(rows.shape)
-
-
-def grads_kernel(
-    factor, rows_ref, dw_ref, dproj_ref, gain_ref, bias_ref, dw_s, dproj_s, ends_s, out_sems
-):
-    channels = dw_s.shape[0]
+    return exchanged(copies(total, near), planes, 2).reshape(rows.shape), beside
+
+
+def grads_kernel(factor, rows_ref, dw_ref, dproj_ref, gain_ref, bias_ref):
+    channels = dw_ref.shape[0]
     blocks = 4 * channels // LANES
+    joined = jnp.concatenate(
+        [rows_ref[i * channels : (i + 1) * channels].astype(F32) for i in range(blocks)], axis=1
+    ) * factor
+    dw_ref[...] = joined[:, : 3 * channels]
+    dproj_ref[...] = joined[:, 3 * channels :]
     used = blocks * channels
-    outgoing = []
-
-    def send(src, dst):
-        copy = pltpu.make_async_copy(src, dst, out_sems.at[len(outgoing)])
-        copy.start()
-        outgoing.append(copy)
-
-    def block(i):
-        return rows_ref[i * channels : (i + 1) * channels].astype(F32) * factor
-
-    whole = 3 * channels // LANES
-    for i in range(whole):
-        dw_s[:, i * LANES : (i + 1) * LANES] = block(i)
-        if i % 2:
-            cols = pl.ds((i - 1) * LANES, 2 * LANES)
-            send(dw_s.at[:, cols], dw_ref.at[:, cols])
-    rest = jnp.concatenate([block(i) for i in range(whole, blocks)], axis=1)
-    edge = 3 * channels - whole * LANES
-    dw_s[:, whole * LANES :] = rest[:, :edge]
-    send(dw_s.at[:, pl.ds(whole * LANES, edge)], dw_ref.at[:, pl.ds(whole * LANES, edge)])
-    dproj_s[...] = rest[:, edge:]
-    send(dproj_s, dproj_ref)
     tail = rows_ref[used : used + 16].astype(F32) * factor
-    ends_s[...] = jnp.concatenate([tail[:8], tail[8:]], axis=1)[:, :channels]
-    gain_ref[...] = ends_s[0:1]
-    bias_ref[...] = ends_s[1:2]
-    for copy in outgoing:
-        copy.wait()
+    tail = jnp.concatenate([tail[:8], tail[8:]], axis=1)[:, :channels]
+    gain_ref[...] = tail[0:1]
+    bias_ref[...] = tail[1:2]
 
 
 def grads_of(rows, channels, factor):
     S = jax.ShapeDtypeStruct
-    anywhere = pl.BlockSpec(memory_space=pltpu.HBM)
     return pl.pallas_call(
         functools.partial(grads_kernel, factor),
         out_shape=(
@@ -524,13 +531,7 @@
             S((1, channels), F32),
         ),
         in_specs=[VMEM],
-        out_specs=(anywhere, anywhere, VMEM, VMEM),
-        scratch_shapes=[
-            pltpu.VMEM((channels, 3 * channels), F32),
-            pltpu.VMEM((channels, channels), F32),
-            pltpu.VMEM((8, channels), F32),
-            pltpu.SemaphoreType.DMA((4,)),
-        ],
+        out_specs=(VMEM,) * 4,
         name="unpack_grads",
     )(rows)
 
@@ -538,10 +539,11 @@
 def shards(tokens, cotangent, ln_gain, ln_bias, qkv_weight, proj_weight):
     tile_x, tile_y, depth, channels = tokens.shape
     nx, ny = lax.axis_size("gx"), lax.axis_size("gy")
-    first, rest = packed(tokens, cotangent)
-    first, ln_gain, ln_bias, qkv_weight, proj_weight = lax.optimization_barrier(
-        (first, ln_gain, ln_bias, qkv_weight, proj_weight)
+    first = packed(tokens, cotangent, True)
+    first, tokens, cotangent, ln_gain, ln_bias, qkv_weight, proj_weight = lax.optimization_barrier(
+        (first, tokens, cotangent, ln_gain, ln_bias, qkv_weight, proj_weight)
     )
+    rest = packed(tokens, cotangent, False)
     gain, bias, wqkv_t, proj_t, *features = prepared(ln_gain, ln_bias, qkv_weight, proj_weight)
     weights = (gain, bias, wqkv_t, qkv_weight, proj_weight, proj_t)
 
@@ -560,7 +562,7 @@
     *y, sums = attend(2, rest, features, weights, (sums,))
     middle = returned(y)
     sums, paired = lax.optimization_barrier((sums, paired))
-    total = summed(sums)
+    total, middle[:3] = summed(sums, middle[:3])
     block_out, d_tokens = unpacked(paired, middle, tokens.shape)
     factor = 1.0 / math.sqrt(tile_x * nx * tile_y * ny * depth)
     dw, dproj, dgain, dbias = grads_of(total, channels, factor)

time: 120 us -> 118 us (0.983)
  blocking collectives: 33.3 us -> 0 us
  starting transfers between devices: 30.8 us -> 49.1 us
  waiting for transfers between devices: 7.71 us -> 21.3 us
    all_to_all x2 -> x0, blocking collectives: 33.3 us -> none  [exchanged(): return lax.all_to_all(pieces, ('gx', 'gy'), 0, 0, axis_index_groups=groups)]
    all_to_all x1 -> x3, starting transfers between devices: 5.31 us -> 19.6 us  [exchanged(): got = lax.all_to_all(pieces, ('gx', 'gy'), 0, 0, axis_index_groups=groups)]
    ppermute x12, waiting for transfers between devices: 6.29 us -> 13.9 us  [moved(): return lax.ppermute(block, ('gx', 'gy'), route)]
    all_to_all x1 -> x3, waiting for transfers between devices: 1.42 us -> 7.39 us  [exchanged(): got = lax.all_to_all(pieces, ('gx', 'gy'), 0, 0, axis_index_groups=groups)]
    ppermute x12, starting transfers between devices: 25.5 us -> 29.5 us  [moved(): return lax.ppermute(block, ('gx', 'gy'), route)]
    pallas_call x3, Pallas kernels: 35.3 us -> 33.1 us  [attend(): pl.pallas_call(functools.partial(attend_kernel, turn), out_shape=(S((2, *...]
    pallas_call x1 -> x2, Pallas kernels: 3.05 us -> 4.8 us  [packed(): pl.pallas_call(pack_first_kernel if first else pack_rest_kernel, out_shap...]
  transfers between devices with their start and end apart: 13 -> 15, of which waited for: 3 -> 5; matrix products, arithmetic and copies ran while one was open for 0% -> 0% of each run, Pallas kernels for 21% -> 27%
where the time goes in v1:
time: 118 us; the launch traced here: 116 us
  starting transfers between devices  49.1 us (42%)
  Pallas kernels  41.7 us (35%)
  waiting for transfers between devices  21.3 us (18%)
  local copies, waits for them, and re-layouts  3.35 us (3%)
    pallas_call x3, Pallas kernels, attend(): pl.pallas_call(functools.partial(attend_kernel, turn), out_shape=(S((2, *...  33.1 us
    ppermute x12, starting transfers between devices, moved(): return lax.ppermute(block, ('gx', 'gy'), route)  29.5 us
    all_to_all x3, starting transfers between devices, exchanged(): got = lax.all_to_all(pieces, ('gx', 'gy'), 0, 0, axis_index_groups=groups)  19.6 us
    ppermute x12, waiting for transfers between devices, moved(): return lax.ppermute(block, ('gx', 'gy'), route)  13.9 us
    all_to_all x3, waiting for transfers between devices, exchanged(): got = lax.all_to_all(pieces, ('gx', 'gy'), 0, 0, axis_index_groups=groups)  7.39 us
    pallas_call x2, Pallas kernels, packed(): pl.pallas_call(pack_first_kernel if first else pack_rest_kernel, out_shap...  4.8 us
  transfers between devices with their start and end apart: 15, of which 5 were waited for; matrix products, arithmetic and copies ran while one was open for 0% of the time, Pallas kernels for 27%

profile of v1, /device:TPU:1, one launch (start us, length us, event | category | flops | bytes accessed | tf_op | source)
XLA Modules:
  0.0 116.3 jit_solution(12668584672913302004)
XLA Ops:
  0.6 2.2 %pack_first.1 = (bf16[2,192,128]{2,1,0:T(8,128)(2,1)}, bf16[2,192,128]{2,1,0:T(8,128)(2,1)}, bf16[2,192,128]{2,1,0:T(8,128)(2,1)}, bf16[2,192,128]{2,1,0:T(8,128)(2,1)}) custom-call(bf16[8,8,24,192]{3,2,1,0:T(8,128)(2,1)} %tokens_ref.2, bf16[8,8,24,192]{3,2,1,0:T(8,128)(2,1)} %cot_ref.2), custom_call_target="tpu_custom_call" | custom-call | tf_op jit(solution)/shard_map/pack_first/pallas_call | solution.py:104
  2.9 0.0 copy-start
  2.9 0.0 copy-start.1
  2.9 8.0 %collective-permute-start.3 = (bf16[2,192,128]{2,1,0:T(8,128)(2,1)}, bf16[2,192,128]{2,1,0:T(8,128)(2,1)S(1)}, u32[]{:S(2)}, u32[]{:S(2)}) collective-permute-start(bf16[2,192,128]{2,1,0:T(8,128)(2,1)} %get-tuple-element.80), channel_id=1, source_target_pairs={{0,255},{1,240},{2,241},{3,242},{4,243},{5,244},{6,245},{7,246},{8... | collective-permute-start | bytes 294920 | tf_op jit(solution)/shard_map/ppermute | solution.py:482
  10.9 0.3 collective-permute-start.4
  11.1 3.5 %collective-permute-start.5 = (bf16[2,192,128]{2,1,0:T(8,128)(2,1)}, bf16[2,192,128]{2,1,0:T(8,128)(2,1)S(1)}, u32[]{:S(2)}, u32[]{:S(2)}) collective-permute-start(bf16[2,192,128]{2,1,0:T(8,128)(2,1)} %get-tuple-element.82), channel_id=1, source_target_pairs={{0,15},{1,0},{2,1},{3,2},{4,3},{5,4},{6,5},{7,6},{8,7},{9,8},{10,9... | collective-permute-start | bytes 294920 | tf_op jit(solution)/shard_map/ppermute | solution.py:482
  14.6 2.6 %pack_rest.1 = (bf16[2,2,192,128]{3,2,1,0:T(8,128)(2,1)}, bf16[2,2,192,128]{3,2,1,0:T(8,128)(2,1)}, bf16[2,2,192,128]{3,2,1,0:T(8,128)(2,1)}, bf16[2,2,192,128]{3,2,1,0:T(8,128)(2,1)}) custom-call(bf16[8,8,24,192]{3,2,1,0:T(8,128)(2,1)} %tokens_ref.2, bf16[8,8,24,192]{3,2,1,0:T(8,128)(2,1)} %cot_ref.2), custom_call_target="tpu_custom_call" | custom-call | tf_op jit(solution)/shard_map/pack_rest/pallas_call | solution.py:104
  17.2 2.8 %collective-permute-start = (bf16[2,2,192,128]{3,2,1,0:T(8,128)(2,1)}, bf16[2,2,192,128]{3,2,1,0:T(8,128)(2,1)S(1)}, u32[]{:S(2)}, u32[]{:S(2)}) collective-permute-start(bf16[2,2,192,128]{3,2,1,0:T(8,128)(2,1)} %get-tuple-element.66), channel_id=1, source_target_pairs={{0,255},{1,240},{2,241},{3,242},{4,243},{5,244},{6,245},{7,246},{8... | collective-permute-start | bytes 589832 | tf_op jit(solution)/shard_map/ppermute | solution.py:482
  20.0 1.2 collective-permute-start.1
  21.2 0.0 copy-done
  21.2 0.0 copy-done.1
  21.2 0.7 copy-done.2
  21.8 0.3 prepare.1
  22.1 0.0 collective-permute-done.3.q00_ref
  22.1 0.1 collective-permute-start.2
  22.2 0.0 collective-permute-done.4.q01_ref
  22.2 0.0 collective-permute-done.5.q10_ref
  22.2 0.5 copy-done.5
  22.8 10.7 %attend.3 = (bf16[2,192,128]{2,1,0:T(8,128)(2,1)S(1)}, bf16[2,192,128]{2,1,0:T(8,128)(2,1)S(1)}, bf16[2,192,128]{2,1,0:T(8,128)(2,1)S(1)}, bf16[2,192,128]{2,1,0:T(8,128)(2,1)S(1)}, f32[1280,128]{1,0:T(8,128)S(1)}) custom-call(bf16[2,192,128]{2,1,0:T(8,128)(2,1)S(1)} %collective-permute-done.3.q00_ref, ...), custom_call_target="tpu_custom_call" | custom-call | flops 9663676416 | bytes 4194304 | tf_op jit(solution)/shard_map/attend/pallas_call | solution.py:443
  33.4 0.0 collective-permute-done.q00_ref
  33.4 0.0 collective-permute-done.1.q01_ref
  33.4 0.0 collective-permute-done.2.q10_ref
  33.4 6.0 %attend.4 = (bf16[2,2,192,128]{3,2,1,0:T(8,128)(2,1)S(1)}, bf16[2,2,192,128]{3,2,1,0:T(8,128)(2,1)S(1)}, bf16[2,2,192,128]{3,2,1,0:T(8,128)(2,1)S(1)}, bf16[2,2,...) custom-call(bf16[2,2,192,128]{3,2,1,0:T(8,128)(2,1)S(1)} %collective-permute-done.q00_ref, ...), custom_call_target="tpu_custom_call" | custom-call | flops 9663676416 | bytes 4194304 | tf_op jit(solution)/shard_map/attend/pallas_call | solution.py:443
  39.5 6.0 %collective-permute-start.6 = (bf16[2,2,192,128]{3,2,1,0:T(8,128)(2,1)S(1)}, bf16[2,2,192,128]{3,2,1,0:T(8,128)(2,1)S(1)}, u32[]{:S(2)}, u32[]{:S(2)}) collective-permute-start(bf16[2,2,192,128]{3,2,1,0:T(8,128)(2,1)S(1)} %get-tuple-element.91), channel_id=1, source_target_pairs={{0,17},{1,18},{2,19},{3,20},{4,21},{5,22},{6,23},{7,24},{8,25},{9,... | collective-permute-start | bytes 589832 | tf_op jit(solution)/shard_map/ppermute | solution.py:482
  45.5 1.6 %collective-permute-start.7 = (bf16[2,2,192,128]{3,2,1,0:T(8,128)(2,1)S(1)}, bf16[2,2,192,128]{3,2,1,0:T(8,128)(2,1)S(1)}, u32[]{:S(2)}, u32[]{:S(2)}) collective-permute-start(bf16[2,2,192,128]{3,2,1,0:T(8,128)(2,1)S(1)} %get-tuple-element.92), channel_id=1, source_target_pairs={{0,16},{1,17},{2,18},{3,19},{4,20},{5,21},{6,22},{7,23},{8,24},{9,... | collective-permute-start | bytes 589832 | tf_op jit(solution)/shard_map/ppermute | solution.py:482
  47.1 0.0 collective-permute-start.8
  47.1 16.5 %attend.5 = (bf16[2,192,128]{2,1,0:T(8,128)(2,1)S(1)}, bf16[2,192,128]{2,1,0:T(8,128)(2,1)S(1)}, bf16[2,192,128]{2,1,0:T(8,128)(2,1)S(1)}, bf16[2,192,128]{2,1,0:T(8,128)(2,1)S(1)}, bf16[1280,128]{1,0:T(8,128)(2,1)}) custom-call(bf16[2,2,192,128]{3,2,1,0:T(8,128)(2,1)S(1)} %collective-permute-done.q00_ref, ...), custom_call_target="tpu_custom_call" | custom-call | flops 9663676416 | bytes 4194304 | tf_op jit(solution)/shard_map/attend/pallas_call | solution.py:443
  63.6 0.0 collective-permute-done.6.refs_0_
  63.6 0.0 collective-permute-done.7.refs_1_
  63.6 0.0 collective-permute-done.8.refs_2_
  63.6 11.3 %all-to-all-start = ((bf16[32,40,128]{2,1,0:T(8,128)(2,1)}), bf16[32,40,128]{2,1,0:T(8,128)(2,1)S(1)}, u32[]{:S(2)}, u32[]{:S(2)}) async-start(bf16[32,40,128]{2,1,0:T(8,128)(2,1)} %bitcast.2), calls=%async_computation | async-start | bytes 655360 | tf_op jit(solution)/shard_map/all_to_all | solution.py:493
  74.9 2.6 %collective-permute-start.9 = (bf16[2,192,128]{2,1,0:T(8,128)(2,1)S(1)}, bf16[2,192,128]{2,1,0:T(8,128)(2,1)S(1)}, u32[]{:S(2)}, u32[]{:S(2)}) collective-permute-start(bf16[2,192,128]{2,1,0:T(8,128)(2,1)S(1)} %get-tuple-element.100), channel_id=1, source_target_pairs={{0,17},{1,18},{2,19},{3,20},{4,21},{5,22},{6,23},{7,24},{8,25},{9,... | collective-permute-start | bytes 294920 | tf_op jit(solution)/shard_map/ppermute | solution.py:482
  77.5 4.2 %collective-permute-done.9.refs_4_ = bf16[2,192,128]{2,1,0:T(8,128)(2,1)S(1)} collective-permute-done((bf16[2,192,128]{2,1,0:T(8,128)(2,1)S(1)}, bf16[2,192,128]{2,1,0:T(8,128)(2,1)S(1)}, u32[]{:S(2)}, u32[]{:S(2)}) %collective-permute-start.9) | collective-permute-done | bytes 98336 | tf_op jit(solution)/shard_map/ppermute | solution.py:482
  81.8 3.7 %all-to-all-done = bf16[32,40,128]{2,1,0:T(8,128)(2,1)S(1)} async-done(((bf16[32,40,128]{2,1,0:T(8,128)(2,1)}), bf16[32,40,128]{2,1,0:T(8,128)(2,1)S(1)}, u32[]{:S(2)}, u32[]{:S(2)}) %all-to-all-start) | async-done | bytes 327712 | tf_op jit(solution)/shard_map/all_to_all | solution.py:493
  85.4 0.1 reduce_sum.24
  85.5 0.6 broadcast_in_dim.20
  86.1 3.4 %all-to-all-start.1 = ((bf16[8,40,128]{2,1,0:T(8,128)(2,1)}), bf16[8,40,128]{2,1,0:T(8,128)(2,1)S(1)}, u32[]{:S(2)}, u32[]{:S(2)}) async-start(bf16[8,40,128]{2,1,0:T(8,128)(2,1)} %broadcast_in_dim.20), calls=%async_computation.1 | async-start | bytes 163840 | tf_op jit(solution)/shard_map/all_to_all | solution.py:493
  89.5 1.8 %collective-permute-start.10 = (bf16[2,192,128]{2,1,0:T(8,128)(2,1)S(1)}, bf16[2,192,128]{2,1,0:T(8,128)(2,1)S(1)}, u32[]{:S(2)}, u32[]{:S(2)}) collective-permute-start(bf16[2,192,128]{2,1,0:T(8,128)(2,1)S(1)} %get-tuple-element.103), channel_id=1, source_target_pairs={{0,16},{1,17},{2,18},{3,19},{4,20},{5,21},{6,22},{7,23},{8,24},{9,... | collective-permute-start | bytes 294920 | tf_op jit(solution)/shard_map/ppermute | solution.py:482
  91.3 6.9 %collective-permute-done.10.refs_5_ = bf16[2,192,128]{2,1,0:T(8,128)(2,1)S(1)} collective-permute-done((bf16[2,192,128]{2,1,0:T(8,128)(2,1)S(1)}, bf16[2,192,128]{2,1,0:T(8,128)(2,1)S(1)}, u32[]{:S(2)}, u32[]{:S(2)}) %collective-permute-start.10) | collective-permute-done | bytes 98336 | tf_op jit(solution)/shard_map/ppermute | solution.py:482
  98.2 0.0 all-to-all-done.1
  98.2 0.8 broadcast_in_dim.21
  99.0 4.9 %all-to-all-start.2 = ((bf16[32,40,128]{2,1,0:T(8,128)(2,1)}), bf16[32,40,128]{2,1,0:T(8,128)(2,1)S(1)}, u32[]{:S(2)}, u32[]{:S(2)}) async-start(bf16[32,40,128]{2,1,0:T(8,128)(2,1)} %broadcast_in_dim.21), calls=%async_computation.2 | async-start | bytes 655360 | tf_op jit(solution)/shard_map/all_to_all | solution.py:493
  103.9 1.7 %collective-permute-start.11 = (bf16[2,192,128]{2,1,0:T(8,128)(2,1)S(1)}, bf16[2,192,128]{2,1,0:T(8,128)(2,1)S(1)}, u32[]{:S(2)}, u32[]{:S(2)}) collective-permute-start(bf16[2,192,128]{2,1,0:T(8,128)(2,1)S(1)} %get-tuple-element.105), channel_id=1, source_target_pairs={{0,1},{1,2},{2,3},{3,4},{4,5},{5,6},{6,7},{7,8},{8,9},{9,10},{10,1... | collective-permute-start | bytes 294920 | tf_op jit(solution)/shard_map/ppermute | solution.py:482
  105.6 2.8 %collective-permute-done.11.refs_6_ = bf16[2,192,128]{2,1,0:T(8,128)(2,1)S(1)} collective-permute-done((bf16[2,192,128]{2,1,0:T(8,128)(2,1)S(1)}, bf16[2,192,128]{2,1,0:T(8,128)(2,1)S(1)}, u32[]{:S(2)}, u32[]{:S(2)}) %collective-permute-start.11) | collective-permute-done | bytes 98336 | tf_op jit(solution)/shard_map/ppermute | solution.py:482
  108.4 1.6 %unpack.1 = (bf16[8,8,24,192]{3,2,1,0:T(8,128)(2,1)}, bf16[8,8,24,192]{3,2,1,0:T(8,128)(2,1)}) custom-call(bf16[2,2,192,128]{3,2,1,0:T(8,128)(2,1)S(1)} %collective-permute-done.6.refs_0_, bf16[2,2,192,128]{3,2,1,0:T(8,128)(2,1)S(1)} %collective-permute-done.7.refs_1_, bf16[2,2,192,128]{3,2,1,0:T(8,128)(2,1)S(1)} %collective-permute-done.8.refs_2_, ...), custom_call_target="tpu_custom_call" | custom-call | tf_op jit(solution)/shard_map/unpack/pallas_call | solution.py:173
  110.0 3.7 %all-to-all-done.2 = bf16[32,40,128]{2,1,0:T(8,128)(2,1)S(1)} async-done(((bf16[32,40,128]{2,1,0:T(8,128)(2,1)}), bf16[32,40,128]{2,1,0:T(8,128)(2,1)S(1)}, u32[]{:S(2)}, u32[]{:S(2)}) %all-to-all-start.2) | async-done | bytes 327712 | tf_op jit(solution)/shard_map/all_to_all | solution.py:493
  113.7 0.7 copy-done.6
  114.4 1.9 %unpack_grads.1 = (f32[192,576]{1,0:T(8,128)}, f32[192,192]{1,0:T(8,128)}, f32[1,192]{1,0:T(1,128)}, f32[1,192]{1,0:T(1,128)}) custom-call(bf16[1280,128]{1,0:T(8,128)(2,1)} %bitcast.8), custom_call_target="tpu_custom_call" | custom-call | tf_op jit(solution)/shard_map/unpack_grads/pallas_call | solution.py:525
  (10 shorter events, 0.0 us)
Async XLA Ops:
  2.9 18.3 %copy-start = (bf16[192,576]{1,0:T(8,128)(2,1)S(1)}, bf16[192,576]{1,0:T(8,128)(2,1)}, u32[]{:S(2)}) copy-start(bf16[192,576]{1,0:T(8,128)(2,1)} %wqkv_ref.3) | copy-start | bytes 663556
  2.9 18.3 %copy-start.1 = (bf16[192,192]{1,0:T(8,128)(2,1)S(1)}, bf16[192,192]{1,0:T(8,128)(2,1)}, u32[]{:S(2)}) copy-start(bf16[192,192]{1,0:T(8,128)(2,1)} %proj_ref.3) | copy-start | bytes 221188
  2.9 19.2 %collective-permute-start.3 = (bf16[2,192,128]{2,1,0:T(8,128)(2,1)}, bf16[2,192,128]{2,1,0:T(8,128)(2,1)S(1)}, u32[]{:S(2)}, u32[]{:S(2)}) collective-permute-start(bf16[2,192,128]{2,1,0:T(8,128)(2,1)} %get-tuple-element.80), channel_id=1, source_target_pairs={{0,255},{1,240},{2,241},{3,242},{4,243},{5,244},{6,245},{7,246},{8... | collective-permute-start | bytes 294920 | tf_op jit(solution)/shard_map/ppermute | solution.py:482
  10.9 11.3 %collective-permute-start.4 = (bf16[2,192,128]{2,1,0:T(8,128)(2,1)}, bf16[2,192,128]{2,1,0:T(8,128)(2,1)S(1)}, u32[]{:S(2)}, u32[]{:S(2)}) collective-permute-start(bf16[2,192,128]{2,1,0:T(8,128)(2,1)} %get-tuple-element.81), channel_id=1, source_target_pairs={{0,240},{1,241},{2,242},{3,243},{4,244},{5,245},{6,246},{7,247},{8... | collective-permute-start | bytes 294920 | tf_op jit(solution)/shard_map/ppermute | solution.py:482
  11.1 11.1 %collective-permute-start.5 = (bf16[2,192,128]{2,1,0:T(8,128)(2,1)}, bf16[2,192,128]{2,1,0:T(8,128)(2,1)S(1)}, u32[]{:S(2)}, u32[]{:S(2)}) collective-permute-start(bf16[2,192,128]{2,1,0:T(8,128)(2,1)} %get-tuple-element.82), channel_id=1, source_target_pairs={{0,15},{1,0},{2,1},{3,2},{4,3},{5,4},{6,5},{7,6},{8,7},{9,8},{10,9... | collective-permute-start | bytes 294920 | tf_op jit(solution)/shard_map/ppermute | solution.py:482
  14.6 6.5 %copy-start.3 = (f32[192]{0:T(256)S(1)}, f32[192]{0:T(256)}, u32[]{:S(2)}) copy-start(f32[192]{0:T(256)} %param.9) | copy-start | bytes 2308
  17.2 16.2 %collective-permute-start = (bf16[2,2,192,128]{3,2,1,0:T(8,128)(2,1)}, bf16[2,2,192,128]{3,2,1,0:T(8,128)(2,1)S(1)}, u32[]{:S(2)}, u32[]{:S(2)}) collective-permute-start(bf16[2,2,192,128]{3,2,1,0:T(8,128)(2,1)} %get-tuple-element.66), channel_id=1, source_target_pairs={{0,255},{1,240},{2,241},{3,242},{4,243},{5,244},{6,245},{7,246},{8... | collective-permute-start | bytes 589832 | tf_op jit(solution)/shard_map/ppermute | solution.py:482
  20.0 13.4 %collective-permute-start.1 = (bf16[2,2,192,128]{3,2,1,0:T(8,128)(2,1)}, bf16[2,2,192,128]{3,2,1,0:T(8,128)(2,1)S(1)}, u32[]{:S(2)}, u32[]{:S(2)}) collective-permute-start(bf16[2,2,192,128]{3,2,1,0:T(8,128)(2,1)} %get-tuple-element.67), channel_id=1, source_target_pairs={{0,240},{1,241},{2,242},{3,243},{4,244},{5,245},{6,246},{7,247},{8... | collective-permute-start | bytes 589832 | tf_op jit(solution)/shard_map/ppermute | solution.py:482
  21.2 0.7 copy-start.2
  21.2 1.0 copy-start.7
  21.8 0.9 copy-start.5
  22.1 11.3 %collective-permute-start.2 = (bf16[2,2,192,128]{3,2,1,0:T(8,128)(2,1)S(1)}, bf16[2,2,192,128]{3,2,1,0:T(8,128)(2,1)S(1)}, u32[]{:S(2)}, u32[]{:S(2)}) collective-permute-start(bf16[2,2,192,128]{3,2,1,0:T(8,128)(2,1)S(1)} %copy-done.7), channel_id=1, source_target_pairs={{0,15},{1,0},{2,1},{3,2},{4,3},{5,4},{6,5},{7,6},{8,7},{9,8},{10,9... | collective-permute-start | bytes 589832 | tf_op jit(solution)/shard_map/ppermute | solution.py:482
  22.8 10.7 %copy-start.4 = (bf16[2,2,192,128]{3,2,1,0:T(8,128)(2,1)S(1)}, bf16[2,2,192,128]{3,2,1,0:T(8,128)(2,1)}, u32[]{:S(2)}) copy-start(bf16[2,2,192,128]{3,2,1,0:T(8,128)(2,1)} %get-tuple-element.69.q11_ref) | copy-start | bytes 589828
  39.5 24.1 %collective-permute-start.6 = (bf16[2,2,192,128]{3,2,1,0:T(8,128)(2,1)S(1)}, bf16[2,2,192,128]{3,2,1,0:T(8,128)(2,1)S(1)}, u32[]{:S(2)}, u32[]{:S(2)}) collective-permute-start(bf16[2,2,192,128]{3,2,1,0:T(8,128)(2,1)S(1)} %get-tuple-element.91), channel_id=1, source_target_pairs={{0,17},{1,18},{2,19},{3,20},{4,21},{5,22},{6,23},{7,24},{8,25},{9,... | collective-permute-start | bytes 589832 | tf_op jit(solution)/shard_map/ppermute | solution.py:482
  45.5 18.1 %collective-permute-start.7 = (bf16[2,2,192,128]{3,2,1,0:T(8,128)(2,1)S(1)}, bf16[2,2,192,128]{3,2,1,0:T(8,128)(2,1)S(1)}, u32[]{:S(2)}, u32[]{:S(2)}) collective-permute-start(bf16[2,2,192,128]{3,2,1,0:T(8,128)(2,1)S(1)} %get-tuple-element.92), channel_id=1, source_target_pairs={{0,16},{1,17},{2,18},{3,19},{4,20},{5,21},{6,22},{7,23},{8,24},{9,... | collective-permute-start | bytes 589832 | tf_op jit(solution)/shard_map/ppermute | solution.py:482
  47.1 16.5 %collective-permute-start.8 = (bf16[2,2,192,128]{3,2,1,0:T(8,128)(2,1)S(1)}, bf16[2,2,192,128]{3,2,1,0:T(8,128)(2,1)S(1)}, u32[]{:S(2)}, u32[]{:S(2)}) collective-permute-start(bf16[2,2,192,128]{3,2,1,0:T(8,128)(2,1)S(1)} %get-tuple-element.93), channel_id=1, source_target_pairs={{0,1},{1,2},{2,3},{3,4},{4,5},{5,6},{6,7},{7,8},{8,9},{9,10},{10,1... | collective-permute-start | bytes 589832 | tf_op jit(solution)/shard_map/ppermute | solution.py:482
  63.6 21.8 %all-to-all-start = ((bf16[32,40,128]{2,1,0:T(8,128)(2,1)}), bf16[32,40,128]{2,1,0:T(8,128)(2,1)S(1)}, u32[]{:S(2)}, u32[]{:S(2)}) async-start(bf16[32,40,128]{2,1,0:T(8,128)(2,1)} %bitcast.2), calls=%async_computation | async-start | bytes 655360 | tf_op jit(solution)/shard_map/all_to_all | solution.py:493
  74.9 6.8 %collective-permute-start.9 = (bf16[2,192,128]{2,1,0:T(8,128)(2,1)S(1)}, bf16[2,192,128]{2,1,0:T(8,128)(2,1)S(1)}, u32[]{:S(2)}, u32[]{:S(2)}) collective-permute-start(bf16[2,192,128]{2,1,0:T(8,128)(2,1)S(1)} %get-tuple-element.100), channel_id=1, source_target_pairs={{0,17},{1,18},{2,19},{3,20},{4,21},{5,22},{6,23},{7,24},{8,25},{9,... | collective-permute-start | bytes 294920 | tf_op jit(solution)/shard_map/ppermute | solution.py:482
  86.1 12.1 %all-to-all-start.1 = ((bf16[8,40,128]{2,1,0:T(8,128)(2,1)}), bf16[8,40,128]{2,1,0:T(8,128)(2,1)S(1)}, u32[]{:S(2)}, u32[]{:S(2)}) async-start(bf16[8,40,128]{2,1,0:T(8,128)(2,1)} %broadcast_in_dim.20), calls=%async_computation.1 | async-start | bytes 163840 | tf_op jit(solution)/shard_map/all_to_all | solution.py:493
  89.5 8.7 %collective-permute-start.10 = (bf16[2,192,128]{2,1,0:T(8,128)(2,1)S(1)}, bf16[2,192,128]{2,1,0:T(8,128)(2,1)S(1)}, u32[]{:S(2)}, u32[]{:S(2)}) collective-permute-start(bf16[2,192,128]{2,1,0:T(8,128)(2,1)S(1)} %get-tuple-element.103), channel_id=1, source_target_pairs={{0,16},{1,17},{2,18},{3,19},{4,20},{5,21},{6,22},{7,23},{8,24},{9,... | collective-permute-start | bytes 294920 | tf_op jit(solution)/shard_map/ppermute | solution.py:482
  99.0 14.7 %all-to-all-start.2 = ((bf16[32,40,128]{2,1,0:T(8,128)(2,1)}), bf16[32,40,128]{2,1,0:T(8,128)(2,1)S(1)}, u32[]{:S(2)}, u32[]{:S(2)}) async-start(bf16[32,40,128]{2,1,0:T(8,128)(2,1)} %broadcast_in_dim.21), calls=%async_computation.2 | async-start | bytes 655360 | tf_op jit(solution)/shard_map/all_to_all | solution.py:493
  103.9 4.5 %collective-permute-start.11 = (bf16[2,192,128]{2,1,0:T(8,128)(2,1)S(1)}, bf16[2,192,128]{2,1,0:T(8,128)(2,1)S(1)}, u32[]{:S(2)}, u32[]{:S(2)}) collective-permute-start(bf16[2,192,128]{2,1,0:T(8,128)(2,1)S(1)} %get-tuple-element.105), channel_id=1, source_target_pairs={{0,1},{1,2},{2,3},{3,4},{4,5},{5,6},{6,7},{7,8},{8,9},{9,10},{10,1... | collective-permute-start | bytes 294920 | tf_op jit(solution)/shard_map/ppermute | solution.py:482
  113.7 0.7 copy-start.6

commit v2 on v1

--- a/solution.py
+++ b/solution.py
@@ -159,25 +159,31 @@
     )(gain[None], bias[None], wqkv, proj)
 
 
-def unpack_kernel(*refs):
-    paired, middle, outs = refs[:4], refs[4:8], refs[8:]
+def unpack_kernel(low_y_ref, paired_low, paired_high, middle_low, middle_high, *outs):
     for which, out in enumerate(outs):
-        for xh in range(2):
+        for xh, (paired, middle) in enumerate(
+            ((paired_low, middle_low), (paired_high, middle_high))
+        ):
             for yh in range(2):
-                i = xh * 2 + yh
-                quad = quadrant_of(paired[i][0, which], middle[i][which], paired[i][1, which])
+                if yh:
+                    first, last = paired[1, 0, which], paired[1, 1, which]
+                    second = middle[1, which]
+                else:
+                    first, last = low_y_ref[2 * xh, which], low_y_ref[2 * xh + 1, which]
+                    second = low_y_ref[4 + xh, which]
+                quad = quadrant_of(first, second, last)
                 out[xh * 4 : xh * 4 + 4, yh * 4 : yh * 4 + 4] = quad
 
 
-def unpacked(paired, middle, shape):
+def unpacked(low_y, paired, middle, shape):
     return pl.pallas_call(
         unpack_kernel,
         out_shape=(jax.ShapeDtypeStruct(shape, BF16),) * 2,
-        in_specs=[VMEM] * 8,
+        in_specs=[VMEM] * 5,
         out_specs=(VMEM,) * 2,
         compiler_params=pltpu.CompilerParams(vmem_limit_bytes=40 * 2**20),
         name="unpack",
-    )(*paired, *middle)
+    )(low_y, *paired, *middle)
 
 
 def attend_kernel(
@@ -187,9 +193,9 @@
     *refs,
 ):
     halves = turn == 1
-    given = (0, 5, 1)[turn]
+    given = (0, 3, 1)[turn]
     earlier_refs, refs = refs[:given], refs[given:]
-    y_refs, grads_ref, scratch = refs[:4], refs[4], refs[5:]
+    y_refs, grads_ref, scratch = refs[:2], refs[2], refs[3:]
     (qkv_s, gm_s, mix_s, gqkv_s, k_s, q_s, v_s, g_s, e_s, p_s, pb_s, dp_s, ds_s, dst_s, r_s, d_s) = scratch
     quads = (q00_ref, q01_ref, q10_ref, q11_ref)
     if turn:
@@ -394,18 +400,16 @@
     )
     d_tokens = gf + gx
     for which, y in enumerate((block_out, d_tokens)):
-        for i, ref in enumerate(y_refs):
+        for i in range(4):
+            ref, yh = y_refs[i // 2], i % 2
             if halves:
                 lo = y[:, i * half : (i + 1) * half]
                 hi = y[:, cells // 2 + i * half : cells // 2 + (i + 1) * half]
                 part = jnp.concatenate([lo, hi], axis=1)
+                ref[yh, 0, which] = earlier_refs[i // 2][yh, which]
+                ref[yh, 1, which] = part.astype(BF16)
             else:
-                part = y[:, i * LANES : (i + 1) * LANES]
-            if turn == 1:
-                ref[0, which] = earlier_refs[i][which]
-                ref[1, which] = part.astype(BF16)
-            else:
-                ref[which] = part.astype(BF16)
+                ref[yh, which] = y[:, i * LANES : (i + 1) * LANES].astype(BF16)
 
     dw = lax.dot_general(normed, gqkv, NT, preferred_element_type=F32)
     dproj = lax.dot_general(mixed, g, NT, preferred_element_type=F32)
@@ -442,10 +446,10 @@
     piece = (2, channels, LANES)
     return pl.pallas_call(
         functools.partial(attend_kernel, turn),
-        out_shape=(S((2, *piece) if turn == 1 else piece, BF16),) * 4
+        out_shape=(S((2, 2, *piece) if turn == 1 else (2, *piece), BF16),) * 2
         + (S((GRAD_ROWS, LANES), BF16 if turn == 2 else F32),),
         in_specs=[VMEM] * (12 + len(earlier)),
-        out_specs=(VMEM,) * 5,
+        out_specs=(VMEM,) * 3,
         scratch_shapes=[
             pltpu.VMEM((3 * channels, cells), BF16),
             pltpu.VMEM((channels, cells), BF16),
@@ -482,27 +486,27 @@
     return lax.ppermute(block, ("gx", "gy"), route)
 
 
-def summed(rows, beside):
+def summed(rows, paired, middle):
     nx, ny = lax.axis_size("gx"), lax.axis_size("gy")
     near = 2 * ny
     planes = [[near * i + j for j in range(near)] for i in range(nx // 2)]
     across = [list(ids) for ids in zip(*planes)]
-    beside = list(beside)
-
-    def exchanged(pieces, groups, turn):
-        got = lax.all_to_all(pieces, ("gx", "gy"), 0, 0, axis_index_groups=groups)
-        if turn < 2:
-            got, beside[turn] = lax.optimization_barrier((got, beside[turn]))
-        return got
+
+    def exchanged(pieces, groups):
+        return lax.all_to_all(pieces, ("gx", "gy"), 0, 0, axis_index_groups=groups)
 
     def copies(piece, count):
         return jnp.broadcast_to(piece[None], (count, *piece.shape))
 
-    got = exchanged(rows.reshape(near, -1, LANES), planes, 0)
+    got = exchanged(rows.reshape(near, -1, LANES), planes)
+    middle = (moved(middle[0], 1, 0), middle[1])
+    got, middle = lax.optimization_barrier((got, middle))
     mine = jnp.sum(got.astype(F32), axis=0).astype(BF16)
-    got = exchanged(copies(mine, nx // 2), across, 1)
+    got = exchanged(copies(mine, nx // 2), across)
+    low_y = moved(jnp.concatenate([paired[0][0], paired[1][0], middle[0][:1], middle[1][:1]]), 0, 1)
+    got, low_y = lax.optimization_barrier((got, low_y))
     total = jnp.sum(got.astype(F32), axis=0).astype(BF16)
-    return exchanged(copies(total, near), planes, 2).reshape(rows.shape), beside
+    return exchanged(copies(total, near), planes).reshape(rows.shape), low_y, middle
 
 
 def grads_kernel(factor, rows_ref, dw_ref, dproj_ref, gain_ref, bias_ref):
@@ -552,18 +556,14 @@
     def gathered(quads):
         return [moved(quad, -x, -y) for quad, (x, y) in zip(quads, steps)] + [quads[3]]
 
-    def returned(quads):
-        return [moved(quad, x, y) for quad, (x, y) in zip(quads, steps)] + [quads[3]]
-
     first, rest = gathered(first), gathered(rest)
-    *y, sums = attend(0, first, features, weights, ())
-    *y, sums = attend(1, rest, features, weights, (*y, sums))
-    paired = returned(y)
-    *y, sums = attend(2, rest, features, weights, (sums,))
-    middle = returned(y)
+    low, high, sums = attend(0, first, features, weights, ())
+    low, high, sums = attend(1, rest, features, weights, (low, high, sums))
+    paired = (moved(low, 1, 0), high)
+    *middle, sums = attend(2, rest, features, weights, (sums,))
     sums, paired = lax.optimization_barrier((sums, paired))
-    total, middle[:3] = summed(sums, middle[:3])
-    block_out, d_tokens = unpacked(paired, middle, tokens.shape)
+    total, low_y, middle = summed(sums, paired, middle)
+    block_out, d_tokens = unpacked(low_y, paired, middle, tokens.shape)
     factor = 1.0 / math.sqrt(tile_x * nx * tile_y * ny * depth)
     dw, dproj, dgain, dbias = grads_of(total, channels, factor)
     return block_out, d_tokens, dw, dproj, dgain[0], dbias[0]

time: 118 us -> 115 us (0.975); the launches traced: 116 us -> 115 us
  starting transfers between devices: 49.1 us -> 30.5 us
  blocking collectives: 0 us -> 10.3 us
  Pallas kernels: 41.7 us -> 51.2 us
  waiting for transfers between devices: 21.3 us -> 19 us
    ppermute x12 -> x9, starting transfers between devices: 29.5 us -> 17.7 us  [moved(): return lax.ppermute(block, ('gx', 'gy'), route)]
    all_to_all x0 -> x1, blocking collectives: none -> 10.3 us  [exchanged(): return lax.all_to_all(pieces, ('gx', 'gy'), 0, 0, axis_index_groups=groups)]
    pallas_call x3, Pallas kernels: 33.1 us -> 42.7 us  [attend(): pl.pallas_call(functools.partial(attend_kernel, turn), out_shape=(S((2, 2...]
    ppermute x12 -> x9, waiting for transfers between devices: 13.9 us -> 7.02 us  [moved(): return lax.ppermute(block, ('gx', 'gy'), route)]
    all_to_all x3 -> x2, starting transfers between devices: 19.6 us -> 12.8 us  [exchanged(): return lax.all_to_all(pieces, ('gx', 'gy'), 0, 0, axis_index_groups=groups)]
    all_to_all x3 -> x2, waiting for transfers between devices: 7.39 us -> 12 us  [exchanged(): return lax.all_to_all(pieces, ('gx', 'gy'), 0, 0, axis_index_groups=groups)]
  transfers between devices with their start and end apart: 15 -> 11, of which waited for: 5 -> 3; matrix products, arithmetic and copies ran while one was open for 0% -> 0% of each run, Pallas kernels for 27% -> 32%
where the time goes in v2:
time: 115 us
  Pallas kernels  51.2 us (45%)
  starting transfers between devices  30.5 us (27%)
  waiting for transfers between devices  19 us (17%)
  blocking collectives  10.3 us (9%)
  local copies, waits for them, and re-layouts  2.76 us (2%)
    pallas_call x3, Pallas kernels, attend(): pl.pallas_call(functools.partial(attend_kernel, turn), out_shape=(S((2, 2...  42.7 us
    ppermute x9, starting transfers between devices, moved(): return lax.ppermute(block, ('gx', 'gy'), route)  17.7 us
    all_to_all x2, starting transfers between devices, exchanged(): return lax.all_to_all(pieces, ('gx', 'gy'), 0, 0, axis_index_groups=groups)  12.8 us
    all_to_all x2, waiting for transfers between devices, exchanged(): return lax.all_to_all(pieces, ('gx', 'gy'), 0, 0, axis_index_groups=groups)  12 us
    all_to_all x1, blocking collectives, exchanged(): return lax.all_to_all(pieces, ('gx', 'gy'), 0, 0, axis_index_groups=groups)  10.3 us
    ppermute x9, waiting for transfers between devices, moved(): return lax.ppermute(block, ('gx', 'gy'), route)  7.02 us
    pallas_call x2, Pallas kernels, packed(): pl.pallas_call(pack_first_kernel if first else pack_rest_kernel, out_shap...  4.78 us
  transfers between devices with their start and end apart: 11, of which 3 were waited for; matrix products, arithmetic and copies ran while one was open for 0% of the time, Pallas kernels for 32%

profile of v2, /device:TPU:1, one launch (start us, length us, event | category | flops | bytes accessed | tf_op | source)
XLA Modules:
  0.0 114.7 jit_solution(12790539672235803429)
XLA Ops:
  0.6 2.2 %pack_first.1 = (bf16[2,192,128]{2,1,0:T(8,128)(2,1)}, bf16[2,192,128]{2,1,0:T(8,128)(2,1)}, bf16[2,192,128]{2,1,0:T(8,128)(2,1)}, bf16[2,192,128]{2,1,0:T(8,128)(2,1)}) custom-call(bf16[8,8,24,192]{3,2,1,0:T(8,128)(2,1)} %tokens_ref.2, bf16[8,8,24,192]{3,2,1,0:T(8,128)(2,1)} %cot_ref.2), custom_call_target="tpu_custom_call" | custom-call | tf_op jit(solution)/shard_map/pack_first/pallas_call | solution.py:104
  2.8 0.0 copy-start
  2.9 0.0 copy-start.1
  2.9 8.0 %collective-permute-start.3 = (bf16[2,192,128]{2,1,0:T(8,128)(2,1)}, bf16[2,192,128]{2,1,0:T(8,128)(2,1)S(1)}, u32[]{:S(2)}, u32[]{:S(2)}) collective-permute-start(bf16[2,192,128]{2,1,0:T(8,128)(2,1)} %get-tuple-element.73), channel_id=1, source_target_pairs={{0,255},{1,240},{2,241},{3,242},{4,243},{5,244},{6,245},{7,246},{8... | collective-permute-start | bytes 294920 | tf_op jit(solution)/shard_map/ppermute | solution.py:486
  10.8 0.3 collective-permute-start.4
  11.1 3.5 %collective-permute-start.5 = (bf16[2,192,128]{2,1,0:T(8,128)(2,1)}, bf16[2,192,128]{2,1,0:T(8,128)(2,1)S(1)}, u32[]{:S(2)}, u32[]{:S(2)}) collective-permute-start(bf16[2,192,128]{2,1,0:T(8,128)(2,1)} %get-tuple-element.75), channel_id=1, source_target_pairs={{0,15},{1,0},{2,1},{3,2},{4,3},{5,4},{6,5},{7,6},{8,7},{9,8},{10,9... | collective-permute-start | bytes 294920 | tf_op jit(solution)/shard_map/ppermute | solution.py:486
  14.6 0.0 copy-start.3
  14.6 2.6 %pack_rest.1 = (bf16[2,2,192,128]{3,2,1,0:T(8,128)(2,1)}, bf16[2,2,192,128]{3,2,1,0:T(8,128)(2,1)}, bf16[2,2,192,128]{3,2,1,0:T(8,128)(2,1)}, bf16[2,2,192,128]{3,2,1,0:T(8,128)(2,1)}) custom-call(bf16[8,8,24,192]{3,2,1,0:T(8,128)(2,1)} %tokens_ref.2, bf16[8,8,24,192]{3,2,1,0:T(8,128)(2,1)} %cot_ref.2), custom_call_target="tpu_custom_call" | custom-call | tf_op jit(solution)/shard_map/pack_rest/pallas_call | solution.py:104
  17.2 2.8 %collective-permute-start = (bf16[2,2,192,128]{3,2,1,0:T(8,128)(2,1)}, bf16[2,2,192,128]{3,2,1,0:T(8,128)(2,1)S(1)}, u32[]{:S(2)}, u32[]{:S(2)}) collective-permute-start(bf16[2,2,192,128]{3,2,1,0:T(8,128)(2,1)} %get-tuple-element.59), channel_id=1, source_target_pairs={{0,255},{1,240},{2,241},{3,242},{4,243},{5,244},{6,245},{7,246},{8... | collective-permute-start | bytes 589832 | tf_op jit(solution)/shard_map/ppermute | solution.py:486
  20.0 1.2 %collective-permute-start.1 = (bf16[2,2,192,128]{3,2,1,0:T(8,128)(2,1)}, bf16[2,2,192,128]{3,2,1,0:T(8,128)(2,1)S(1)}, u32[]{:S(2)}, u32[]{:S(2)}) collective-permute-start(bf16[2,2,192,128]{3,2,1,0:T(8,128)(2,1)} %get-tuple-element.60), channel_id=1, source_target_pairs={{0,240},{1,241},{2,242},{3,243},{4,244},{5,245},{6,246},{7,247},{8... | collective-permute-start | bytes 589832 | tf_op jit(solution)/shard_map/ppermute | solution.py:486
  21.1 0.0 copy-start.2
  21.1 0.0 copy-start.7
  21.1 0.0 copy-done
  21.1 0.0 copy-done.1
  21.2 0.0 copy-done.3
  21.2 0.7 copy-done.2
  21.8 0.0 copy-start.5
  21.8 0.3 prepare.1
  22.1 0.0 collective-permute-done.3.q00_ref
  22.1 0.0 copy-done.7
  22.1 0.1 collective-permute-start.2
  22.2 0.0 collective-permute-done.4.q01_ref
  22.2 0.0 collective-permute-done.5.q10_ref
  22.2 0.5 copy-done.5
  22.7 15.7 %attend.3 = (bf16[2,2,192,128]{3,2,1,0:T(8,128)(2,1)S(1)}, bf16[2,2,192,128]{3,2,1,0:T(8,128)(2,1)S(1)}, f32[1280,128]{1,0:T(8,128)S(1)}) custom-call(bf16[2,192,128]{2,1,0:T(8,128)(2,1)S(1)} %collective-permute-done.3.q00_ref, bf16[2,192,128]{2,1,0:T(8,128)(2,1)S(1)} %collective-permute-done.4.q01_ref, ...), custom_call_target="tpu_custom_call" | custom-call | flops 9663676416 | bytes 4194304 | tf_op jit(solution)/shard_map/attend/pallas_call | solution.py:447
  38.4 0.0 collective-permute-done.q00_ref
  38.4 0.0 collective-permute-done.1.q01_ref
  38.4 0.0 collective-permute-done.2.q10_ref
  38.4 0.0 copy-done.4
  38.5 10.7 %attend.4 = (bf16[2,2,2,192,128]{4,3,2,1,0:T(8,128)(2,1)S(1)}, bf16[2,2,2,192,128]{4,3,2,1,0:T(8,128)(2,1)S(1)}, f32[1280,128]{1,0:T(8,128)S(1)}) custom-call(bf16[2,2,192,128]{3,2,1,0:T(8,128)(2,1)S(1)} %collective-permute-done.q00_ref, bf16[2,2,192,128]{3,2,1,0:T(8,128)(2,1)S(1)} %collective-permute-done.1.q01_ref, ...), custom_call_target="tpu_custom_call" | custom-call | flops 9663676416 | bytes 4194304 | tf_op jit(solution)/shard_map/attend/pallas_call | solution.py:447
  49.2 0.4 collective-permute-start.6
  49.6 16.3 %attend.5 = (bf16[2,2,192,128]{3,2,1,0:T(8,128)(2,1)S(1)}, bf16[2,2,192,128]{3,2,1,0:T(8,128)(2,1)S(1)}, bf16[1280,128]{1,0:T(8,128)(2,1)}) custom-call(bf16[2,2,192,128]{3,2,1,0:T(8,128)(2,1)S(1)} %collective-permute-done.q00_ref, bf16[2,2,192,128]{3,2,1,0:T(8,128)(2,1)S(1)} %collective-permute-done.1.q01_ref, ...), custom_call_target="tpu_custom_call" | custom-call | flops 9663676416 | bytes 4194304 | tf_op jit(solution)/shard_map/attend/pallas_call | solution.py:447
  65.8 0.0 collective-permute-done.6.paired_low
  65.8 4.6 %all-to-all-start = ((bf16[32,40,128]{2,1,0:T(8,128)(2,1)}), bf16[32,40,128]{2,1,0:T(8,128)(2,1)S(1)}, u32[]{:S(2)}, u32[]{:S(2)}) async-start(bf16[32,40,128]{2,1,0:T(8,128)(2,1)} %bitcast.2), calls=%async_computation | async-start | bytes 655360 | tf_op jit(solution)/shard_map/all_to_all | solution.py:496
  70.5 1.5 %collective-permute-start.7 = (bf16[2,2,192,128]{3,2,1,0:T(8,128)(2,1)S(1)}, bf16[2,2,192,128]{3,2,1,0:T(8,128)(2,1)S(1)}, u32[]{:S(2)}, u32[]{:S(2)}) collective-permute-start(bf16[2,2,192,128]{3,2,1,0:T(8,128)(2,1)S(1)} %get-tuple-element.85), channel_id=1, source_target_pairs={{0,16},{1,17},{2,18},{3,19},{4,20},{5,21},{6,22},{7,23},{8,24},{9,... | collective-permute-start | bytes 589832 | tf_op jit(solution)/shard_map/ppermute | solution.py:486
  72.0 7.0 %collective-permute-done.7.middle_low = bf16[2,2,192,128]{3,2,1,0:T(8,128)(2,1)S(1)} collective-permute-done((bf16[2,2,192,128]{3,2,1,0:T(8,128)(2,1)S(1)}, bf16[2,2,192,128]{3,2,1,0:T(8,128)(2,1)S(1)}, u32[]{:S(2)}, u32[]{:S(2)}) %collective-permute-start.7) | collective-permute-done | bytes 196640 | tf_op jit(solution)/shard_map/ppermute | solution.py:486
  79.0 3.9 %all-to-all-done = bf16[32,40,128]{2,1,0:T(8,128)(2,1)S(1)} async-done(((bf16[32,40,128]{2,1,0:T(8,128)(2,1)}), bf16[32,40,128]{2,1,0:T(8,128)(2,1)S(1)}, u32[]{:S(2)}, u32[]{:S(2)}) %all-to-all-start) | async-done | bytes 327712 | tf_op jit(solution)/shard_map/all_to_all | solution.py:496
  82.9 0.1 pad_maximum_fusion
  83.0 0.1 collective-permute-start.8
  83.0 0.1 reduce_sum.24
  83.1 10.3 %all_to_all.15 = bf16[8,40,128]{2,1,0:T(8,128)(2,1)S(1)} all-to-all(bf16[8,40,128]{2,1,0:T(8,128)(2,1)S(1)} %broadcast_in_dim.20), channel_id=1, replica_groups={{0,32,64,96,128,160,192,224},{1,33,65,97,129,161,193,225},{2,34,66,98,1..., dimensions={0} | all-to-all | bytes 163840 | tf_op jit(solution)/shard_map/all_to_all | solution.py:496
  93.4 0.0 collective-permute-done.8.low_y_ref
  93.5 0.8 broadcast_in_dim.21
  94.2 8.1 %all-to-all-start.2 = ((bf16[32,40,128]{2,1,0:T(8,128)(2,1)}), bf16[32,40,128]{2,1,0:T(8,128)(2,1)S(1)}, u32[]{:S(2)}, u32[]{:S(2)}) async-start(bf16[32,40,128]{2,1,0:T(8,128)(2,1)} %broadcast_in_dim.21), calls=%async_computation.2 | async-start | bytes 655360 | tf_op jit(solution)/shard_map/all_to_all | solution.py:496
  102.4 1.6 %unpack.1 = (bf16[8,8,24,192]{3,2,1,0:T(8,128)(2,1)}, bf16[8,8,24,192]{3,2,1,0:T(8,128)(2,1)}) custom-call(bf16[6,2,192,128]{3,2,1,0:T(8,128)(2,1)S(1)} %collective-permute-done.8.low_y_ref, bf16[2,2,2,192,128]{4,3,2,1,0:T(8,128)(2,1)S(1)} %collective-permute-done.6.paired_low, bf16[2,2,2,192,128]{4,3,2,1,0:T(8,128)(2,1)S(1)} %get-tuple-element.89.paired_high, ...), custom_call_target="tpu_custom_call" | custom-call | tf_op jit(solution)/shard_map/unpack/pallas_call | solution.py:179
  104.0 8.1 %all-to-all-done.2 = bf16[32,40,128]{2,1,0:T(8,128)(2,1)S(1)} async-done(((bf16[32,40,128]{2,1,0:T(8,128)(2,1)}), bf16[32,40,128]{2,1,0:T(8,128)(2,1)S(1)}, u32[]{:S(2)}, u32[]{:S(2)}) %all-to-all-start.2) | async-done | bytes 327712 | tf_op jit(solution)/shard_map/all_to_all | solution.py:496
  112.1 0.7 copy-done.6
  112.8 1.9 %unpack_grads.1 = (f32[192,576]{1,0:T(8,128)}, f32[192,192]{1,0:T(8,128)}, f32[1,192]{1,0:T(1,128)}, f32[1,192]{1,0:T(1,128)}) custom-call(bf16[1280,128]{1,0:T(8,128)(2,1)} %bitcast.12), custom_call_target="tpu_custom_call" | custom-call | tf_op jit(solution)/shard_map/unpack_grads/pallas_call | solution.py:529
  (7 shorter events, 0.1 us)
Async XLA Ops:
  2.8 18.3 %copy-start = (bf16[192,576]{1,0:T(8,128)(2,1)S(1)}, bf16[192,576]{1,0:T(8,128)(2,1)}, u32[]{:S(2)}) copy-start(bf16[192,576]{1,0:T(8,128)(2,1)} %wqkv_ref.3) | copy-start | bytes 663556
  2.9 18.3 %copy-start.1 = (bf16[192,192]{1,0:T(8,128)(2,1)S(1)}, bf16[192,192]{1,0:T(8,128)(2,1)}, u32[]{:S(2)}) copy-start(bf16[192,192]{1,0:T(8,128)(2,1)} %proj_ref.3) | copy-start | bytes 221188
  2.9 19.2 %collective-permute-start.3 = (bf16[2,192,128]{2,1,0:T(8,128)(2,1)}, bf16[2,192,128]{2,1,0:T(8,128)(2,1)S(1)}, u32[]{:S(2)}, u32[]{:S(2)}) collective-permute-start(bf16[2,192,128]{2,1,0:T(8,128)(2,1)} %get-tuple-element.73), channel_id=1, source_target_pairs={{0,255},{1,240},{2,241},{3,242},{4,243},{5,244},{6,245},{7,246},{8... | collective-permute-start | bytes 294920 | tf_op jit(solution)/shard_map/ppermute | solution.py:486
  10.8 11.3 %collective-permute-start.4 = (bf16[2,192,128]{2,1,0:T(8,128)(2,1)}, bf16[2,192,128]{2,1,0:T(8,128)(2,1)S(1)}, u32[]{:S(2)}, u32[]{:S(2)}) collective-permute-start(bf16[2,192,128]{2,1,0:T(8,128)(2,1)} %get-tuple-element.74), channel_id=1, source_target_pairs={{0,240},{1,241},{2,242},{3,243},{4,244},{5,245},{6,246},{7,247},{8... | collective-permute-start | bytes 294920 | tf_op jit(solution)/shard_map/ppermute | solution.py:486
  11.1 11.1 %collective-permute-start.5 = (bf16[2,192,128]{2,1,0:T(8,128)(2,1)}, bf16[2,192,128]{2,1,0:T(8,128)(2,1)S(1)}, u32[]{:S(2)}, u32[]{:S(2)}) collective-permute-start(bf16[2,192,128]{2,1,0:T(8,128)(2,1)} %get-tuple-element.75), channel_id=1, source_target_pairs={{0,15},{1,0},{2,1},{3,2},{4,3},{5,4},{6,5},{7,6},{8,7},{9,8},{10,9... | collective-permute-start | bytes 294920 | tf_op jit(solution)/shard_map/ppermute | solution.py:486
  14.6 6.5 %copy-start.3 = (f32[192]{0:T(256)S(1)}, f32[192]{0:T(256)}, u32[]{:S(2)}) copy-start(f32[192]{0:T(256)} %param.9) | copy-start | bytes 2308
  17.2 21.2 %collective-permute-start = (bf16[2,2,192,128]{3,2,1,0:T(8,128)(2,1)}, bf16[2,2,192,128]{3,2,1,0:T(8,128)(2,1)S(1)}, u32[]{:S(2)}, u32[]{:S(2)}) collective-permute-start(bf16[2,2,192,128]{3,2,1,0:T(8,128)(2,1)} %get-tuple-element.59), channel_id=1, source_target_pairs={{0,255},{1,240},{2,241},{3,242},{4,243},{5,244},{6,245},{7,246},{8... | collective-permute-start | bytes 589832 | tf_op jit(solution)/shard_map/ppermute | solution.py:486
  20.0 18.4 %collective-permute-start.1 = (bf16[2,2,192,128]{3,2,1,0:T(8,128)(2,1)}, bf16[2,2,192,128]{3,2,1,0:T(8,128)(2,1)S(1)}, u32[]{:S(2)}, u32[]{:S(2)}) collective-permute-start(bf16[2,2,192,128]{3,2,1,0:T(8,128)(2,1)} %get-tuple-element.60), channel_id=1, source_target_pairs={{0,240},{1,241},{2,242},{3,243},{4,244},{5,245},{6,246},{7,247},{8... | collective-permute-start | bytes 589832 | tf_op jit(solution)/shard_map/ppermute | solution.py:486
  21.1 0.7 copy-start.2
  21.1 1.0 copy-start.7
  21.8 0.9 copy-start.5
  22.1 16.3 %collective-permute-start.2 = (bf16[2,2,192,128]{3,2,1,0:T(8,128)(2,1)S(1)}, bf16[2,2,192,128]{3,2,1,0:T(8,128)(2,1)S(1)}, u32[]{:S(2)}, u32[]{:S(2)}) collective-permute-start(bf16[2,2,192,128]{3,2,1,0:T(8,128)(2,1)S(1)} %copy-done.7), channel_id=1, source_target_pairs={{0,15},{1,0},{2,1},{3,2},{4,3},{5,4},{6,5},{7,6},{8,7},{9,8},{10,9... | collective-permute-start | bytes 589832 | tf_op jit(solution)/shard_map/ppermute | solution.py:486
  22.7 15.7 %copy-start.4 = (bf16[2,2,192,128]{3,2,1,0:T(8,128)(2,1)S(1)}, bf16[2,2,192,128]{3,2,1,0:T(8,128)(2,1)}, u32[]{:S(2)}) copy-start(bf16[2,2,192,128]{3,2,1,0:T(8,128)(2,1)} %get-tuple-element.62.q11_ref) | copy-start | bytes 589828
  49.2 16.6 %collective-permute-start.6 = (bf16[2,2,2,192,128]{4,3,2,1,0:T(8,128)(2,1)S(1)}, bf16[2,2,2,192,128]{4,3,2,1,0:T(8,128)(2,1)S(1)}, u32[]{:S(2)}, u32[]{:S(2)}) collective-permute-start(bf16[2,2,2,192,128]{4,3,2,1,0:T(8,128)(2,1)S(1)} %get-tuple-element.82), channel_id=1, source_target_pairs={{0,16},{1,17},{2,18},{3,19},{4,20},{5,21},{6,22},{7,23},{8,24},{9,... | collective-permute-start | bytes 1179656 | tf_op jit(solution)/shard_map/ppermute | solution.py:486
  65.8 17.0 %all-to-all-start = ((bf16[32,40,128]{2,1,0:T(8,128)(2,1)}), bf16[32,40,128]{2,1,0:T(8,128)(2,1)S(1)}, u32[]{:S(2)}, u32[]{:S(2)}) async-start(bf16[32,40,128]{2,1,0:T(8,128)(2,1)} %bitcast.2), calls=%async_computation | async-start | bytes 655360 | tf_op jit(solution)/shard_map/all_to_all | solution.py:496
  70.5 8.5 %collective-permute-start.7 = (bf16[2,2,192,128]{3,2,1,0:T(8,128)(2,1)S(1)}, bf16[2,2,192,128]{3,2,1,0:T(8,128)(2,1)S(1)}, u32[]{:S(2)}, u32[]{:S(2)}) collective-permute-start(bf16[2,2,192,128]{3,2,1,0:T(8,128)(2,1)S(1)} %get-tuple-element.85), channel_id=1, source_target_pairs={{0,16},{1,17},{2,18},{3,19},{4,20},{5,21},{6,22},{7,23},{8,24},{9,... | collective-permute-start | bytes 589832 | tf_op jit(solution)/shard_map/ppermute | solution.py:486
  83.0 10.5 %collective-permute-start.8 = (bf16[6,2,192,128]{3,2,1,0:T(8,128)(2,1)S(1)}, bf16[6,2,192,128]{3,2,1,0:T(8,128)(2,1)S(1)}, u32[]{:S(2)}, u32[]{:S(2)}) collective-permute-start(bf16[6,2,192,128]{3,2,1,0:T(8,128)(2,1)S(1)} %pad_maximum_fusion), channel_id=1, source_target_pairs={{0,1},{1,2},{2,3},{3,4},{4,5},{5,6},{6,7},{7,8},{8,9},{9,10},{10,1... | collective-permute-start | bytes 1769480 | tf_op jit(solution)/shard_map/ppermute | solution.py:486
  94.2 17.9 %all-to-all-start.2 = ((bf16[32,40,128]{2,1,0:T(8,128)(2,1)}), bf16[32,40,128]{2,1,0:T(8,128)(2,1)S(1)}, u32[]{:S(2)}, u32[]{:S(2)}) async-start(bf16[32,40,128]{2,1,0:T(8,128)(2,1)} %broadcast_in_dim.21), calls=%async_computation.2 | async-start | bytes 655360 | tf_op jit(solution)/shard_map/all_to_all | solution.py:496
  112.1 0.7 copy-start.6

commit v3 on v2

--- a/solution.py
+++ b/solution.py
@@ -60,59 +60,39 @@
     return whole.reshape(4, 4, 24, channels).astype(BF16)
 
 
-def read_block(sources, buffer, sems, depth):
+def pack_kernel(tokens_ref, cot_ref, *refs):
+    first_refs, rest_refs, (buffer, sems) = refs[:4], refs[4:8], refs[8:]
     copies = [
         pltpu.make_async_copy(
-            source.at[pl.ds(2 * x, 2), :, pl.ds(0, depth)],
-            buffer.at[which, pl.ds(2 * x, 2)],
-            sems.at[which, x],
+            source.at[pl.ds(2 * x, 2)], buffer.at[which, pl.ds(2 * x, 2)], sems.at[which, x]
         )
-        for which, source in enumerate(sources)
+        for which, source in enumerate((tokens_ref, cot_ref))
         for x in range(4)
     ]
     for copy in copies:
         copy.start()
-    return copies
-
-
-def pack_first_kernel(tokens_ref, cot_ref, *refs):
-    outs, (buffer, sems) = refs[:4], refs[4:]
-    copies = read_block((tokens_ref, cot_ref), buffer, sems, buffer.shape[3])
     for which in range(2):
         for copy in copies[4 * which : 4 * which + 4]:
             copy.wait()
         for i, quad in enumerate(quadrants(buffer[which].astype(F32))):
-            outs[i][which] = piece_of(quad[:, 4:12])
-
-
-def pack_rest_kernel(tokens_ref, cot_ref, *refs):
-    outs, (buffer, sems) = refs[:4], refs[4:]
-    copies = read_block((tokens_ref, cot_ref), buffer, sems, buffer.shape[3])
-    for which in range(2):
-        for copy in copies[4 * which : 4 * which + 4]:
-            copy.wait()
-        for i, quad in enumerate(quadrants(buffer[which].astype(F32))):
-            outs[i][0, which] = last_piece_of(quad)
-            outs[i][1, which] = piece_of(quad[:, 12:20])
-
-
-def packed(tokens, cotangent, first):
-    tile_x, tile_y, depth, channels = tokens.shape
-    piece = (2, channels, LANES)
-    shape = piece if first else (2, *piece)
-    held = 2 * WIN if first else depth
-    return pl.pallas_call(
-        pack_first_kernel if first else pack_rest_kernel,
-        out_shape=(jax.ShapeDtypeStruct(shape, BF16),) * 4,
+            first_refs[i][which] = piece_of(quad[:, 4:12])
+            rest_refs[i][0, which] = last_piece_of(quad)
+            rest_refs[i][1, which] = piece_of(quad[:, 12:20])
+
+
+def packed(tokens, cotangent):
+    channels = tokens.shape[-1]
+    S = jax.ShapeDtypeStruct
+    outs = pl.pallas_call(
+        pack_kernel,
+        out_shape=(S((2, channels, LANES), BF16),) * 4 + (S((2, 2, channels, LANES), BF16),) * 4,
         in_specs=[pl.BlockSpec(memory_space=pltpu.HBM)] * 2,
-        out_specs=(VMEM,) * 4,
-        scratch_shapes=[
-            pltpu.VMEM((2, tile_x, tile_y, held, channels), BF16),
-            pltpu.SemaphoreType.DMA((2, 4)),
-        ],
+        out_specs=(VMEM,) * 8,
+        scratch_shapes=[pltpu.VMEM((2, *tokens.shape), BF16), pltpu.SemaphoreType.DMA((2, 4))],
         compiler_params=pltpu.CompilerParams(vmem_limit_bytes=62 * 2**20),
-        name="pack_first" if first else "pack_rest",
+        name="pack",
     )(tokens, cotangent)
+    return outs[:4], outs[4:]
 
 
 def prepare_kernel(
@@ -354,12 +334,8 @@
         step(1, 1, three=False, four=False)
         step(2, 0, four=False)
 
-        def two_steps(j, carry):
-            step(3 + 2 * j, 1)
-            step(4 + 2 * j, 0)
-            return carry
-
-        lax.fori_loop(0, (HEADS - 4) // 2, two_steps, 0)
+        for i in range(3, HEADS - 1):
+            step(i, i % 2)
         step(HEADS - 1, 1, ahead=False)
         step(HEADS, 0, one=False, ahead=False)
         step(HEADS + 1, 1, one=False, two=False, ahead=False)
@@ -543,11 +519,8 @@
 def shards(tokens, cotangent, ln_gain, ln_bias, qkv_weight, proj_weight):
     tile_x, tile_y, depth, channels = tokens.shape
     nx, ny = lax.axis_size("gx"), lax.axis_size("gy")
-    first = packed(tokens, cotangent, True)
-    first, tokens, cotangent, ln_gain, ln_bias, qkv_weight, proj_weight = lax.optimization_barrier(
-        (first, tokens, cotangent, ln_gain, ln_bias, qkv_weight, proj_weight)
-    )
-    rest = packed(tokens, cotangent, False)
+    first, rest = packed(tokens, cotangent)
+    first, proj_weight = lax.optimization_barrier((first, proj_weight))
     gain, bias, wqkv_t, proj_t, *features = prepared(ln_gain, ln_bias, qkv_weight, proj_weight)
     weights = (gain, bias, wqkv_t, qkv_weight, proj_weight, proj_t)
 

time: 115 us -> 116 us (level)
  Pallas kernels: 51.2 us -> 43.7 us
  starting transfers between devices: 30.5 us -> 35.3 us
  blocking collectives: 10.3 us -> 14.2 us
    pallas_call x3, Pallas kernels: 42.7 us -> 37.1 us  [attend(): pl.pallas_call(functools.partial(attend_kernel, turn), out_shape=(S((2, 2...]
    all_to_all x2, starting transfers between devices: 12.8 us -> 16.9 us  [exchanged(): return lax.all_to_all(pieces, ('gx', 'gy'), 0, 0, axis_index_groups=groups)]
    all_to_all x1, blocking collectives: 10.3 us -> 14.2 us  [exchanged(): return lax.all_to_all(pieces, ('gx', 'gy'), 0, 0, axis_index_groups=groups)]
    pallas_call x2 -> x1, Pallas kernels: 4.78 us -> 2.88 us  [packed(): pl.pallas_call(pack_kernel, out_shape=(S((2, channels, LANES), BF16),) *...]
  transfers between devices with their start and end apart: 11 -> 11, of which waited for: 3 -> 3; matrix products, arithmetic and copies ran while one was open for 0% -> 0% of each run, Pallas kernels for 32% -> 24%
where the time goes in v3:
time: 116 us
  Pallas kernels  43.7 us (38%)
  starting transfers between devices  35.3 us (30%)
  waiting for transfers between devices  19 us (16%)
  blocking collectives  14.2 us (12%)
  local copies, waits for them, and re-layouts  2.74 us (2%)
    pallas_call x3, Pallas kernels, attend(): pl.pallas_call(functools.partial(attend_kernel, turn), out_shape=(S((2, 2...  37.1 us
    ppermute x9, starting transfers between devices, moved(): return lax.ppermute(block, ('gx', 'gy'), route)  18.3 us
    all_to_all x2, starting transfers between devices, exchanged(): return lax.all_to_all(pieces, ('gx', 'gy'), 0, 0, axis_index_groups=groups)  16.9 us
    all_to_all x1, blocking collectives, exchanged(): return lax.all_to_all(pieces, ('gx', 'gy'), 0, 0, axis_index_groups=groups)  14.2 us
    all_to_all x2, waiting for transfers between devices, exchanged(): return lax.all_to_all(pieces, ('gx', 'gy'), 0, 0, axis_index_groups=groups)  11 us
    ppermute x9, waiting for transfers between devices, moved(): return lax.ppermute(block, ('gx', 'gy'), route)  8 us
    pallas_call x1, Pallas kernels, packed(): pl.pallas_call(pack_kernel, out_shape=(S((2, channels, LANES), BF16),) *...  2.88 us
  transfers between devices with their start and end apart: 11, of which 3 were waited for; matrix products, arithmetic and copies ran while one was open for 0% of the time, Pallas kernels for 24%

profile of v3, /device:TPU:1, one launch (start us, length us, event | category | flops | bytes accessed | tf_op | source)
XLA Modules:
  0.0 116.0 jit_solution(17107847963937721665)
XLA Ops:
  0.6 0.0 copy-start.1
  0.6 0.0 copy-start
  0.7 0.0 copy-start.3
  0.7 2.9 %pack.1 = (bf16[2,192,128]{2,1,0:T(8,128)(2,1)}, bf16[2,192,128]{2,1,0:T(8,128)(2,1)}, bf16[2,192,128]{2,1,0:T(8,128)(2,1)}, bf16[2,192,128]{2,1,0:T(8,128)(2,1)...) custom-call(bf16[8,8,24,192]{3,2,1,0:T(8,128)(2,1)} %tokens_ref.1, ...), custom_call_target="tpu_custom_call" | custom-call | tf_op jit(solution)/shard_map/pack/pallas_call | solution.py:86
  3.5 8.0 %collective-permute-start.3 = (bf16[2,192,128]{2,1,0:T(8,128)(2,1)}, bf16[2,192,128]{2,1,0:T(8,128)(2,1)S(1)}, u32[]{:S(2)}, u32[]{:S(2)}) collective-permute-start(bf16[2,192,128]{2,1,0:T(8,128)(2,1)} %get-tuple-element.63), channel_id=1, source_target_pairs={{0,255},{1,240},{2,241},{3,242},{4,243},{5,244},{6,245},{7,246},{8... | collective-permute-start | bytes 294920 | tf_op jit(solution)/shard_map/ppermute | solution.py:462
  11.5 0.3 collective-permute-start.4
  11.8 3.5 %collective-permute-start.5 = (bf16[2,192,128]{2,1,0:T(8,128)(2,1)}, bf16[2,192,128]{2,1,0:T(8,128)(2,1)S(1)}, u32[]{:S(2)}, u32[]{:S(2)}) collective-permute-start(bf16[2,192,128]{2,1,0:T(8,128)(2,1)} %get-tuple-element.65), channel_id=1, source_target_pairs={{0,15},{1,0},{2,1},{3,2},{4,3},{5,4},{6,5},{7,6},{8,7},{9,8},{10,9... | collective-permute-start | bytes 294920 | tf_op jit(solution)/shard_map/ppermute | solution.py:462
  15.3 2.7 %collective-permute-start = (bf16[2,2,192,128]{3,2,1,0:T(8,128)(2,1)}, bf16[2,2,192,128]{3,2,1,0:T(8,128)(2,1)S(1)}, u32[]{:S(2)}, u32[]{:S(2)}) collective-permute-start(bf16[2,2,192,128]{3,2,1,0:T(8,128)(2,1)} %get-tuple-element.48), channel_id=1, source_target_pairs={{0,255},{1,240},{2,241},{3,242},{4,243},{5,244},{6,245},{7,246},{8... | collective-permute-start | bytes 589832 | tf_op jit(solution)/shard_map/ppermute | solution.py:462
  18.0 1.2 collective-permute-start.1
  19.2 0.0 copy-start.2
  19.2 0.0 copy-start.7
  19.2 0.0 copy-done.1
  19.2 0.0 copy-done
  19.2 0.0 copy-done.3
  19.2 0.7 copy-done.2
  19.8 0.0 copy-start.5
  19.8 0.3 prepare.1
  20.1 0.0 collective-permute-done.3.q00_ref
  20.1 0.0 copy-done.7
  20.1 0.1 collective-permute-start.2
  20.2 0.0 collective-permute-done.4.q01_ref
  20.2 0.0 collective-permute-done.5.q10_ref
  20.2 0.5 copy-done.5
  20.8 0.0 copy-start.4
  20.8 9.9 %attend.3 = (bf16[2,2,192,128]{3,2,1,0:T(8,128)(2,1)S(1)}, bf16[2,2,192,128]{3,2,1,0:T(8,128)(2,1)S(1)}, f32[1280,128]{1,0:T(8,128)S(1)}) custom-call(bf16[2,192,128]{2,1,0:T(8,128)(2,1)S(1)} %collective-permute-done.3.q00_ref, bf16[2,192,128]{2,1,0:T(8,128)(2,1)S(1)} %collective-permute-done.4.q01_ref, ...), custom_call_target="tpu_custom_call" | custom-call | flops 9663676416 | bytes 4194304 | tf_op jit(solution)/shard_map/attend/pallas_call | solution.py:423
  30.6 0.0 collective-permute-done.q00_ref
  30.6 0.0 collective-permute-done.1.q01_ref
  30.6 0.0 collective-permute-done.2.q10_ref
  30.7 0.0 copy-done.4
  30.7 10.9 %attend.4 = (bf16[2,2,2,192,128]{4,3,2,1,0:T(8,128)(2,1)S(1)}, bf16[2,2,2,192,128]{4,3,2,1,0:T(8,128)(2,1)S(1)}, f32[1280,128]{1,0:T(8,128)S(1)}) custom-call(bf16[2,2,192,128]{3,2,1,0:T(8,128)(2,1)S(1)} %collective-permute-done.q00_ref, bf16[2,2,192,128]{3,2,1,0:T(8,128)(2,1)S(1)} %collective-permute-done.1.q01_ref, ...), custom_call_target="tpu_custom_call" | custom-call | flops 9663676416 | bytes 4194304 | tf_op jit(solution)/shard_map/attend/pallas_call | solution.py:423
  41.6 1.1 collective-permute-start.6
  42.7 16.3 %attend.5 = (bf16[2,2,192,128]{3,2,1,0:T(8,128)(2,1)S(1)}, bf16[2,2,192,128]{3,2,1,0:T(8,128)(2,1)S(1)}, bf16[1280,128]{1,0:T(8,128)(2,1)}) custom-call(bf16[2,2,192,128]{3,2,1,0:T(8,128)(2,1)S(1)} %collective-permute-done.q00_ref, bf16[2,2,192,128]{3,2,1,0:T(8,128)(2,1)S(1)} %collective-permute-done.1.q01_ref, ...), custom_call_target="tpu_custom_call" | custom-call | flops 9663676416 | bytes 4194304 | tf_op jit(solution)/shard_map/attend/pallas_call | solution.py:423
  58.9 0.0 collective-permute-done.6.paired_low
  58.9 8.5 %all-to-all-start = ((bf16[32,40,128]{2,1,0:T(8,128)(2,1)}), bf16[32,40,128]{2,1,0:T(8,128)(2,1)S(1)}, u32[]{:S(2)}, u32[]{:S(2)}) async-start(bf16[32,40,128]{2,1,0:T(8,128)(2,1)} %bitcast.2), calls=%async_computation | async-start | bytes 655360 | tf_op jit(solution)/shard_map/all_to_all | solution.py:472
  67.5 1.5 %collective-permute-start.7 = (bf16[2,2,192,128]{3,2,1,0:T(8,128)(2,1)S(1)}, bf16[2,2,192,128]{3,2,1,0:T(8,128)(2,1)S(1)}, u32[]{:S(2)}, u32[]{:S(2)}) collective-permute-start(bf16[2,2,192,128]{3,2,1,0:T(8,128)(2,1)S(1)} %get-tuple-element.75), channel_id=1, source_target_pairs={{0,16},{1,17},{2,18},{3,19},{4,20},{5,21},{6,22},{7,23},{8,24},{9,... | collective-permute-start | bytes 589832 | tf_op jit(solution)/shard_map/ppermute | solution.py:462
  69.0 8.0 %collective-permute-done.7.middle_low = bf16[2,2,192,128]{3,2,1,0:T(8,128)(2,1)S(1)} collective-permute-done((bf16[2,2,192,128]{3,2,1,0:T(8,128)(2,1)S(1)}, bf16[2,2,192,128]{3,2,1,0:T(8,128)(2,1)S(1)}, u32[]{:S(2)}, u32[]{:S(2)}) %collective-permute-start.7) | collective-permute-done | bytes 196640 | tf_op jit(solution)/shard_map/ppermute | solution.py:462
  77.0 2.9 %all-to-all-done = bf16[32,40,128]{2,1,0:T(8,128)(2,1)S(1)} async-done(((bf16[32,40,128]{2,1,0:T(8,128)(2,1)}), bf16[32,40,128]{2,1,0:T(8,128)(2,1)S(1)}, u32[]{:S(2)}, u32[]{:S(2)}) %all-to-all-start) | async-done | bytes 327712 | tf_op jit(solution)/shard_map/all_to_all | solution.py:472
  79.9 0.1 pad_maximum_fusion
  80.0 0.1 collective-permute-start.8
  80.1 0.1 reduce_sum.24
  80.1 14.2 %all_to_all.15 = bf16[8,40,128]{2,1,0:T(8,128)(2,1)S(1)} all-to-all(bf16[8,40,128]{2,1,0:T(8,128)(2,1)S(1)} %broadcast_in_dim.20), channel_id=1, replica_groups={{0,32,64,96,128,160,192,224},{1,33,65,97,129,161,193,225},{2,34,66,98,1..., dimensions={0} | all-to-all | bytes 163840 | tf_op jit(solution)/shard_map/all_to_all | solution.py:472
  94.4 0.0 collective-permute-done.8.low_y_ref
  94.4 0.8 broadcast_in_dim.21
  95.2 8.4 %all-to-all-start.2 = ((bf16[32,40,128]{2,1,0:T(8,128)(2,1)}), bf16[32,40,128]{2,1,0:T(8,128)(2,1)S(1)}, u32[]{:S(2)}, u32[]{:S(2)}) async-start(bf16[32,40,128]{2,1,0:T(8,128)(2,1)} %broadcast_in_dim.21), calls=%async_computation.2 | async-start | bytes 655360 | tf_op jit(solution)/shard_map/all_to_all | solution.py:472
  103.6 1.6 %unpack.1 = (bf16[8,8,24,192]{3,2,1,0:T(8,128)(2,1)}, bf16[8,8,24,192]{3,2,1,0:T(8,128)(2,1)}) custom-call(bf16[6,2,192,128]{3,2,1,0:T(8,128)(2,1)S(1)} %collective-permute-done.8.low_y_ref, bf16[2,2,2,192,128]{4,3,2,1,0:T(8,128)(2,1)S(1)} %collective-permute-done.6.paired_low, bf16[2,2,2,192,128]{4,3,2,1,0:T(8,128)(2,1)S(1)} %get-tuple-element.79.paired_high, ...), custom_call_target="tpu_custom_call" | custom-call | tf_op jit(solution)/shard_map/unpack/pallas_call | solution.py:159
  105.2 8.1 %all-to-all-done.2 = bf16[32,40,128]{2,1,0:T(8,128)(2,1)S(1)} async-done(((bf16[32,40,128]{2,1,0:T(8,128)(2,1)}), bf16[32,40,128]{2,1,0:T(8,128)(2,1)S(1)}, u32[]{:S(2)}, u32[]{:S(2)}) %all-to-all-start.2) | async-done | bytes 327712 | tf_op jit(solution)/shard_map/all_to_all | solution.py:472
  113.3 0.7 copy-done.6
  114.1 1.9 %unpack_grads.1 = (f32[192,576]{1,0:T(8,128)}, f32[192,192]{1,0:T(8,128)}, f32[1,192]{1,0:T(1,128)}, f32[1,192]{1,0:T(1,128)}) custom-call(bf16[1280,128]{1,0:T(8,128)(2,1)} %bitcast.12), custom_call_target="tpu_custom_call" | custom-call | tf_op jit(solution)/shard_map/unpack_grads/pallas_call | solution.py:505
  (6 shorter events, 0.1 us)
Async XLA Ops:
  0.6 18.5 %copy-start.1 = (bf16[192,192]{1,0:T(8,128)(2,1)S(1)}, bf16[192,192]{1,0:T(8,128)(2,1)}, u32[]{:S(2)}) copy-start(bf16[192,192]{1,0:T(8,128)(2,1)} %proj_ref.3) | copy-start | bytes 221188
  0.6 18.5 %copy-start = (bf16[192,576]{1,0:T(8,128)(2,1)S(1)}, bf16[192,576]{1,0:T(8,128)(2,1)}, u32[]{:S(2)}) copy-start(bf16[192,576]{1,0:T(8,128)(2,1)} %wqkv_ref.7) | copy-start | bytes 663556
  0.7 18.5 %copy-start.3 = (f32[192]{0:T(256)S(1)}, f32[192]{0:T(256)}, u32[]{:S(2)}) copy-start(f32[192]{0:T(256)} %param.9) | copy-start | bytes 2308
  3.5 16.6 %collective-permute-start.3 = (bf16[2,192,128]{2,1,0:T(8,128)(2,1)}, bf16[2,192,128]{2,1,0:T(8,128)(2,1)S(1)}, u32[]{:S(2)}, u32[]{:S(2)}) collective-permute-start(bf16[2,192,128]{2,1,0:T(8,128)(2,1)} %get-tuple-element.63), channel_id=1, source_target_pairs={{0,255},{1,240},{2,241},{3,242},{4,243},{5,244},{6,245},{7,246},{8... | collective-permute-start | bytes 294920 | tf_op jit(solution)/shard_map/ppermute | solution.py:462
  11.5 8.7 %collective-permute-start.4 = (bf16[2,192,128]{2,1,0:T(8,128)(2,1)}, bf16[2,192,128]{2,1,0:T(8,128)(2,1)S(1)}, u32[]{:S(2)}, u32[]{:S(2)}) collective-permute-start(bf16[2,192,128]{2,1,0:T(8,128)(2,1)} %get-tuple-element.64), channel_id=1, source_target_pairs={{0,240},{1,241},{2,242},{3,243},{4,244},{5,245},{6,246},{7,247},{8... | collective-permute-start | bytes 294920 | tf_op jit(solution)/shard_map/ppermute | solution.py:462
  11.8 8.4 %collective-permute-start.5 = (bf16[2,192,128]{2,1,0:T(8,128)(2,1)}, bf16[2,192,128]{2,1,0:T(8,128)(2,1)S(1)}, u32[]{:S(2)}, u32[]{:S(2)}) collective-permute-start(bf16[2,192,128]{2,1,0:T(8,128)(2,1)} %get-tuple-element.65), channel_id=1, source_target_pairs={{0,15},{1,0},{2,1},{3,2},{4,3},{5,4},{6,5},{7,6},{8,7},{9,8},{10,9... | collective-permute-start | bytes 294920 | tf_op jit(solution)/shard_map/ppermute | solution.py:462
  15.3 15.3 %collective-permute-start = (bf16[2,2,192,128]{3,2,1,0:T(8,128)(2,1)}, bf16[2,2,192,128]{3,2,1,0:T(8,128)(2,1)S(1)}, u32[]{:S(2)}, u32[]{:S(2)}) collective-permute-start(bf16[2,2,192,128]{3,2,1,0:T(8,128)(2,1)} %get-tuple-element.48), channel_id=1, source_target_pairs={{0,255},{1,240},{2,241},{3,242},{4,243},{5,244},{6,245},{7,246},{8... | collective-permute-start | bytes 589832 | tf_op jit(solution)/shard_map/ppermute | solution.py:462
  18.0 12.6 %collective-permute-start.1 = (bf16[2,2,192,128]{3,2,1,0:T(8,128)(2,1)}, bf16[2,2,192,128]{3,2,1,0:T(8,128)(2,1)S(1)}, u32[]{:S(2)}, u32[]{:S(2)}) collective-permute-start(bf16[2,2,192,128]{3,2,1,0:T(8,128)(2,1)} %get-tuple-element.49), channel_id=1, source_target_pairs={{0,240},{1,241},{2,242},{3,243},{4,244},{5,245},{6,246},{7,247},{8... | collective-permute-start | bytes 589832 | tf_op jit(solution)/shard_map/ppermute | solution.py:462
  19.2 0.7 copy-start.2
  19.2 1.0 copy-start.7
  19.8 0.9 copy-start.5
  20.1 10.5 %collective-permute-start.2 = (bf16[2,2,192,128]{3,2,1,0:T(8,128)(2,1)S(1)}, bf16[2,2,192,128]{3,2,1,0:T(8,128)(2,1)S(1)}, u32[]{:S(2)}, u32[]{:S(2)}) collective-permute-start(bf16[2,2,192,128]{3,2,1,0:T(8,128)(2,1)S(1)} %copy-done.7), channel_id=1, source_target_pairs={{0,15},{1,0},{2,1},{3,2},{4,3},{5,4},{6,5},{7,6},{8,7},{9,8},{10,9... | collective-permute-start | bytes 589832 | tf_op jit(solution)/shard_map/ppermute | solution.py:462
  20.8 9.9 %copy-start.4 = (bf16[2,2,192,128]{3,2,1,0:T(8,128)(2,1)S(1)}, bf16[2,2,192,128]{3,2,1,0:T(8,128)(2,1)}, u32[]{:S(2)}) copy-start(bf16[2,2,192,128]{3,2,1,0:T(8,128)(2,1)} %get-tuple-element.51.q11_ref) | copy-start | bytes 589828
  41.6 17.3 %collective-permute-start.6 = (bf16[2,2,2,192,128]{4,3,2,1,0:T(8,128)(2,1)S(1)}, bf16[2,2,2,192,128]{4,3,2,1,0:T(8,128)(2,1)S(1)}, u32[]{:S(2)}, u32[]{:S(2)}) collective-permute-start(bf16[2,2,2,192,128]{4,3,2,1,0:T(8,128)(2,1)S(1)} %get-tuple-element.72), channel_id=1, source_target_pairs={{0,16},{1,17},{2,18},{3,19},{4,20},{5,21},{6,22},{7,23},{8,24},{9,... | collective-permute-start | bytes 1179656 | tf_op jit(solution)/shard_map/ppermute | solution.py:462
  58.9 20.9 %all-to-all-start = ((bf16[32,40,128]{2,1,0:T(8,128)(2,1)}), bf16[32,40,128]{2,1,0:T(8,128)(2,1)S(1)}, u32[]{:S(2)}, u32[]{:S(2)}) async-start(bf16[32,40,128]{2,1,0:T(8,128)(2,1)} %bitcast.2), calls=%async_computation | async-start | bytes 655360 | tf_op jit(solution)/shard_map/all_to_all | solution.py:472
  67.5 9.5 %collective-permute-start.7 = (bf16[2,2,192,128]{3,2,1,0:T(8,128)(2,1)S(1)}, bf16[2,2,192,128]{3,2,1,0:T(8,128)(2,1)S(1)}, u32[]{:S(2)}, u32[]{:S(2)}) collective-permute-start(bf16[2,2,192,128]{3,2,1,0:T(8,128)(2,1)S(1)} %get-tuple-element.75), channel_id=1, source_target_pairs={{0,16},{1,17},{2,18},{3,19},{4,20},{5,21},{6,22},{7,23},{8,24},{9,... | collective-permute-start | bytes 589832 | tf_op jit(solution)/shard_map/ppermute | solution.py:462
  80.0 14.4 %collective-permute-start.8 = (bf16[6,2,192,128]{3,2,1,0:T(8,128)(2,1)S(1)}, bf16[6,2,192,128]{3,2,1,0:T(8,128)(2,1)S(1)}, u32[]{:S(2)}, u32[]{:S(2)}) collective-permute-start(bf16[6,2,192,128]{3,2,1,0:T(8,128)(2,1)S(1)} %pad_maximum_fusion), channel_id=1, source_target_pairs={{0,1},{1,2},{2,3},{3,4},{4,5},{5,6},{6,7},{7,8},{8,9},{9,10},{10,1... | collective-permute-start | bytes 1769480 | tf_op jit(solution)/shard_map/ppermute | solution.py:462
  95.2 18.2 %all-to-all-start.2 = ((bf16[32,40,128]{2,1,0:T(8,128)(2,1)}), bf16[32,40,128]{2,1,0:T(8,128)(2,1)S(1)}, u32[]{:S(2)}, u32[]{:S(2)}) async-start(bf16[32,40,128]{2,1,0:T(8,128)(2,1)} %broadcast_in_dim.21), calls=%async_computation.2 | async-start | bytes 655360 | tf_op jit(solution)/shard_map/all_to_all | solution.py:472
  113.3 0.7 copy-start.6

commit v4 on v2

--- a/solution.py
+++ b/solution.py
@@ -354,12 +354,8 @@
         step(1, 1, three=False, four=False)
         step(2, 0, four=False)
 
-        def two_steps(j, carry):
-            step(3 + 2 * j, 1)
-            step(4 + 2 * j, 0)
-            return carry
-
-        lax.fori_loop(0, (HEADS - 4) // 2, two_steps, 0)
+        for i in range(3, HEADS - 1):
+            step(i, i % 2)
         step(HEADS - 1, 1, ahead=False)
         step(HEADS, 0, one=False, ahead=False)
         step(HEADS + 1, 1, one=False, two=False, ahead=False)
@@ -544,8 +540,8 @@
     tile_x, tile_y, depth, channels = tokens.shape
     nx, ny = lax.axis_size("gx"), lax.axis_size("gy")
     first = packed(tokens, cotangent, True)
-    first, tokens, cotangent, ln_gain, ln_bias, qkv_weight, proj_weight = lax.optimization_barrier(
-        (first, tokens, cotangent, ln_gain, ln_bias, qkv_weight, proj_weight)
+    first, tokens, cotangent, proj_weight = lax.optimization_barrier(
+        (first, tokens, cotangent, proj_weight)
     )
     rest = packed(tokens, cotangent, False)
     gain, bias, wqkv_t, proj_t, *features = prepared(ln_gain, ln_bias, qkv_weight, proj_weight)

time: 115 us -> 115 us (level)
  no operation moved by 1% of the time
where the time goes in v4:
time: 115 us
  Pallas kernels  51.5 us (45%)
  starting transfers between devices  30.6 us (27%)
  waiting for transfers between devices  19 us (17%)
  blocking collectives  10.5 us (9%)
  local copies, waits for them, and re-layouts  2.76 us (2%)
    pallas_call x3, Pallas kernels, attend(): pl.pallas_call(functools.partial(attend_kernel, turn), out_shape=(S((2, 2...  43 us
    ppermute x9, starting transfers between devices, moved(): return lax.ppermute(block, ('gx', 'gy'), route)  17.7 us
    all_to_all x2, starting transfers between devices, exchanged(): return lax.all_to_all(pieces, ('gx', 'gy'), 0, 0, axis_index_groups=groups)  12.9 us
    all_to_all x2, waiting for transfers between devices, exchanged(): return lax.all_to_all(pieces, ('gx', 'gy'), 0, 0, axis_index_groups=groups)  12 us
    all_to_all x1, blocking collectives, exchanged(): return lax.all_to_all(pieces, ('gx', 'gy'), 0, 0, axis_index_groups=groups)  10.5 us
    ppermute x9, waiting for transfers between devices, moved(): return lax.ppermute(block, ('gx', 'gy'), route)  7.02 us
    pallas_call x2, Pallas kernels, packed(): pl.pallas_call(pack_first_kernel if first else pack_rest_kernel, out_shap...  4.78 us
  transfers between devices with their start and end apart: 11, of which 3 were waited for; matrix products, arithmetic and copies ran while one was open for 0% of the time, Pallas kernels for 32%

profile of v4, /device:TPU:1, one launch (start us, length us, event | category | flops | bytes accessed | tf_op | source)
XLA Modules:
  0.0 115.4 jit_solution(14346921017735926899)
XLA Ops:
  0.6 2.2 %pack_first.1 = (bf16[2,192,128]{2,1,0:T(8,128)(2,1)}, bf16[2,192,128]{2,1,0:T(8,128)(2,1)}, bf16[2,192,128]{2,1,0:T(8,128)(2,1)}, bf16[2,192,128]{2,1,0:T(8,128)(2,1)}) custom-call(bf16[8,8,24,192]{3,2,1,0:T(8,128)(2,1)} %tokens_ref.2, bf16[8,8,24,192]{3,2,1,0:T(8,128)(2,1)} %cot_ref.2), custom_call_target="tpu_custom_call" | custom-call | tf_op jit(solution)/shard_map/pack_first/pallas_call | solution.py:104
  2.8 0.0 copy-start
  2.9 0.0 copy-start.1
  2.9 8.0 %collective-permute-start.3 = (bf16[2,192,128]{2,1,0:T(8,128)(2,1)}, bf16[2,192,128]{2,1,0:T(8,128)(2,1)S(1)}, u32[]{:S(2)}, u32[]{:S(2)}) collective-permute-start(bf16[2,192,128]{2,1,0:T(8,128)(2,1)} %get-tuple-element.67), channel_id=1, source_target_pairs={{0,255},{1,240},{2,241},{3,242},{4,243},{5,244},{6,245},{7,246},{8... | collective-permute-start | bytes 294920 | tf_op jit(solution)/shard_map/ppermute | solution.py:482
  10.8 0.3 collective-permute-start.4
  11.1 3.5 %collective-permute-start.5 = (bf16[2,192,128]{2,1,0:T(8,128)(2,1)}, bf16[2,192,128]{2,1,0:T(8,128)(2,1)S(1)}, u32[]{:S(2)}, u32[]{:S(2)}) collective-permute-start(bf16[2,192,128]{2,1,0:T(8,128)(2,1)} %get-tuple-element.69), channel_id=1, source_target_pairs={{0,15},{1,0},{2,1},{3,2},{4,3},{5,4},{6,5},{7,6},{8,7},{9,8},{10,9... | collective-permute-start | bytes 294920 | tf_op jit(solution)/shard_map/ppermute | solution.py:482
  14.6 0.0 copy-start.3
  14.6 2.6 %pack_rest.1 = (bf16[2,2,192,128]{3,2,1,0:T(8,128)(2,1)}, bf16[2,2,192,128]{3,2,1,0:T(8,128)(2,1)}, bf16[2,2,192,128]{3,2,1,0:T(8,128)(2,1)}, bf16[2,2,192,128]{3,2,1,0:T(8,128)(2,1)}) custom-call(bf16[8,8,24,192]{3,2,1,0:T(8,128)(2,1)} %tokens_ref.2, bf16[8,8,24,192]{3,2,1,0:T(8,128)(2,1)} %cot_ref.2), custom_call_target="tpu_custom_call" | custom-call | tf_op jit(solution)/shard_map/pack_rest/pallas_call | solution.py:104
  17.2 2.8 %collective-permute-start = (bf16[2,2,192,128]{3,2,1,0:T(8,128)(2,1)}, bf16[2,2,192,128]{3,2,1,0:T(8,128)(2,1)S(1)}, u32[]{:S(2)}, u32[]{:S(2)}) collective-permute-start(bf16[2,2,192,128]{3,2,1,0:T(8,128)(2,1)} %get-tuple-element.56), channel_id=1, source_target_pairs={{0,255},{1,240},{2,241},{3,242},{4,243},{5,244},{6,245},{7,246},{8... | collective-permute-start | bytes 589832 | tf_op jit(solution)/shard_map/ppermute | solution.py:482
  20.0 1.2 %collective-permute-start.1 = (bf16[2,2,192,128]{3,2,1,0:T(8,128)(2,1)}, bf16[2,2,192,128]{3,2,1,0:T(8,128)(2,1)S(1)}, u32[]{:S(2)}, u32[]{:S(2)}) collective-permute-start(bf16[2,2,192,128]{3,2,1,0:T(8,128)(2,1)} %get-tuple-element.57), channel_id=1, source_target_pairs={{0,240},{1,241},{2,242},{3,243},{4,244},{5,245},{6,246},{7,247},{8... | collective-permute-start | bytes 589832 | tf_op jit(solution)/shard_map/ppermute | solution.py:482
  21.1 0.0 copy-start.2
  21.1 0.0 copy-start.7
  21.1 0.0 copy-done
  21.1 0.0 copy-done.1
  21.2 0.0 copy-done.3
  21.2 0.7 copy-done.2
  21.8 0.0 copy-start.5
  21.8 0.3 prepare.1
  22.1 0.0 collective-permute-done.3.q00_ref
  22.1 0.0 copy-done.7
  22.1 0.1 collective-permute-start.2
  22.2 0.0 collective-permute-done.4.q01_ref
  22.2 0.0 collective-permute-done.5.q10_ref
  22.2 0.5 copy-done.5
  22.7 15.8 %attend.3 = (bf16[2,2,192,128]{3,2,1,0:T(8,128)(2,1)S(1)}, bf16[2,2,192,128]{3,2,1,0:T(8,128)(2,1)S(1)}, f32[1280,128]{1,0:T(8,128)S(1)}) custom-call(bf16[2,192,128]{2,1,0:T(8,128)(2,1)S(1)} %collective-permute-done.3.q00_ref, bf16[2,192,128]{2,1,0:T(8,128)(2,1)S(1)} %collective-permute-done.4.q01_ref, ...), custom_call_target="tpu_custom_call" | custom-call | flops 9663676416 | bytes 4194304 | tf_op jit(solution)/shard_map/attend/pallas_call | solution.py:443
  38.5 0.0 collective-permute-done.q00_ref
  38.5 0.0 collective-permute-done.1.q01_ref
  38.5 0.0 collective-permute-done.2.q10_ref
  38.5 0.0 copy-done.4
  38.5 10.9 %attend.4 = (bf16[2,2,2,192,128]{4,3,2,1,0:T(8,128)(2,1)S(1)}, bf16[2,2,2,192,128]{4,3,2,1,0:T(8,128)(2,1)S(1)}, f32[1280,128]{1,0:T(8,128)S(1)}) custom-call(bf16[2,2,192,128]{3,2,1,0:T(8,128)(2,1)S(1)} %collective-permute-done.q00_ref, bf16[2,2,192,128]{3,2,1,0:T(8,128)(2,1)S(1)} %collective-permute-done.1.q01_ref, ...), custom_call_target="tpu_custom_call" | custom-call | flops 9663676416 | bytes 4194304 | tf_op jit(solution)/shard_map/attend/pallas_call | solution.py:443
  49.5 0.4 collective-permute-start.6
  49.9 16.3 %attend.5 = (bf16[2,2,192,128]{3,2,1,0:T(8,128)(2,1)S(1)}, bf16[2,2,192,128]{3,2,1,0:T(8,128)(2,1)S(1)}, bf16[1280,128]{1,0:T(8,128)(2,1)}) custom-call(bf16[2,2,192,128]{3,2,1,0:T(8,128)(2,1)S(1)} %collective-permute-done.q00_ref, bf16[2,2,192,128]{3,2,1,0:T(8,128)(2,1)S(1)} %collective-permute-done.1.q01_ref, ...), custom_call_target="tpu_custom_call" | custom-call | flops 9663676416 | bytes 4194304 | tf_op jit(solution)/shard_map/attend/pallas_call | solution.py:443
  66.1 0.0 collective-permute-done.6.paired_low
  66.1 4.8 %all-to-all-start = ((bf16[32,40,128]{2,1,0:T(8,128)(2,1)}), bf16[32,40,128]{2,1,0:T(8,128)(2,1)S(1)}, u32[]{:S(2)}, u32[]{:S(2)}) async-start(bf16[32,40,128]{2,1,0:T(8,128)(2,1)} %bitcast.2), calls=%async_computation | async-start | bytes 655360 | tf_op jit(solution)/shard_map/all_to_all | solution.py:492
  70.9 1.5 %collective-permute-start.7 = (bf16[2,2,192,128]{3,2,1,0:T(8,128)(2,1)S(1)}, bf16[2,2,192,128]{3,2,1,0:T(8,128)(2,1)S(1)}, u32[]{:S(2)}, u32[]{:S(2)}) collective-permute-start(bf16[2,2,192,128]{3,2,1,0:T(8,128)(2,1)S(1)} %get-tuple-element.79), channel_id=1, source_target_pairs={{0,16},{1,17},{2,18},{3,19},{4,20},{5,21},{6,22},{7,23},{8,24},{9,... | collective-permute-start | bytes 589832 | tf_op jit(solution)/shard_map/ppermute | solution.py:482
  72.4 7.0 %collective-permute-done.7.middle_low = bf16[2,2,192,128]{3,2,1,0:T(8,128)(2,1)S(1)} collective-permute-done((bf16[2,2,192,128]{3,2,1,0:T(8,128)(2,1)S(1)}, bf16[2,2,192,128]{3,2,1,0:T(8,128)(2,1)S(1)}, u32[]{:S(2)}, u32[]{:S(2)}) %collective-permute-start.7) | collective-permute-done | bytes 196640 | tf_op jit(solution)/shard_map/ppermute | solution.py:482
  79.4 3.9 %all-to-all-done = bf16[32,40,128]{2,1,0:T(8,128)(2,1)S(1)} async-done(((bf16[32,40,128]{2,1,0:T(8,128)(2,1)}), bf16[32,40,128]{2,1,0:T(8,128)(2,1)S(1)}, u32[]{:S(2)}, u32[]{:S(2)}) %all-to-all-start) | async-done | bytes 327712 | tf_op jit(solution)/shard_map/all_to_all | solution.py:492
  83.3 0.1 pad_maximum_fusion
  83.4 0.1 collective-permute-start.8
  83.5 0.1 reduce_sum.24
  83.6 10.5 %all_to_all.15 = bf16[8,40,128]{2,1,0:T(8,128)(2,1)S(1)} all-to-all(bf16[8,40,128]{2,1,0:T(8,128)(2,1)S(1)} %broadcast_in_dim.20), channel_id=1, replica_groups={{0,32,64,96,128,160,192,224},{1,33,65,97,129,161,193,225},{2,34,66,98,1..., dimensions={0} | all-to-all | bytes 163840 | tf_op jit(solution)/shard_map/all_to_all | solution.py:492
  94.1 0.0 collective-permute-done.8.low_y_ref
  94.1 0.8 broadcast_in_dim.21
  94.8 8.1 %all-to-all-start.2 = ((bf16[32,40,128]{2,1,0:T(8,128)(2,1)}), bf16[32,40,128]{2,1,0:T(8,128)(2,1)S(1)}, u32[]{:S(2)}, u32[]{:S(2)}) async-start(bf16[32,40,128]{2,1,0:T(8,128)(2,1)} %broadcast_in_dim.21), calls=%async_computation.2 | async-start | bytes 655360 | tf_op jit(solution)/shard_map/all_to_all | solution.py:492
  103.0 1.6 %unpack.1 = (bf16[8,8,24,192]{3,2,1,0:T(8,128)(2,1)}, bf16[8,8,24,192]{3,2,1,0:T(8,128)(2,1)}) custom-call(bf16[6,2,192,128]{3,2,1,0:T(8,128)(2,1)S(1)} %collective-permute-done.8.low_y_ref, bf16[2,2,2,192,128]{4,3,2,1,0:T(8,128)(2,1)S(1)} %collective-permute-done.6.paired_low, bf16[2,2,2,192,128]{4,3,2,1,0:T(8,128)(2,1)S(1)} %get-tuple-element.83.paired_high, ...), custom_call_target="tpu_custom_call" | custom-call | tf_op jit(solution)/shard_map/unpack/pallas_call | solution.py:179
  104.6 8.1 %all-to-all-done.2 = bf16[32,40,128]{2,1,0:T(8,128)(2,1)S(1)} async-done(((bf16[32,40,128]{2,1,0:T(8,128)(2,1)}), bf16[32,40,128]{2,1,0:T(8,128)(2,1)S(1)}, u32[]{:S(2)}, u32[]{:S(2)}) %all-to-all-start.2) | async-done | bytes 327712 | tf_op jit(solution)/shard_map/all_to_all | solution.py:492
  112.7 0.7 copy-done.6
  113.5 1.9 %unpack_grads.1 = (f32[192,576]{1,0:T(8,128)}, f32[192,192]{1,0:T(8,128)}, f32[1,192]{1,0:T(1,128)}, f32[1,192]{1,0:T(1,128)}) custom-call(bf16[1280,128]{1,0:T(8,128)(2,1)} %bitcast.12), custom_call_target="tpu_custom_call" | custom-call | tf_op jit(solution)/shard_map/unpack_grads/pallas_call | solution.py:525
  (7 shorter events, 0.1 us)
Async XLA Ops:
  2.8 18.3 %copy-start = (bf16[192,576]{1,0:T(8,128)(2,1)S(1)}, bf16[192,576]{1,0:T(8,128)(2,1)}, u32[]{:S(2)}) copy-start(bf16[192,576]{1,0:T(8,128)(2,1)} %wqkv_ref.7) | copy-start | bytes 663556
  2.9 18.3 %copy-start.1 = (bf16[192,192]{1,0:T(8,128)(2,1)S(1)}, bf16[192,192]{1,0:T(8,128)(2,1)}, u32[]{:S(2)}) copy-start(bf16[192,192]{1,0:T(8,128)(2,1)} %proj_ref.3) | copy-start | bytes 221188
  2.9 19.2 %collective-permute-start.3 = (bf16[2,192,128]{2,1,0:T(8,128)(2,1)}, bf16[2,192,128]{2,1,0:T(8,128)(2,1)S(1)}, u32[]{:S(2)}, u32[]{:S(2)}) collective-permute-start(bf16[2,192,128]{2,1,0:T(8,128)(2,1)} %get-tuple-element.67), channel_id=1, source_target_pairs={{0,255},{1,240},{2,241},{3,242},{4,243},{5,244},{6,245},{7,246},{8... | collective-permute-start | bytes 294920 | tf_op jit(solution)/shard_map/ppermute | solution.py:482
  10.8 11.3 %collective-permute-start.4 = (bf16[2,192,128]{2,1,0:T(8,128)(2,1)}, bf16[2,192,128]{2,1,0:T(8,128)(2,1)S(1)}, u32[]{:S(2)}, u32[]{:S(2)}) collective-permute-start(bf16[2,192,128]{2,1,0:T(8,128)(2,1)} %get-tuple-element.68), channel_id=1, source_target_pairs={{0,240},{1,241},{2,242},{3,243},{4,244},{5,245},{6,246},{7,247},{8... | collective-permute-start | bytes 294920 | tf_op jit(solution)/shard_map/ppermute | solution.py:482
  11.1 11.1 %collective-permute-start.5 = (bf16[2,192,128]{2,1,0:T(8,128)(2,1)}, bf16[2,192,128]{2,1,0:T(8,128)(2,1)S(1)}, u32[]{:S(2)}, u32[]{:S(2)}) collective-permute-start(bf16[2,192,128]{2,1,0:T(8,128)(2,1)} %get-tuple-element.69), channel_id=1, source_target_pairs={{0,15},{1,0},{2,1},{3,2},{4,3},{5,4},{6,5},{7,6},{8,7},{9,8},{10,9... | collective-permute-start | bytes 294920 | tf_op jit(solution)/shard_map/ppermute | solution.py:482
  14.6 6.5 %copy-start.3 = (f32[192]{0:T(256)S(1)}, f32[192]{0:T(256)}, u32[]{:S(2)}) copy-start(f32[192]{0:T(256)} %param.9) | copy-start | bytes 2308
  17.2 21.3 %collective-permute-start = (bf16[2,2,192,128]{3,2,1,0:T(8,128)(2,1)}, bf16[2,2,192,128]{3,2,1,0:T(8,128)(2,1)S(1)}, u32[]{:S(2)}, u32[]{:S(2)}) collective-permute-start(bf16[2,2,192,128]{3,2,1,0:T(8,128)(2,1)} %get-tuple-element.56), channel_id=1, source_target_pairs={{0,255},{1,240},{2,241},{3,242},{4,243},{5,244},{6,245},{7,246},{8... | collective-permute-start | bytes 589832 | tf_op jit(solution)/shard_map/ppermute | solution.py:482
  20.0 18.5 %collective-permute-start.1 = (bf16[2,2,192,128]{3,2,1,0:T(8,128)(2,1)}, bf16[2,2,192,128]{3,2,1,0:T(8,128)(2,1)S(1)}, u32[]{:S(2)}, u32[]{:S(2)}) collective-permute-start(bf16[2,2,192,128]{3,2,1,0:T(8,128)(2,1)} %get-tuple-element.57), channel_id=1, source_target_pairs={{0,240},{1,241},{2,242},{3,243},{4,244},{5,245},{6,246},{7,247},{8... | collective-permute-start | bytes 589832 | tf_op jit(solution)/shard_map/ppermute | solution.py:482
  21.1 0.7 copy-start.2
  21.1 1.0 copy-start.7
  21.8 0.9 copy-start.5
  22.1 16.4 %collective-permute-start.2 = (bf16[2,2,192,128]{3,2,1,0:T(8,128)(2,1)S(1)}, bf16[2,2,192,128]{3,2,1,0:T(8,128)(2,1)S(1)}, u32[]{:S(2)}, u32[]{:S(2)}) collective-permute-start(bf16[2,2,192,128]{3,2,1,0:T(8,128)(2,1)S(1)} %copy-done.7), channel_id=1, source_target_pairs={{0,15},{1,0},{2,1},{3,2},{4,3},{5,4},{6,5},{7,6},{8,7},{9,8},{10,9... | collective-permute-start | bytes 589832 | tf_op jit(solution)/shard_map/ppermute | solution.py:482
  22.7 15.8 %copy-start.4 = (bf16[2,2,192,128]{3,2,1,0:T(8,128)(2,1)S(1)}, bf16[2,2,192,128]{3,2,1,0:T(8,128)(2,1)}, u32[]{:S(2)}) copy-start(bf16[2,2,192,128]{3,2,1,0:T(8,128)(2,1)} %get-tuple-element.59.q11_ref) | copy-start | bytes 589828
  49.5 16.6 %collective-permute-start.6 = (bf16[2,2,2,192,128]{4,3,2,1,0:T(8,128)(2,1)S(1)}, bf16[2,2,2,192,128]{4,3,2,1,0:T(8,128)(2,1)S(1)}, u32[]{:S(2)}, u32[]{:S(2)}) collective-permute-start(bf16[2,2,2,192,128]{4,3,2,1,0:T(8,128)(2,1)S(1)} %get-tuple-element.76), channel_id=1, source_target_pairs={{0,16},{1,17},{2,18},{3,19},{4,20},{5,21},{6,22},{7,23},{8,24},{9,... | collective-permute-start | bytes 1179656 | tf_op jit(solution)/shard_map/ppermute | solution.py:482
  66.1 17.1 %all-to-all-start = ((bf16[32,40,128]{2,1,0:T(8,128)(2,1)}), bf16[32,40,128]{2,1,0:T(8,128)(2,1)S(1)}, u32[]{:S(2)}, u32[]{:S(2)}) async-start(bf16[32,40,128]{2,1,0:T(8,128)(2,1)} %bitcast.2), calls=%async_computation | async-start | bytes 655360 | tf_op jit(solution)/shard_map/all_to_all | solution.py:492
  70.9 8.5 %collective-permute-start.7 = (bf16[2,2,192,128]{3,2,1,0:T(8,128)(2,1)S(1)}, bf16[2,2,192,128]{3,2,1,0:T(8,128)(2,1)S(1)}, u32[]{:S(2)}, u32[]{:S(2)}) collective-permute-start(bf16[2,2,192,128]{3,2,1,0:T(8,128)(2,1)S(1)} %get-tuple-element.79), channel_id=1, source_target_pairs={{0,16},{1,17},{2,18},{3,19},{4,20},{5,21},{6,22},{7,23},{8,24},{9,... | collective-permute-start | bytes 589832 | tf_op jit(solution)/shard_map/ppermute | solution.py:482
  83.4 10.7 %collective-permute-start.8 = (bf16[6,2,192,128]{3,2,1,0:T(8,128)(2,1)S(1)}, bf16[6,2,192,128]{3,2,1,0:T(8,128)(2,1)S(1)}, u32[]{:S(2)}, u32[]{:S(2)}) collective-permute-start(bf16[6,2,192,128]{3,2,1,0:T(8,128)(2,1)S(1)} %pad_maximum_fusion), channel_id=1, source_target_pairs={{0,1},{1,2},{2,3},{3,4},{4,5},{5,6},{6,7},{7,8},{8,9},{9,10},{10,1... | collective-permute-start | bytes 1769480 | tf_op jit(solution)/shard_map/ppermute | solution.py:482
  94.8 17.9 %all-to-all-start.2 = ((bf16[32,40,128]{2,1,0:T(8,128)(2,1)}), bf16[32,40,128]{2,1,0:T(8,128)(2,1)S(1)}, u32[]{:S(2)}, u32[]{:S(2)}) async-start(bf16[32,40,128]{2,1,0:T(8,128)(2,1)} %broadcast_in_dim.21), calls=%async_computation.2 | async-start | bytes 655360 | tf_op jit(solution)/shard_map/all_to_all | solution.py:492
  112.7 0.7 copy-start.6

commit v5 on v3

--- a/solution.py
+++ b/solution.py
@@ -523,11 +523,14 @@
     first, proj_weight = lax.optimization_barrier((first, proj_weight))
     gain, bias, wqkv_t, proj_t, *features = prepared(ln_gain, ln_bias, qkv_weight, proj_weight)
     weights = (gain, bias, wqkv_t, qkv_weight, proj_weight, proj_t)
+    rest, features = lax.optimization_barrier((rest, features))
 
     steps = ((1, 1), (1, 0), (0, 1))
 
     def gathered(quads):
-        return [moved(quad, -x, -y) for quad, (x, y) in zip(quads, steps)] + [quads[3]]
+        order = [2, 0, 1]
+        got = {i: moved(quads[i], -steps[i][0], -steps[i][1]) for i in order}
+        return [got[0], got[1], got[2], quads[3]]
 
     first, rest = gathered(first), gathered(rest)
     low, high, sums = attend(0, first, features, weights, ())

time: 116 us -> 116 us (level)
  starting transfers between devices: 35.3 us -> 46.5 us
  Pallas kernels: 43.7 us -> 32.7 us
    all_to_all x2, starting transfers between devices: 16.9 us -> 28.4 us  [exchanged(): return lax.all_to_all(pieces, ('gx', 'gy'), 0, 0, axis_index_groups=groups)]
    pallas_call x3, Pallas kernels: 37.1 us -> 26 us  [attend(): pl.pallas_call(functools.partial(attend_kernel, turn), out_shape=(S((2, 2...]
  transfers between devices with their start and end apart: 11 -> 11, of which waited for: 3 -> 3; matrix products, arithmetic and copies ran while one was open for 0% -> 0% of each run, Pallas kernels for 24% -> 19%
where the time goes in v5:
time: 116 us; the launch traced here: 115 us
  starting transfers between devices  46.5 us (40%)
  Pallas kernels  32.7 us (28%)
  waiting for transfers between devices  19 us (16%)
  blocking collectives  13.8 us (12%)
  local copies, waits for them, and re-layouts  2.22 us (2%)
    all_to_all x2, starting transfers between devices, exchanged(): return lax.all_to_all(pieces, ('gx', 'gy'), 0, 0, axis_index_groups=groups)  28.4 us
    pallas_call x3, Pallas kernels, attend(): pl.pallas_call(functools.partial(attend_kernel, turn), out_shape=(S((2, 2...  26 us
    ppermute x9, starting transfers between devices, moved(): return lax.ppermute(block, ('gx', 'gy'), route)  18 us
    all_to_all x1, blocking collectives, exchanged(): return lax.all_to_all(pieces, ('gx', 'gy'), 0, 0, axis_index_groups=groups)  13.8 us
    all_to_all x2, waiting for transfers between devices, exchanged(): return lax.all_to_all(pieces, ('gx', 'gy'), 0, 0, axis_index_groups=groups)  12 us
    ppermute x9, waiting for transfers between devices, moved(): return lax.ppermute(block, ('gx', 'gy'), route)  7.02 us
    pallas_call x1, Pallas kernels, packed(): pl.pallas_call(pack_kernel, out_shape=(S((2, channels, LANES), BF16),) *...  2.88 us
  transfers between devices with their start and end apart: 11, of which 3 were waited for; matrix products, arithmetic and copies ran while one was open for 0% of the time, Pallas kernels for 19%

profile of v5, /device:TPU:1, one launch (start us, length us, event | category | flops | bytes accessed | tf_op | source)
XLA Modules:
  0.0 115.1 jit_solution(5022755663137261941)
XLA Ops:
  0.6 0.0 copy-start.1
  0.6 0.0 copy-start
  0.7 0.0 copy-start.3
  0.7 2.9 %pack.1 = (bf16[2,192,128]{2,1,0:T(8,128)(2,1)}, bf16[2,192,128]{2,1,0:T(8,128)(2,1)}, bf16[2,192,128]{2,1,0:T(8,128)(2,1)}, bf16[2,192,128]{2,1,0:T(8,128)(2,1)...) custom-call(bf16[8,8,24,192]{3,2,1,0:T(8,128)(2,1)} %tokens_ref.1, ...), custom_call_target="tpu_custom_call" | custom-call | tf_op jit(solution)/shard_map/pack/pallas_call | solution.py:86
  3.5 8.0 %collective-permute-start.3 = (bf16[2,192,128]{2,1,0:T(8,128)(2,1)}, bf16[2,192,128]{2,1,0:T(8,128)(2,1)S(1)}, u32[]{:S(2)}, u32[]{:S(2)}) collective-permute-start(bf16[2,192,128]{2,1,0:T(8,128)(2,1)} %get-tuple-element.75), channel_id=1, source_target_pairs={{0,255},{1,240},{2,241},{3,242},{4,243},{5,244},{6,245},{7,246},{8... | collective-permute-start | bytes 294920 | tf_op jit(solution)/shard_map/ppermute | solution.py:462
  11.5 0.3 collective-permute-start.4
  11.8 3.5 %collective-permute-start.5 = (bf16[2,192,128]{2,1,0:T(8,128)(2,1)}, bf16[2,192,128]{2,1,0:T(8,128)(2,1)S(1)}, u32[]{:S(2)}, u32[]{:S(2)}) collective-permute-start(bf16[2,192,128]{2,1,0:T(8,128)(2,1)} %get-tuple-element.77), channel_id=1, source_target_pairs={{0,15},{1,0},{2,1},{3,2},{4,3},{5,4},{6,5},{7,6},{8,7},{9,8},{10,9... | collective-permute-start | bytes 294920 | tf_op jit(solution)/shard_map/ppermute | solution.py:462
  15.3 0.0 copy-start.2
  15.3 0.0 copy-start.7
  15.3 0.0 copy-done.1
  15.3 0.0 copy-done
  15.3 0.0 copy-done.3
  15.3 0.7 copy-done.2
  16.0 0.0 copy-start.5
  16.0 0.3 prepare.1
  16.2 2.8 %collective-permute-start = (bf16[2,2,192,128]{3,2,1,0:T(8,128)(2,1)}, bf16[2,2,192,128]{3,2,1,0:T(8,128)(2,1)S(1)}, u32[]{:S(2)}, u32[]{:S(2)}) collective-permute-start(bf16[2,2,192,128]{3,2,1,0:T(8,128)(2,1)} %get-tuple-element.65), channel_id=1, source_target_pairs={{0,255},{1,240},{2,241},{3,242},{4,243},{5,244},{6,245},{7,246},{8... | collective-permute-start | bytes 589832 | tf_op jit(solution)/shard_map/ppermute | solution.py:462
  19.0 1.2 %collective-permute-start.1 = (bf16[2,2,192,128]{3,2,1,0:T(8,128)(2,1)}, bf16[2,2,192,128]{3,2,1,0:T(8,128)(2,1)S(1)}, u32[]{:S(2)}, u32[]{:S(2)}) collective-permute-start(bf16[2,2,192,128]{3,2,1,0:T(8,128)(2,1)} %get-tuple-element.66), channel_id=1, source_target_pairs={{0,240},{1,241},{2,242},{3,243},{4,244},{5,245},{6,246},{7,247},{8... | collective-permute-start | bytes 589832 | tf_op jit(solution)/shard_map/ppermute | solution.py:462
  20.2 0.0 collective-permute-done.3.q00_ref
  20.2 0.0 copy-done.7
  20.2 0.0 collective-permute-start.2
  20.2 0.0 collective-permute-done.4.q01_ref
  20.2 0.0 collective-permute-done.5.q10_ref
  20.2 0.0 copy-done.5
  20.2 0.0 copy-start.4
  20.2 9.9 %attend.3 = (bf16[2,2,192,128]{3,2,1,0:T(8,128)(2,1)S(1)}, bf16[2,2,192,128]{3,2,1,0:T(8,128)(2,1)S(1)}, f32[1280,128]{1,0:T(8,128)S(1)}) custom-call(bf16[2,192,128]{2,1,0:T(8,128)(2,1)S(1)} %collective-permute-done.3.q00_ref, bf16[2,192,128]{2,1,0:T(8,128)(2,1)S(1)} %collective-permute-done.4.q01_ref, ...), custom_call_target="tpu_custom_call" | custom-call | flops 9663676416 | bytes 4194304 | tf_op jit(solution)/shard_map/attend/pallas_call | solution.py:423
  30.1 0.0 collective-permute-done.q00_ref
  30.1 0.0 collective-permute-done.1.q01_ref
  30.1 0.0 collective-permute-done.2.q10_ref
  30.1 0.0 copy-done.4
  30.1 5.8 %attend.4 = (bf16[2,2,2,192,128]{4,3,2,1,0:T(8,128)(2,1)S(1)}, bf16[2,2,2,192,128]{4,3,2,1,0:T(8,128)(2,1)S(1)}, f32[1280,128]{1,0:T(8,128)S(1)}) custom-call(bf16[2,2,192,128]{3,2,1,0:T(8,128)(2,1)S(1)} %collective-permute-done.q00_ref, bf16[2,2,192,128]{3,2,1,0:T(8,128)(2,1)S(1)} %collective-permute-done.1.q01_ref, ...), custom_call_target="tpu_custom_call" | custom-call | flops 9663676416 | bytes 4194304 | tf_op jit(solution)/shard_map/attend/pallas_call | solution.py:423
  35.9 0.8 collective-permute-start.6
  36.7 10.4 %attend.5 = (bf16[2,2,192,128]{3,2,1,0:T(8,128)(2,1)S(1)}, bf16[2,2,192,128]{3,2,1,0:T(8,128)(2,1)S(1)}, bf16[1280,128]{1,0:T(8,128)(2,1)}) custom-call(bf16[2,2,192,128]{3,2,1,0:T(8,128)(2,1)S(1)} %collective-permute-done.q00_ref, bf16[2,2,192,128]{3,2,1,0:T(8,128)(2,1)S(1)} %collective-permute-done.1.q01_ref, ...), custom_call_target="tpu_custom_call" | custom-call | flops 9663676416 | bytes 4194304 | tf_op jit(solution)/shard_map/attend/pallas_call | solution.py:423
  47.1 0.0 collective-permute-done.6.paired_low
  47.1 20.0 %all-to-all-start = ((bf16[32,40,128]{2,1,0:T(8,128)(2,1)}), bf16[32,40,128]{2,1,0:T(8,128)(2,1)S(1)}, u32[]{:S(2)}, u32[]{:S(2)}) async-start(bf16[32,40,128]{2,1,0:T(8,128)(2,1)} %bitcast.2), calls=%async_computation | async-start | bytes 655360 | tf_op jit(solution)/shard_map/all_to_all | solution.py:472
  67.1 1.5 %collective-permute-start.7 = (bf16[2,2,192,128]{3,2,1,0:T(8,128)(2,1)S(1)}, bf16[2,2,192,128]{3,2,1,0:T(8,128)(2,1)S(1)}, u32[]{:S(2)}, u32[]{:S(2)}) collective-permute-start(bf16[2,2,192,128]{3,2,1,0:T(8,128)(2,1)S(1)} %get-tuple-element.87), channel_id=1, source_target_pairs={{0,16},{1,17},{2,18},{3,19},{4,20},{5,21},{6,22},{7,23},{8,24},{9,... | collective-permute-start | bytes 589832 | tf_op jit(solution)/shard_map/ppermute | solution.py:462
  68.6 7.0 %collective-permute-done.7.middle_low = bf16[2,2,192,128]{3,2,1,0:T(8,128)(2,1)S(1)} collective-permute-done((bf16[2,2,192,128]{3,2,1,0:T(8,128)(2,1)S(1)}, bf16[2,2,192,128]{3,2,1,0:T(8,128)(2,1)S(1)}, u32[]{:S(2)}, u32[]{:S(2)}) %collective-permute-start.7) | collective-permute-done | bytes 196640 | tf_op jit(solution)/shard_map/ppermute | solution.py:462
  75.6 3.9 %all-to-all-done = bf16[32,40,128]{2,1,0:T(8,128)(2,1)S(1)} async-done(((bf16[32,40,128]{2,1,0:T(8,128)(2,1)}), bf16[32,40,128]{2,1,0:T(8,128)(2,1)S(1)}, u32[]{:S(2)}, u32[]{:S(2)}) %all-to-all-start) | async-done | bytes 327712 | tf_op jit(solution)/shard_map/all_to_all | solution.py:472
  79.5 0.1 pad_maximum_fusion
  79.6 0.1 collective-permute-start.8
  79.7 0.1 reduce_sum.24
  79.8 13.8 %all_to_all.15 = bf16[8,40,128]{2,1,0:T(8,128)(2,1)S(1)} all-to-all(bf16[8,40,128]{2,1,0:T(8,128)(2,1)S(1)} %broadcast_in_dim.20), channel_id=1, replica_groups={{0,32,64,96,128,160,192,224},{1,33,65,97,129,161,193,225},{2,34,66,98,1..., dimensions={0} | all-to-all | bytes 163840 | tf_op jit(solution)/shard_map/all_to_all | solution.py:472
  93.5 0.0 collective-permute-done.8.low_y_ref
  93.6 0.8 broadcast_in_dim.21
  94.3 8.4 %all-to-all-start.2 = ((bf16[32,40,128]{2,1,0:T(8,128)(2,1)}), bf16[32,40,128]{2,1,0:T(8,128)(2,1)S(1)}, u32[]{:S(2)}, u32[]{:S(2)}) async-start(bf16[32,40,128]{2,1,0:T(8,128)(2,1)} %broadcast_in_dim.21), calls=%async_computation.2 | async-start | bytes 655360 | tf_op jit(solution)/shard_map/all_to_all | solution.py:472
  102.8 1.6 %unpack.1 = (bf16[8,8,24,192]{3,2,1,0:T(8,128)(2,1)}, bf16[8,8,24,192]{3,2,1,0:T(8,128)(2,1)}) custom-call(bf16[6,2,192,128]{3,2,1,0:T(8,128)(2,1)S(1)} %collective-permute-done.8.low_y_ref, bf16[2,2,2,192,128]{4,3,2,1,0:T(8,128)(2,1)S(1)} %collective-permute-done.6.paired_low, bf16[2,2,2,192,128]{4,3,2,1,0:T(8,128)(2,1)S(1)} %get-tuple-element.91.paired_high, ...), custom_call_target="tpu_custom_call" | custom-call | tf_op jit(solution)/shard_map/unpack/pallas_call | solution.py:159
  104.4 8.1 %all-to-all-done.2 = bf16[32,40,128]{2,1,0:T(8,128)(2,1)S(1)} async-done(((bf16[32,40,128]{2,1,0:T(8,128)(2,1)}), bf16[32,40,128]{2,1,0:T(8,128)(2,1)S(1)}, u32[]{:S(2)}, u32[]{:S(2)}) %all-to-all-start.2) | async-done | bytes 327712 | tf_op jit(solution)/shard_map/all_to_all | solution.py:472
  112.5 0.7 copy-done.6
  113.2 1.9 %unpack_grads.1 = (f32[192,576]{1,0:T(8,128)}, f32[192,192]{1,0:T(8,128)}, f32[1,192]{1,0:T(1,128)}, f32[1,192]{1,0:T(1,128)}) custom-call(bf16[1280,128]{1,0:T(8,128)(2,1)} %bitcast.12), custom_call_target="tpu_custom_call" | custom-call | tf_op jit(solution)/shard_map/unpack_grads/pallas_call | solution.py:505
  (6 shorter events, 0.1 us)
Async XLA Ops:
  0.6 14.7 %copy-start.1 = (bf16[192,192]{1,0:T(8,128)(2,1)S(1)}, bf16[192,192]{1,0:T(8,128)(2,1)}, u32[]{:S(2)}) copy-start(bf16[192,192]{1,0:T(8,128)(2,1)} %proj_ref.3) | copy-start | bytes 221188
  0.6 14.7 %copy-start = (bf16[192,576]{1,0:T(8,128)(2,1)S(1)}, bf16[192,576]{1,0:T(8,128)(2,1)}, u32[]{:S(2)}) copy-start(bf16[192,576]{1,0:T(8,128)(2,1)} %wqkv_ref.7) | copy-start | bytes 663556
  0.7 14.7 %copy-start.3 = (f32[192]{0:T(256)S(1)}, f32[192]{0:T(256)}, u32[]{:S(2)}) copy-start(f32[192]{0:T(256)} %param.9) | copy-start | bytes 2308
  3.5 16.6 %collective-permute-start.3 = (bf16[2,192,128]{2,1,0:T(8,128)(2,1)}, bf16[2,192,128]{2,1,0:T(8,128)(2,1)S(1)}, u32[]{:S(2)}, u32[]{:S(2)}) collective-permute-start(bf16[2,192,128]{2,1,0:T(8,128)(2,1)} %get-tuple-element.75), channel_id=1, source_target_pairs={{0,255},{1,240},{2,241},{3,242},{4,243},{5,244},{6,245},{7,246},{8... | collective-permute-start | bytes 294920 | tf_op jit(solution)/shard_map/ppermute | solution.py:462
  11.5 8.7 %collective-permute-start.4 = (bf16[2,192,128]{2,1,0:T(8,128)(2,1)}, bf16[2,192,128]{2,1,0:T(8,128)(2,1)S(1)}, u32[]{:S(2)}, u32[]{:S(2)}) collective-permute-start(bf16[2,192,128]{2,1,0:T(8,128)(2,1)} %get-tuple-element.76), channel_id=1, source_target_pairs={{0,240},{1,241},{2,242},{3,243},{4,244},{5,245},{6,246},{7,247},{8... | collective-permute-start | bytes 294920 | tf_op jit(solution)/shard_map/ppermute | solution.py:462
  11.8 8.4 %collective-permute-start.5 = (bf16[2,192,128]{2,1,0:T(8,128)(2,1)}, bf16[2,192,128]{2,1,0:T(8,128)(2,1)S(1)}, u32[]{:S(2)}, u32[]{:S(2)}) collective-permute-start(bf16[2,192,128]{2,1,0:T(8,128)(2,1)} %get-tuple-element.77), channel_id=1, source_target_pairs={{0,15},{1,0},{2,1},{3,2},{4,3},{5,4},{6,5},{7,6},{8,7},{9,8},{10,9... | collective-permute-start | bytes 294920 | tf_op jit(solution)/shard_map/ppermute | solution.py:462
  15.3 0.7 copy-start.2
  15.3 4.9 %copy-start.7 = (bf16[2,2,192,128]{3,2,1,0:T(8,128)(2,1)S(1)}, bf16[2,2,192,128]{3,2,1,0:T(8,128)(2,1)}, u32[]{:S(2)}) copy-start(bf16[2,2,192,128]{3,2,1,0:T(8,128)(2,1)} %get-tuple-element.67) | copy-start | bytes 589828
  16.0 4.2 %copy-start.5 = (bf16[2,192,128]{2,1,0:T(8,128)(2,1)S(1)}, bf16[2,192,128]{2,1,0:T(8,128)(2,1)}, u32[]{:S(2)}) copy-start(bf16[2,192,128]{2,1,0:T(8,128)(2,1)} %get-tuple-element.78.q11_ref) | copy-start | bytes 294916
  16.2 13.9 %collective-permute-start = (bf16[2,2,192,128]{3,2,1,0:T(8,128)(2,1)}, bf16[2,2,192,128]{3,2,1,0:T(8,128)(2,1)S(1)}, u32[]{:S(2)}, u32[]{:S(2)}) collective-permute-start(bf16[2,2,192,128]{3,2,1,0:T(8,128)(2,1)} %get-tuple-element.65), channel_id=1, source_target_pairs={{0,255},{1,240},{2,241},{3,242},{4,243},{5,244},{6,245},{7,246},{8... | collective-permute-start | bytes 589832 | tf_op jit(solution)/shard_map/ppermute | solution.py:462
  19.0 11.1 %collective-permute-start.1 = (bf16[2,2,192,128]{3,2,1,0:T(8,128)(2,1)}, bf16[2,2,192,128]{3,2,1,0:T(8,128)(2,1)S(1)}, u32[]{:S(2)}, u32[]{:S(2)}) collective-permute-start(bf16[2,2,192,128]{3,2,1,0:T(8,128)(2,1)} %get-tuple-element.66), channel_id=1, source_target_pairs={{0,240},{1,241},{2,242},{3,243},{4,244},{5,245},{6,246},{7,247},{8... | collective-permute-start | bytes 589832 | tf_op jit(solution)/shard_map/ppermute | solution.py:462
  20.2 9.9 %collective-permute-start.2 = (bf16[2,2,192,128]{3,2,1,0:T(8,128)(2,1)S(1)}, bf16[2,2,192,128]{3,2,1,0:T(8,128)(2,1)S(1)}, u32[]{:S(2)}, u32[]{:S(2)}) collective-permute-start(bf16[2,2,192,128]{3,2,1,0:T(8,128)(2,1)S(1)} %copy-done.7), channel_id=1, source_target_pairs={{0,15},{1,0},{2,1},{3,2},{4,3},{5,4},{6,5},{7,6},{8,7},{9,8},{10,9... | collective-permute-start | bytes 589832 | tf_op jit(solution)/shard_map/ppermute | solution.py:462
  20.2 9.9 %copy-start.4 = (bf16[2,2,192,128]{3,2,1,0:T(8,128)(2,1)S(1)}, bf16[2,2,192,128]{3,2,1,0:T(8,128)(2,1)}, u32[]{:S(2)}) copy-start(bf16[2,2,192,128]{3,2,1,0:T(8,128)(2,1)} %get-tuple-element.68.q11_ref) | copy-start | bytes 589828
  35.9 11.2 %collective-permute-start.6 = (bf16[2,2,2,192,128]{4,3,2,1,0:T(8,128)(2,1)S(1)}, bf16[2,2,2,192,128]{4,3,2,1,0:T(8,128)(2,1)S(1)}, u32[]{:S(2)}, u32[]{:S(2)}) collective-permute-start(bf16[2,2,2,192,128]{4,3,2,1,0:T(8,128)(2,1)S(1)} %get-tuple-element.84), channel_id=1, source_target_pairs={{0,16},{1,17},{2,18},{3,19},{4,20},{5,21},{6,22},{7,23},{8,24},{9,... | collective-permute-start | bytes 1179656 | tf_op jit(solution)/shard_map/ppermute | solution.py:462
  47.1 32.4 %all-to-all-start = ((bf16[32,40,128]{2,1,0:T(8,128)(2,1)}), bf16[32,40,128]{2,1,0:T(8,128)(2,1)S(1)}, u32[]{:S(2)}, u32[]{:S(2)}) async-start(bf16[32,40,128]{2,1,0:T(8,128)(2,1)} %bitcast.2), calls=%async_computation | async-start | bytes 655360 | tf_op jit(solution)/shard_map/all_to_all | solution.py:472
  67.1 8.5 %collective-permute-start.7 = (bf16[2,2,192,128]{3,2,1,0:T(8,128)(2,1)S(1)}, bf16[2,2,192,128]{3,2,1,0:T(8,128)(2,1)S(1)}, u32[]{:S(2)}, u32[]{:S(2)}) collective-permute-start(bf16[2,2,192,128]{3,2,1,0:T(8,128)(2,1)S(1)} %get-tuple-element.87), channel_id=1, source_target_pairs={{0,16},{1,17},{2,18},{3,19},{4,20},{5,21},{6,22},{7,23},{8,24},{9,... | collective-permute-start | bytes 589832 | tf_op jit(solution)/shard_map/ppermute | solution.py:462
  79.6 13.9 %collective-permute-start.8 = (bf16[6,2,192,128]{3,2,1,0:T(8,128)(2,1)S(1)}, bf16[6,2,192,128]{3,2,1,0:T(8,128)(2,1)S(1)}, u32[]{:S(2)}, u32[]{:S(2)}) collective-permute-start(bf16[6,2,192,128]{3,2,1,0:T(8,128)(2,1)S(1)} %pad_maximum_fusion), channel_id=1, source_target_pairs={{0,1},{1,2},{2,3},{3,4},{4,5},{5,6},{6,7},{7,8},{8,9},{9,10},{10,1... | collective-permute-start | bytes 1769480 | tf_op jit(solution)/shard_map/ppermute | solution.py:462
  94.3 18.2 %all-to-all-start.2 = ((bf16[32,40,128]{2,1,0:T(8,128)(2,1)}), bf16[32,40,128]{2,1,0:T(8,128)(2,1)S(1)}, u32[]{:S(2)}, u32[]{:S(2)}) async-start(bf16[32,40,128]{2,1,0:T(8,128)(2,1)} %broadcast_in_dim.21), calls=%async_computation.2 | async-start | bytes 655360 | tf_op jit(solution)/shard_map/all_to_all | solution.py:472
  112.5 0.7 copy-start.6
